TPU v7x, 32 devices: a whole 2x2x4 slice. The times are simulated.
32 devices in a mesh: section: 2 (over x), tensor: 4 (over y, core), dp: 4 (over z).
Axes of the slice: x: 2, y: 2, z: 4, core: 2. Of those that a mesh axis runs over, the one named last changes fastest.
Arguments:
- boundary: bfloat16 [2, 8, 1024, 1536], P('section', 'dp', 'tensor'), may hold values from -6 to 6
- segments: int32 [8, 1024], P('dp'), may hold values from 0 to 4, as said below
- norm_gains: bfloat16 [2, 2, 1536], replicated, may hold values from 0.5 to 1.5
- qk_gains: bfloat16 [2, 64], replicated, may hold values from 0.5 to 1.5
- conv_in: bfloat16 [1536, 3, 1536], P(None, None, 'tensor'), may hold values from -0.15625 to 0.15625
- conv_kernel: bfloat16 [3, 1536], P(None, 'tensor'), may hold values from -3.5 to 3.5
- conv_out: bfloat16 [1536, 1536], P('tensor'), may hold values from -0.15625 to 0.15625
- attn_query: bfloat16 [1536, 1536], P(None, 'tensor'), may hold values from -0.15625 to 0.15625
- attn_keyval: bfloat16 [1536, 2, 512], P(None, None, 'tensor'), may hold values from -0.15625 to 0.15625
- attn_out: bfloat16 [1536, 1536], P('tensor'), may hold values from -1.25 to 1.25
- ffn_gate_up: bfloat16 [2, 1536, 2, 6912], P('section', None, None, 'tensor'), may hold values from -0.15625 to 0.15625
- ffn_down: bfloat16 [2, 1536, 6912], P('section', None, 'tensor'), may hold values from -0.078125 to 0.078125
Outputs:
- boundary_out: float32 [2, 8, 1024, 1536], P('section', 'dp', 'tensor')
- grad_norm_gains: float32 [2, 2, 1536], replicated
- grad_qk_gains: float32 [2, 64], replicated
- grad_conv_in: float32 [1536, 3, 1536], P(None, None, 'tensor')
- grad_conv_kernel: float32 [3, 1536], P(None, 'tensor')
- grad_conv_out: float32 [1536, 1536], P('tensor')
- grad_attn_query: float32 [1536, 1536], P(None, 'tensor')
- grad_attn_keyval: float32 [1536, 2, 512], P(None, None, 'tensor')
- grad_attn_out: float32 [1536, 1536], P('tensor')
- grad_ffn_gate_up: float32 [2, 1536, 2, 6912], P('section', None, None, 'tensor')
- grad_ffn_down: float32 [2, 1536, 6912], P('section', None, 'tensor')
Inputs may be any that keep to these rules, and one draw needn't show every extreme that they name: `segments`: each row of 1024 positions holds five documents with ids 0 to 4 in order along the row; document 2 begins before position 66 and ends after position 957.
All inputs are finite; a program needn't handle non-finite values.
Results may differ from a plain program's by a relative error of at most 0.024.
Values may be sent and summed in bfloat16 or wider, within the bound.
A program may use at most 448 MiB of HBM per device.

v0:
```python
import jax
import jax.numpy as jnp
from jax import lax
from jax.sharding import PartitionSpec as P

MICRO = 2
ROWS_MB = 1


EPSILON = 1e-05
THETA = 1000000.0
NEGATIVE = -1e30


def from_behind(array, axis, by):
    size = lax.axis_size(axis)
    pairs = [(i, i + by) for i in range(size) if 0 <= i + by < size]
    return lax.ppermute(array, axis, pairs)


def shortened(array):

    def short(part):
        return part.astype(jnp.bfloat16) if part.dtype == jnp.float32 else part

    return jax.tree.map(short, array)


def rms_norm(values, gain):
    return values * lax.rsqrt(jnp.mean(values * values, axis=-1, keepdims=True) + EPSILON) * gain


def gated(gate_up):
    return jax.nn.silu(gate_up[:, :, 0]) * gate_up[:, :, 1]


def delay_rows(values, lag):
    widths = ((0, 0), (lag, 0)) + ((0, 0),) * (values.ndim - 2)
    return jnp.pad(values, widths)[:, : values.shape[1]]


def lag_masks(seg_ids, kernel_len):
    masks_list = []
    for lag in range(1, kernel_len):
        shifted = jnp.pad(seg_ids, ((0, 0), (lag, 0)), constant_values=-1)[:, : seg_ids.shape[1]]
        masks_list.append((shifted == seg_ids).astype(jnp.float32)[..., None])
    return masks_list


def conv_mixer(project, kernel, masks_list):
    gate_in = project[:, :, 0] * project[:, :, 2]
    running = kernel[0] * gate_in
    for lag in range(1, kernel.shape[0]):
        running = running + kernel[lag] * delay_rows(gate_in, lag) * masks_list[lag - 1]
    return project[:, :, 1] * running


def rope_tables(seg_ids, half_dim):
    starts = jnp.sum((seg_ids[:, None, :] < seg_ids[:, :, None]).astype(jnp.int32), axis=2)
    places = jnp.arange(seg_ids.shape[1], dtype=jnp.int32)[None, :] - starts
    freqs = jnp.power(THETA, -(2.0 * jnp.arange(half_dim, dtype=jnp.float32)) / (2.0 * half_dim))
    angles = places.astype(jnp.float32)[..., None] * freqs
    return (jnp.cos(angles), jnp.sin(angles))


def head_prep(values, gain, cosine, sine):
    normed = rms_norm(values, gain)
    half_dim = values.shape[-1] // 2
    low_half = normed[..., :half_dim]
    high_half = normed[..., half_dim:]
    cos_b = cosine[..., None, :]
    sin_b = sine[..., None, :]
    return jnp.concatenate(
        [low_half * cos_b - high_half * sin_b, high_half * cos_b + low_half * sin_b], axis=-1
    )


def allowed_mask(seg_row, start, block_len):
    length = seg_row.shape[0]
    query_pos = start + jnp.arange(block_len, dtype=jnp.int32)
    key_pos = jnp.arange(length, dtype=jnp.int32)
    seg_query = lax.dynamic_slice_in_dim(seg_row, start, block_len)
    return (key_pos[None, :] <= query_pos[:, None]) & (seg_row[None, :] == seg_query[:, None])


def regroup(blocks):
    moved = jnp.moveaxis(blocks, 0, 2)
    return moved.reshape(moved.shape[:2] + (moved.shape[2] * moved.shape[3],) + moved.shape[4:])


def attend_row(query, keyed, valued, seg_row):
    length = query.shape[2]
    block_len = min(512, length)
    scaling = query.shape[3] ** (-0.5)

    def one_block(index):
        start = index * block_len
        q_block = lax.dynamic_slice_in_dim(query, start, block_len, 2)
        scores = (
            jnp.einsum("kgqd,ksd->kgqs", q_block, keyed, preferred_element_type=jnp.float32)
            * scaling
        )
        scores = jnp.where(allowed_mask(seg_row, start, block_len), scores, NEGATIVE)
        largest = jnp.max(scores, axis=-1)
        expon = jnp.exp(scores - largest[..., None])
        totals = jnp.sum(expon, axis=-1)
        probs = (expon / totals[..., None]).astype(jnp.bfloat16)
        attended = jnp.einsum(
            "kgqs,ksd->kgqd", probs, valued, preferred_element_type=jnp.float32
        ).astype(jnp.bfloat16)
        return (attended, largest + jnp.log(totals))

    attended, logsum = lax.map(one_block, jnp.arange(length // block_len, dtype=jnp.int32))
    return (regroup(attended), regroup(logsum))


def attend_back(query, keyed, valued, seg_row, logsum, grad_out):
    length = query.shape[2]
    block_len = min(512, length)
    scaling = query.shape[3] ** (-0.5)

    def one_block(carry, index):
        grad_key, grad_val = carry
        start = index * block_len
        q_block = lax.dynamic_slice_in_dim(query, start, block_len, 2)
        g_block = lax.dynamic_slice_in_dim(grad_out, start, block_len, 2)
        l_block = lax.dynamic_slice_in_dim(logsum, start, block_len, 2)
        scores = (
            jnp.einsum("kgqd,ksd->kgqs", q_block, keyed, preferred_element_type=jnp.float32)
            * scaling
        )
        scores = jnp.where(allowed_mask(seg_row, start, block_len), scores, NEGATIVE)
        probs = jnp.exp(scores - l_block[..., None])
        probs_low = probs.astype(jnp.bfloat16)
        attended = jnp.einsum(
            "kgqs,ksd->kgqd", probs_low, valued, preferred_element_type=jnp.float32
        ).astype(jnp.bfloat16)
        grad_probs = jnp.einsum(
            "kgqd,ksd->kgqs", g_block, valued, preferred_element_type=jnp.float32
        )
        inner = jnp.sum(probs * grad_probs, axis=-1, keepdims=True)
        grad_scores = (probs * (grad_probs - inner)).astype(jnp.bfloat16)
        grad_query = (
            jnp.einsum("kgqs,ksd->kgqd", grad_scores, keyed, preferred_element_type=jnp.float32)
            * scaling
        )
        grad_key = (
            grad_key
            + jnp.einsum("kgqs,kgqd->ksd", grad_scores, q_block, preferred_element_type=jnp.float32)
            * scaling
        )
        grad_val = grad_val + jnp.einsum(
            "kgqs,kgqd->ksd", probs_low, g_block, preferred_element_type=jnp.float32
        )
        return ((grad_key, grad_val), (attended, grad_query))

    zeros_kv = jnp.zeros(keyed.shape, jnp.float32)
    carried, stacked = lax.scan(
        one_block, (zeros_kv, zeros_kv), jnp.arange(length // block_len, dtype=jnp.int32)
    )
    return (regroup(stacked[0]), regroup(stacked[1]), carried[0], carried[1])


def gather_tokens(values):
    return lax.all_gather(values, "tensor", axis=1, tiled=True)


def reduce_tokens(values):
    return lax.psum_scatter(values, "tensor", scatter_dimension=1, tiled=True)


def on_device(
    boundary,
    segments,
    norm_gains,
    qk_gains,
    conv_in,
    conv_kernel,
    conv_out,
    attn_query,
    attn_keyval,
    attn_out,
    ffn_gate_up,
    ffn_down,
):
    section_pos = lax.axis_index("section")
    is_first = section_pos == 0
    local = boundary[0]
    rows_mb = ROWS_MB
    micro = MICRO
    seq_local = local.shape[1]
    width = local.shape[2]
    head_dim = qk_gains.shape[1]
    heads_here = attn_query.shape[1] // head_dim
    kv_here = attn_keyval.shape[2] // head_dim
    groups = heads_here // kv_here
    gain_pair = jnp.where(is_first, norm_gains[0], norm_gains[1]).astype(jnp.float32)
    head_gains = qk_gains.astype(jnp.float32)
    kernel = conv_kernel.astype(jnp.float32)
    gate_up_w = ffn_gate_up[0]
    down_w = ffn_down[0]

    def conv_forward(full, seg_ids):
        project = jnp.einsum("rtd,dce->rtce", full, conv_in, preferred_element_type=jnp.float32)
        mixed = conv_mixer(project, kernel, lag_masks(seg_ids, kernel.shape[0])).astype(
            jnp.bfloat16
        )
        partial_out = jnp.einsum("rte,ed->rtd", mixed, conv_out, preferred_element_type=jnp.float32)
        return (
            partial_out,
            jnp.zeros((full.shape[0], kv_here, groups, full.shape[1]), jnp.float32),
        )

    def project_heads(full, seg_ids):
        rows_now, length = (full.shape[0], full.shape[1])
        query_raw = jnp.einsum("rtd,de->rte", full, attn_query, preferred_element_type=jnp.float32)
        query_raw = query_raw.reshape(rows_now, length, heads_here, head_dim)
        keyval_raw = jnp.einsum(
            "rtd,dce->rtce", full, attn_keyval, preferred_element_type=jnp.float32
        )
        key_raw = keyval_raw[:, :, 0].reshape(rows_now, length, kv_here, head_dim)
        val_raw = keyval_raw[:, :, 1].reshape(rows_now, length, kv_here, head_dim)
        cosine, sine = rope_tables(seg_ids, head_dim // 2)
        return (query_raw, key_raw, val_raw, cosine, sine)

    def arrange(query, keyed, valued):
        rows_now, length = (query.shape[0], query.shape[1])
        q_all = query.reshape(rows_now, length, kv_here, groups, head_dim).transpose(0, 2, 3, 1, 4)
        return (q_all, keyed.transpose(0, 2, 1, 3), valued.transpose(0, 2, 1, 3))

    def attn_forward(full, seg_ids):
        rows_now, length = (full.shape[0], full.shape[1])
        query_raw, key_raw, val_raw, cosine, sine = project_heads(full, seg_ids)
        query = head_prep(query_raw, head_gains[0], cosine, sine).astype(jnp.bfloat16)
        keyed = head_prep(key_raw, head_gains[1], cosine, sine).astype(jnp.bfloat16)
        q_all, k_all, v_all = arrange(query, keyed, val_raw.astype(jnp.bfloat16))
        attended, logsum = lax.map(lambda item: attend_row(*item), (q_all, k_all, v_all, seg_ids))
        flat = attended.transpose(0, 3, 1, 2, 4).reshape(rows_now, length, heads_here * head_dim)
        return (
            jnp.einsum("rte,ed->rtd", flat, attn_out, preferred_element_type=jnp.float32),
            logsum,
        )

    def conv_backward(full, seg_ids, grad_full, logsum):
        project = jnp.einsum("rtd,dce->rtce", full, conv_in, preferred_element_type=jnp.float32)
        masks_list = lag_masks(seg_ids, kernel.shape[0])
        mixed_f, mixer_pull = jax.vjp(
            lambda values, weights: conv_mixer(values, weights, masks_list), project, kernel
        )
        mixed = mixed_f.astype(jnp.bfloat16)
        grad_mixed = jnp.einsum(
            "rtd,ed->rte", grad_full, conv_out, preferred_element_type=jnp.float32
        )
        grad_cout = jnp.einsum("rte,rtd->ed", mixed, grad_full, preferred_element_type=jnp.float32)
        grad_project, grad_kernel = mixer_pull(grad_mixed)
        grad_low = grad_project.astype(jnp.bfloat16)
        grad_cin = jnp.einsum("rtd,rtce->dce", full, grad_low, preferred_element_type=jnp.float32)
        partial_in = jnp.einsum(
            "rtce,dce->rtd", grad_low, conv_in, preferred_element_type=jnp.float32
        )
        return (
            partial_in,
            (
                grad_cin,
                grad_kernel,
                grad_cout,
                jnp.zeros(attn_query.shape, jnp.float32),
                jnp.zeros(attn_keyval.shape, jnp.float32),
                jnp.zeros(attn_out.shape, jnp.float32),
                jnp.zeros(qk_gains.shape, jnp.float32),
            ),
        )

    def attn_backward(full, seg_ids, grad_full, logsum):
        rows_now, length = (full.shape[0], full.shape[1])
        query_raw, key_raw, val_raw, cosine, sine = project_heads(full, seg_ids)
        query_f, query_pull = jax.vjp(
            lambda values, gain: head_prep(values, gain, cosine, sine), query_raw, head_gains[0]
        )
        keyed_f, key_pull = jax.vjp(
            lambda values, gain: head_prep(values, gain, cosine, sine), key_raw, head_gains[1]
        )
        q_all, k_all, v_all = arrange(
            query_f.astype(jnp.bfloat16), keyed_f.astype(jnp.bfloat16), val_raw.astype(jnp.bfloat16)
        )
        grad_flat = jnp.einsum(
            "rtd,ed->rte", grad_full, attn_out, preferred_element_type=jnp.float32
        ).astype(jnp.bfloat16)
        grad_heads = grad_flat.reshape(rows_now, length, kv_here, groups, head_dim).transpose(
            0, 2, 3, 1, 4
        )
        attended, grad_q, grad_k, grad_v = lax.map(
            lambda item: attend_back(*item), (q_all, k_all, v_all, seg_ids, logsum, grad_heads)
        )
        flat = attended.transpose(0, 3, 1, 2, 4).reshape(rows_now, length, heads_here * head_dim)
        grad_aout = jnp.einsum("rte,rtd->ed", flat, grad_full, preferred_element_type=jnp.float32)
        grad_qraw, grad_qgain = query_pull(
            grad_q.transpose(0, 3, 1, 2, 4).reshape(rows_now, length, heads_here, head_dim)
        )
        grad_kraw, grad_kgain = key_pull(grad_k.transpose(0, 2, 1, 3))
        grad_query_low = grad_qraw.reshape(rows_now, length, heads_here * head_dim).astype(
            jnp.bfloat16
        )
        grad_kv_low = jnp.stack(
            [
                grad_kraw.reshape(rows_now, length, kv_here * head_dim),
                grad_v.transpose(0, 2, 1, 3).reshape(rows_now, length, kv_here * head_dim),
            ],
            axis=2,
        ).astype(jnp.bfloat16)
        grad_aq = jnp.einsum(
            "rtd,rte->de", full, grad_query_low, preferred_element_type=jnp.float32
        )
        grad_akv = jnp.einsum(
            "rtd,rtce->dce", full, grad_kv_low, preferred_element_type=jnp.float32
        )
        partial_in = jnp.einsum(
            "rte,de->rtd", grad_query_low, attn_query, preferred_element_type=jnp.float32
        )
        partial_in = partial_in + jnp.einsum(
            "rtce,dce->rtd", grad_kv_low, attn_keyval, preferred_element_type=jnp.float32
        )
        return (
            partial_in,
            (
                jnp.zeros(conv_in.shape, jnp.float32),
                jnp.zeros(kernel.shape, jnp.float32),
                jnp.zeros(conv_out.shape, jnp.float32),
                grad_aq,
                grad_akv,
                grad_aout,
                jnp.stack([grad_qgain, grad_kgain]),
            ),
        )

    def down_partial(full_ffn):
        gate_up = jnp.einsum(
            "rtd,dcf->rtcf", full_ffn, gate_up_w, preferred_element_type=jnp.float32
        )
        active = gated(gate_up).astype(jnp.bfloat16)
        return (
            gate_up,
            jnp.einsum("rtf,df->rtd", active, down_w, preferred_element_type=jnp.float32),
        )

    def block_forward(layer_in, seg_ids):
        normed = rms_norm(layer_in, gain_pair[0]).astype(jnp.bfloat16)
        full = gather_tokens(normed)
        partial_out, logsum = lax.cond(is_first, conv_forward, attn_forward, full, seg_ids)
        hidden = layer_in + reduce_tokens(partial_out)
        normed_ffn = rms_norm(hidden, gain_pair[1]).astype(jnp.bfloat16)
        full_ffn = gather_tokens(normed_ffn)
        gate_up, partial_down = down_partial(full_ffn)
        result = hidden + reduce_tokens(partial_down)
        return (result, (layer_in, seg_ids, full, hidden, full_ffn, gate_up, logsum))

    def block_backward(grad_out, saved):
        layer_in, seg_ids, full, hidden, full_ffn, gate_up, logsum = saved
        grad_full = gather_tokens(grad_out.astype(jnp.bfloat16))
        active_f, gate_pull = jax.vjp(gated, gate_up)
        active = active_f.astype(jnp.bfloat16)
        grad_down = jnp.einsum("rtd,rtf->df", grad_full, active, preferred_element_type=jnp.float32)
        grad_active = jnp.einsum(
            "rtd,df->rtf", grad_full, down_w, preferred_element_type=jnp.float32
        )
        grad_gu_low = gate_pull(grad_active)[0].astype(jnp.bfloat16)
        grad_gu = jnp.einsum(
            "rtd,rtcf->dcf", full_ffn, grad_gu_low, preferred_element_type=jnp.float32
        )
        grad_normed = reduce_tokens(
            jnp.einsum("rtcf,dcf->rtd", grad_gu_low, gate_up_w, preferred_element_type=jnp.float32)
        )
        unused, norm_pull = jax.vjp(rms_norm, hidden, gain_pair[1])
        grad_hidden, grad_gain_ffn = norm_pull(grad_normed)
        grad_hidden = grad_hidden + grad_out
        grad_mix = gather_tokens(grad_hidden.astype(jnp.bfloat16))
        partial_in, mixer_grads = lax.cond(
            is_first, conv_backward, attn_backward, full, seg_ids, grad_mix, logsum
        )
        grad_normed_in = reduce_tokens(partial_in)
        unused, in_pull = jax.vjp(rms_norm, layer_in, gain_pair[0])
        grad_in, grad_gain_in = in_pull(grad_normed_in)
        return (
            grad_in + grad_hidden,
            jnp.stack([grad_gain_in, grad_gain_ffn]),
            grad_gu,
            grad_down,
            mixer_grads,
        )

    def own_block(clock):
        index = jnp.minimum(clock, micro - 1)
        picked = lax.dynamic_slice_in_dim(local, index * rows_mb, rows_mb, 0).astype(jnp.float32)
        return jnp.where(clock < micro, picked, jnp.zeros_like(picked))

    zeros_in = jnp.zeros((rows_mb, seq_local, width), jnp.float32)

    def forward_step(received, clock):
        layer_in = jnp.where(is_first, own_block(clock), received)
        seg_index = jnp.where(is_first, jnp.minimum(clock, micro - 1), jnp.maximum(clock - 1, 0))
        seg_ids = lax.dynamic_slice_in_dim(segments, seg_index * rows_mb, rows_mb, 0)
        result, saved = block_forward(layer_in, seg_ids)
        sent = from_behind(result.astype(jnp.bfloat16), "section", 1).astype(jnp.float32)
        return (sent, (result, saved))

    clocks = jnp.arange(micro + 1, dtype=jnp.int32)
    unused_in, (results, saved_stack) = lax.scan(forward_step, zeros_in, clocks)
    gain_acc = jnp.zeros((2, width), jnp.float32)
    mixer_acc = (
        jnp.zeros(conv_in.shape, jnp.float32),
        jnp.zeros(kernel.shape, jnp.float32),
        jnp.zeros(conv_out.shape, jnp.float32),
        jnp.zeros(attn_query.shape, jnp.float32),
        jnp.zeros(attn_keyval.shape, jnp.float32),
        jnp.zeros(attn_out.shape, jnp.float32),
        jnp.zeros(qk_gains.shape, jnp.float32),
    )
    ffn_acc = (jnp.zeros(gate_up_w.shape, jnp.float32), jnp.zeros(down_w.shape, jnp.float32))

    def backward_step(carry, clock):
        backward, gain_acc, mixer_acc, ffn_acc = carry
        grad_out = jnp.where(is_first, backward, own_block(clock))
        is_valid = jnp.where(
            is_first, (clock >= 1).astype(jnp.float32), (clock < micro).astype(jnp.float32)
        )
        saved_index = jnp.where(is_first, jnp.maximum(clock - 1, 0), jnp.minimum(clock + 1, micro))
        saved = jax.tree.map(lambda stacked: stacked[saved_index], saved_stack)
        grad_in, grad_gains, grad_gu, grad_down, mixer_grads = block_backward(grad_out, saved)
        gain_acc = gain_acc + is_valid * grad_gains
        mixer_acc = jax.tree.map(
            lambda total, term: total + is_valid * term, mixer_acc, mixer_grads
        )
        ffn_acc = (ffn_acc[0] + is_valid * grad_gu, ffn_acc[1] + is_valid * grad_down)
        backward = from_behind(grad_in.astype(jnp.bfloat16), "section", -1).astype(jnp.float32)
        return ((backward, gain_acc, mixer_acc, ffn_acc), grad_in)

    carried, grads_in = lax.scan(backward_step, (zeros_in, gain_acc, mixer_acc, ffn_acc), clocks)
    unused_back, gain_acc, mixer_acc, ffn_acc = carried
    full_gu, full_down = (
        lax.psum(ffn_acc[0].astype(jnp.bfloat16), "dp").astype(jnp.float32),
        lax.psum(ffn_acc[1].astype(jnp.bfloat16), "dp").astype(jnp.float32),
    )
    mixer_sums = jax.tree.map(
        lambda part: part.astype(jnp.float32), lax.psum(shortened(mixer_acc[:6]), ("section", "dp"))
    )
    block_pick = jnp.where(
        is_first, jnp.array([1.0, 0.0], jnp.float32), jnp.array([0.0, 1.0], jnp.float32)
    )
    grad_norm = block_pick[:, None, None] * gain_acc[None]
    grad_norm, grad_head = lax.psum((grad_norm, mixer_acc[6]), ("section", "tensor", "dp"))
    tail_shape = (micro * rows_mb, seq_local, width)
    outputs_rows = results[1:].reshape(tail_shape)
    grads_rows = grads_in[1:].reshape(tail_shape)
    boundary_out = jnp.where(is_first, grads_rows, outputs_rows)[None]
    return (
        boundary_out,
        grad_norm,
        grad_head,
        mixer_sums[0],
        mixer_sums[1],
        mixer_sums[2],
        mixer_sums[3],
        mixer_sums[4],
        mixer_sums[5],
        full_gu[None],
        full_down[None],
    )


def solution(mesh):
    placed = (
        P("section", "dp", "tensor", None),
        P("dp", None),
        P(),
        P(),
        P(None, None, "tensor"),
        P(None, "tensor"),
        P("tensor", None),
        P(None, "tensor"),
        P(None, None, "tensor"),
        P("tensor", None),
        P("section", None, None, "tensor"),
        P("section", None, "tensor"),
    )
    return jax.shard_map(
        on_device,
        mesh=mesh,
        in_specs=placed,
        out_specs=(
            P("section", "dp", "tensor", None),
            P(),
            P(),
            P(None, None, "tensor"),
            P(None, "tensor"),
            P("tensor", None),
            P(None, "tensor"),
            P(None, None, "tensor"),
            P("tensor", None),
            P("section", None, None, "tensor"),
            P("section", None, "tensor"),
        ),
        check_vma=False,
    )
```

profile of v0, /device:TPU:0, one launch (start us, length us, event | category | flops | bytes accessed | tf_op | source)
XLA Modules:
  0.0 2878.3 jit_solution(8364160543460826238)
XLA Ops:
  30.0 846.4 %while.121 = (s32[]{:T(128)}, f32[1,256,1536]{2,1,0:T(8,128)S(1)}, f32[3,1,256,1536]{3,2,1,0:T(8,128)}, f32[3,1,256,1536]{3,2,1,0:T(8,128)}, s32[3,1,1024]{2,1,0...) while((s32[]{:T(128)}, f32[1,256,1536]{2,1,0:T(8,128)S(1)}, ...), condition=%wide.region_14.15_spmd.clone, body=%wide.region_0.14_spmd.clone.sunk | while | flops 21164462080 | bytes 314755232 | solution.py:407
  37.1 29.4 %all-gather.5.cloned.1.call-done = bf16[1,1024,1536]{2,1,0:T(8,128)(2,1)} async-done(((bf16[1,256,1536]{2,1,0:T(8,128)(2,1)}), bf16[1,1024,1536]{2,1,0:T(8,128)(2,1)}) %all-gather.5.cloned.1.call-update) | async-done | bytes 3145744 | tf_op jit(solution)/shard_map/while/body/eval_jaxpr/all_gather | solution.py:165
  66.5 12.7 conditional.6
  79.3 85.5 %reduce-scatter.5.cloned.1.call-done = f32[1,256,1536]{2,1,0:T(8,128)} async-done(((f32[1,1024,1536]{2,1,0:T(8,128)}), f32[1,256,1536]{2,1,0:T(8,128)}) %reduce-scatter.5.cloned.1.call-update) | async-done | bytes 1572880 | tf_op jit(solution)/shard_map/while/body/eval_jaxpr/reduce_scatter | solution.py:169
  170.0 28.7 all-gather.7.cloned.1.call-done
  198.7 21.0 bitcast_dynamic-update-slice_fusion.19
  219.7 12.5 convolution_bitcast_fusion.8
  236.7 54.1 %reduce-scatter.7.cloned.1.call-done = f32[1,256,1536]{2,1,0:T(8,128)} async-done(((f32[1,1024,1536]{2,1,0:T(8,128)}), f32[1,256,1536]{2,1,0:T(8,128)}) %reduce-scatter.7.cloned.1.call-update) | async-done | bytes 1572880 | tf_op jit(solution)/shard_map/while/body/eval_jaxpr/reduce_scatter | solution.py:169
  299.3 13.3 collective-permute-done.1
  320.0 27.7 all-gather.5.cloned.1.call-done
  347.7 12.7 conditional.6
  360.5 85.5 %reduce-scatter.5.cloned.1.call-done = f32[1,256,1536]{2,1,0:T(8,128)} async-done(((f32[1,1024,1536]{2,1,0:T(8,128)}), f32[1,256,1536]{2,1,0:T(8,128)}) %reduce-scatter.5.cloned.1.call-update) | async-done | bytes 1572880 | tf_op jit(solution)/shard_map/while/body/eval_jaxpr/reduce_scatter | solution.py:169
  451.8 28.7 all-gather.7.cloned.1.call-done
  480.5 20.9 bitcast_dynamic-update-slice_fusion.19
  501.4 12.5 convolution_bitcast_fusion.8
  518.3 54.1 %reduce-scatter.7.cloned.1.call-done = f32[1,256,1536]{2,1,0:T(8,128)} async-done(((f32[1,1024,1536]{2,1,0:T(8,128)}), f32[1,256,1536]{2,1,0:T(8,128)}) %reduce-scatter.7.cloned.1.call-update) | async-done | bytes 1572880 | tf_op jit(solution)/shard_map/while/body/eval_jaxpr/reduce_scatter | solution.py:169
  581.0 13.3 collective-permute-done.1
  601.7 27.7 all-gather.5.cloned.1.call-done
  629.5 12.7 conditional.6
  642.3 85.6 %reduce-scatter.5.cloned.1.call-done = f32[1,256,1536]{2,1,0:T(8,128)} async-done(((f32[1,1024,1536]{2,1,0:T(8,128)}), f32[1,256,1536]{2,1,0:T(8,128)}) %reduce-scatter.5.cloned.1.call-update) | async-done | bytes 1572880 | tf_op jit(solution)/shard_map/while/body/eval_jaxpr/reduce_scatter | solution.py:169
  733.4 28.6 all-gather.7.cloned.1.call-done
  762.0 21.2 bitcast_dynamic-update-slice_fusion.19
  783.3 12.5 convolution_bitcast_fusion.8
  800.2 54.1 %reduce-scatter.7.cloned.1.call-done = f32[1,256,1536]{2,1,0:T(8,128)} async-done(((f32[1,1024,1536]{2,1,0:T(8,128)}), f32[1,256,1536]{2,1,0:T(8,128)}) %reduce-scatter.7.cloned.1.call-update) | async-done | bytes 1572880 | tf_op jit(solution)/shard_map/while/body/eval_jaxpr/reduce_scatter | solution.py:169
  862.9 13.3 collective-permute-done.1
  882.0 1157.7 %while.122 = (s32[]{:T(128)}, f32[1,256,1536]{2,1,0:T(8,128)S(1)}, f32[2,1536]{1,0:T(2,128)}, f32[1536,3,384]{2,1,0:T(4,128)}, f32[3,384]{1,0:T(4,128)}, /*index...) while((s32[]{:T(128)}, f32[1,256,1536]{2,1,0:T(8,128)S(1)}, ...), condition=%wide.region_39.40_spmd.clone, body=%wide.region_15.39_spmd.clone.sunk | while | flops 46018383872 | bytes 767438144 | solution.py:437
  895.1 13.1 dynamic-slice_bitcast_fusion.5
  908.3 15.3 all-gather.9.cloned.1.call-done
  923.6 17.5 fusion.251
  941.1 19.7 convolution_bitcast_fusion.9
  964.1 55.2 %reduce-scatter.9.cloned.1.call-done = f32[1,256,1536]{2,1,0:T(8,128)} async-done(((f32[1,1024,1536]{2,1,0:T(8,128)}), f32[1,256,1536]{2,1,0:T(8,128)}) %reduce-scatter.9.cloned.1.call-update) | async-done | bytes 1572880 | tf_op jit(solution)/shard_map/while/body/eval_jaxpr/reduce_scatter | solution.py:169
  1031.0 23.3 all-gather.11.cloned.1.call-done
  1054.4 53.5 %conditional.7 = (f32[1536,3,384]{2,1,0:T(4,128)}, f32[3,384]{1,0:T(4,128)S(1)}, f32[384,1536]{1,0:T(8,128)S(1)}, f32[1536,384]{0,1:T(8,128)}, f32[1536,2,128]{0...) conditional(s32[]{:T(128)} %convert_element_type.490, ...), branch_computations={%region_19.29_spmd, %region_30.33_spmd} | conditional | flops 13306434560 | bytes 301502752 | solution.py:377
  1110.2 12.4 select_add_fusion.24
  1122.6 19.3 select_add_fusion.23
  1164.5 72.0 %reduce-scatter.11.cloned.1.call-done = f32[1,256,1536]{2,1,0:T(8,128)} async-done(((f32[1,1024,1536]{2,1,0:T(8,128)}), f32[1,256,1536]{2,1,0:T(8,128)}) %reduce-scatter.11.cloned.1.call-update) | async-done | bytes 1572880 | tf_op jit(solution)/shard_map/while/body/eval_jaxpr/reduce_scatter | solution.py:169
  1243.5 19.7 collective-permute-done
  1269.1 13.5 dynamic-slice_bitcast_fusion.5
  1282.5 13.0 all-gather.9.cloned.1.call-done
  1295.5 17.5 fusion.251
  1313.1 19.7 convolution_bitcast_fusion.9
  1336.0 55.3 %reduce-scatter.9.cloned.1.call-done = f32[1,256,1536]{2,1,0:T(8,128)} async-done(((f32[1,1024,1536]{2,1,0:T(8,128)}), f32[1,256,1536]{2,1,0:T(8,128)}) %reduce-scatter.9.cloned.1.call-update) | async-done | bytes 1572880 | tf_op jit(solution)/shard_map/while/body/eval_jaxpr/reduce_scatter | solution.py:169
  1403.0 23.3 all-gather.11.cloned.1.call-done
  1426.3 53.5 %conditional.7 = (f32[1536,3,384]{2,1,0:T(4,128)}, f32[3,384]{1,0:T(4,128)S(1)}, f32[384,1536]{1,0:T(8,128)S(1)}, f32[1536,384]{0,1:T(8,128)}, f32[1536,2,128]{0...) conditional(s32[]{:T(128)} %convert_element_type.490, ...), branch_computations={%region_19.29_spmd, %region_30.33_spmd} | conditional | flops 13306434560 | bytes 301502752 | solution.py:377
  1482.1 14.4 select_add_fusion.24
  1496.5 25.7 select_add_fusion.23
  1546.7 61.7 %reduce-scatter.11.cloned.1.call-done = f32[1,256,1536]{2,1,0:T(8,128)} async-done(((f32[1,1024,1536]{2,1,0:T(8,128)}), f32[1,256,1536]{2,1,0:T(8,128)}) %reduce-scatter.11.cloned.1.call-update) | async-done | bytes 1572880 | tf_op jit(solution)/shard_map/while/body/eval_jaxpr/reduce_scatter | solution.py:169
  1615.5 33.2 %collective-permute-done = bf16[1,256,1536]{2,1,0:T(8,128)(2,1)S(1)} collective-permute-done((bf16[1,256,1536]{2,1,0:T(8,128)(2,1)S(1)}, bf16[1,256,1536]{2,1,0:T(8,128)(2,1)S(1)}, u32[]{:S(2)}, u32[]{:S(2)}) %collective-permute-start) | collective-permute-done | bytes 786464 | tf_op jit(solution)/shard_map/while/body/eval_jaxpr/ppermute | solution.py:18
  1654.3 13.4 dynamic-slice_bitcast_fusion.5
  1667.6 13.5 all-gather.9.cloned.1.call-done
  1681.2 17.5 fusion.251
  1698.7 19.7 convolution_bitcast_fusion.9
  1721.9 55.0 %reduce-scatter.9.cloned.1.call-done = f32[1,256,1536]{2,1,0:T(8,128)} async-done(((f32[1,1024,1536]{2,1,0:T(8,128)}), f32[1,256,1536]{2,1,0:T(8,128)}) %reduce-scatter.9.cloned.1.call-update) | async-done | bytes 1572880 | tf_op jit(solution)/shard_map/while/body/eval_jaxpr/reduce_scatter | solution.py:169
  1788.6 23.3 all-gather.11.cloned.1.call-done
  1812.0 53.5 %conditional.7 = (f32[1536,3,384]{2,1,0:T(4,128)}, f32[3,384]{1,0:T(4,128)S(1)}, f32[384,1536]{1,0:T(8,128)S(1)}, f32[1536,384]{0,1:T(8,128)}, f32[1536,2,128]{0...) conditional(s32[]{:T(128)} %convert_element_type.490, ...), branch_computations={%region_19.29_spmd, %region_30.33_spmd} | conditional | flops 13306434560 | bytes 301502752 | solution.py:377
  1867.8 14.4 select_add_fusion.24
  1882.2 25.6 select_add_fusion.23
  1932.4 61.7 %reduce-scatter.11.cloned.1.call-done = f32[1,256,1536]{2,1,0:T(8,128)} async-done(((f32[1,1024,1536]{2,1,0:T(8,128)}), f32[1,256,1536]{2,1,0:T(8,128)}) %reduce-scatter.11.cloned.1.call-update) | async-done | bytes 1572880 | tf_op jit(solution)/shard_map/while/body/eval_jaxpr/reduce_scatter | solution.py:169
  2001.2 33.2 %collective-permute-done = bf16[1,256,1536]{2,1,0:T(8,128)(2,1)S(1)} collective-permute-done((bf16[1,256,1536]{2,1,0:T(8,128)(2,1)S(1)}, bf16[1,256,1536]{2,1,0:T(8,128)(2,1)S(1)}, u32[]{:S(2)}, u32[]{:S(2)}) %collective-permute-start) | collective-permute-done | bytes 786464 | tf_op jit(solution)/shard_map/while/body/eval_jaxpr/ppermute | solution.py:18
  2075.9 21.6 psum.73
  2098.2 42.8 %all-reduce.22 = (f32[2,2,1536]{2,1,0:T(2,128)}, f32[2,64]{1,0:T(2,128)}) all-reduce(f32[2,2,1536]{2,1,0:T(2,128)S(1)} %broadcast_multiply_fusion, f32[2,64]{1,0:T(2,128)S(1)} %copy-done.87), channel_id=1, replica_groups=mesh['section'=2,'tensor'=4,'dp'=4] {'section','tensor','dp'}, use_global_device_ids=true, to_apply=%region_40.41 | all-reduce | flops 6272 | bytes 50176 | tf_op jit(solution)/shard_map/psum | solution.py:450
  2146.2 168.3 %all-reduce.28.cloned.1.call-done = (bf16[1536,3,384]{2,0,1:T(8,128)(2,1)}, bf16[384,1536]{1,0:T(8,128)(2,1)}, bf16[1536,384]{1,0:T(8,128)(2,1)}, bf16[1536,2,128]{2,1,0:T(2,128)(2,1)}, bf16[384,1536]{1,0:T(8,128)(2,1)}) async-done(((bf16[1536,3,384]{2,0,1:T(8,128)(2,1)}, bf16[384,1536]{1,0:T(8,128)(2,1)}, bf16[1536,384]{1,0:T(8,128)(2,1)}, bf16[1536,2,128]{2,1,0:T(2,128)(2,1)}, ...) | async-done | bytes 7864336 | tf_op jit(solution)/shard_map/psum | solution.py:444
  2325.5 526.3 %all-reduce.30.cloned.1.call-done = (bf16[1,1536,2,1728]{1,3,2,0:T(8,128)(2,1)}, bf16[1,1536,1728]{1,2,0:T(8,128)(2,1)}) async-done(((bf16[1,1536,2,1728]{1,3,2,0:T(8,128)(2,1)}, bf16[1,1536,1728]{1,2,0:T(8,128)(2,1)}), (bf16[1,1536,2,1728]{1,3,2,0:T(8,128)(2,1)}, bf16[1,1536,1728]{1,2,0:T(8,128)(2,1)})) %all-reduce.30.cloned.1.call-update) | async-done | bytes 15925264 | tf_op jit(solution)/shard_map/psum | solution.py:440
  2851.8 13.0 broadcast_in_dim.245
  (580 shorter events, 481.0 us)
Async XLA Ops:
  30.0 36.5 %all-gather.5.cloned.1.call-start = ((), (), s32[]{:S(2)}) async-start(), calls=%async_computation.6 | async-start | bytes 3932160 | tf_op jit(solution)/shard_map/while/body/eval_jaxpr/all_gather | solution.py:165
  35.1 129.7 %reduce-scatter.5.cloned.1.call-start = ((), (), s32[]{:S(2)}) async-start(), calls=%async_computation.7 | async-start | bytes 7864320 | tf_op jit(solution)/shard_map/while/body/eval_jaxpr/reduce_scatter | solution.py:169
  79.2 85.6 %copy-start.12 = (bf16[1,2,256,1536]{3,2,1,0:T(8,128)(2,1)S(1)}, bf16[1,2,256,1536]{3,2,1,0:T(8,128)(2,1)}, u32[]{:S(2)}) copy-start(bf16[1,2,256,1536]{3,2,1,0:T(8,128)(2,1)} %get-tuple-element.2603) | copy-start | bytes 4718596 | tf_op jit(solution)/shard_map/while
  79.3 119.4 %all-gather.7.cloned.1.call-start = ((), (), s32[]{:S(2)}) async-start(), calls=%async_computation.8 | async-start | bytes 3932160 | tf_op jit(solution)/shard_map/while/body/eval_jaxpr/all_gather | solution.py:165
  170.0 120.8 %reduce-scatter.7.cloned.1.call-start = ((), (), s32[]{:S(2)}) async-start(), calls=%async_computation.9 | async-start | bytes 7864320 | tf_op jit(solution)/shard_map/while/body/eval_jaxpr/reduce_scatter | solution.py:169
  292.5 20.2 collective-permute-start.1
  312.8 34.9 %all-gather.5.cloned.1.call-start = ((), (), s32[]{:S(2)}) async-start(), calls=%async_computation.6 | async-start | bytes 3932160 | tf_op jit(solution)/shard_map/while/body/eval_jaxpr/all_gather | solution.py:165
  318.0 128.0 %reduce-scatter.5.cloned.1.call-start = ((), (), s32[]{:S(2)}) async-start(), calls=%async_computation.7 | async-start | bytes 7864320 | tf_op jit(solution)/shard_map/while/body/eval_jaxpr/reduce_scatter | solution.py:169
  360.4 85.6 %copy-start.12 = (bf16[1,2,256,1536]{3,2,1,0:T(8,128)(2,1)S(1)}, bf16[1,2,256,1536]{3,2,1,0:T(8,128)(2,1)}, u32[]{:S(2)}) copy-start(bf16[1,2,256,1536]{3,2,1,0:T(8,128)(2,1)} %get-tuple-element.2603) | copy-start | bytes 4718596 | tf_op jit(solution)/shard_map/while
  360.5 120.0 %all-gather.7.cloned.1.call-start = ((), (), s32[]{:S(2)}) async-start(), calls=%async_computation.8 | async-start | bytes 3932160 | tf_op jit(solution)/shard_map/while/body/eval_jaxpr/all_gather | solution.py:165
  451.7 120.7 %reduce-scatter.7.cloned.1.call-start = ((), (), s32[]{:S(2)}) async-start(), calls=%async_computation.9 | async-start | bytes 7864320 | tf_op jit(solution)/shard_map/while/body/eval_jaxpr/reduce_scatter | solution.py:169
  574.2 20.2 collective-permute-start.1
  594.6 34.9 %all-gather.5.cloned.1.call-start = ((), (), s32[]{:S(2)}) async-start(), calls=%async_computation.6 | async-start | bytes 3932160 | tf_op jit(solution)/shard_map/while/body/eval_jaxpr/all_gather | solution.py:165
  599.7 128.1 %reduce-scatter.5.cloned.1.call-start = ((), (), s32[]{:S(2)}) async-start(), calls=%async_computation.7 | async-start | bytes 7864320 | tf_op jit(solution)/shard_map/while/body/eval_jaxpr/reduce_scatter | solution.py:169
  642.2 85.6 %copy-start.12 = (bf16[1,2,256,1536]{3,2,1,0:T(8,128)(2,1)S(1)}, bf16[1,2,256,1536]{3,2,1,0:T(8,128)(2,1)}, u32[]{:S(2)}) copy-start(bf16[1,2,256,1536]{3,2,1,0:T(8,128)(2,1)} %get-tuple-element.2603) | copy-start | bytes 4718596 | tf_op jit(solution)/shard_map/while
  642.2 119.8 %all-gather.7.cloned.1.call-start = ((), (), s32[]{:S(2)}) async-start(), calls=%async_computation.8 | async-start | bytes 3932160 | tf_op jit(solution)/shard_map/while/body/eval_jaxpr/all_gather | solution.py:165
  733.3 121.0 %reduce-scatter.7.cloned.1.call-start = ((), (), s32[]{:S(2)}) async-start(), calls=%async_computation.9 | async-start | bytes 7864320 | tf_op jit(solution)/shard_map/while/body/eval_jaxpr/reduce_scatter | solution.py:169
  856.1 20.2 collective-permute-start.1
  890.0 132.2 %copy-start.13 = (bf16[2,256,1536]{2,1,0:T(8,128)(2,1)}, bf16[2,256,1536]{2,1,0:T(8,128)(2,1)S(1)}, u32[]{:S(2)}) copy-start(bf16[2,256,1536]{2,1,0:T(8,128)(2,1)S(1)} %get-tuple-element.2527) | copy-start | bytes 4718596 | tf_op jit(solution)/shard_map/while
  890.0 164.3 %copy-start.69 = (f32[3,1,2,3,1024]{4,3,2,1,0:T(4,128)}, f32[3,1,2,3,1024]{4,3,2,1,0:T(4,128)S(1)}, u32[]{:S(2)}) copy-start(f32[3,1,2,3,1024]{4,3,2,1,0:T(4,128)S(1)} %get-tuple-element.2535) | copy-start | bytes 221188 | tf_op jit(solution)/shard_map/while
  890.0 33.5 %all-gather.9.cloned.1.call-start = ((), (), s32[]{:S(2)}) async-start(), calls=%async_computation.10 | async-start | bytes 3932160 | tf_op jit(solution)/shard_map/while/body/eval_jaxpr/all_gather | solution.py:165
  893.8 125.5 %reduce-scatter.9.cloned.1.call-start = ((), (), s32[]{:S(2)}) async-start(), calls=%async_computation.11 | async-start | bytes 7864320 | tf_op jit(solution)/shard_map/while/body/eval_jaxpr/reduce_scatter | solution.py:169
  960.8 93.6 %all-gather.11.cloned.1.call-start = ((), (), s32[]{:S(2)}) async-start(), calls=%async_computation.12 | async-start | bytes 3932160 | tf_op jit(solution)/shard_map/while/body/eval_jaxpr/all_gather | solution.py:165
  1025.7 210.8 %reduce-scatter.11.cloned.1.call-start = ((), (), s32[]{:S(2)}) async-start(), calls=%async_computation.13 | async-start | bytes 7864320 | tf_op jit(solution)/shard_map/while/body/eval_jaxpr/reduce_scatter | solution.py:169
  1027.1 27.3 copy-start.21
  1027.1 27.3 copy-start.45
  1027.1 27.3 copy-start.51
  1154.1 82.4 %copy-start.61 = (f32[1536]{0:T(1024)S(1)}, f32[1536]{0:T(1024)}, u32[]{:S(2)}) copy-start(f32[1536]{0:T(1024)} %get-tuple-element.2191) | copy-start | bytes 18436 | tf_op jit(solution)/shard_map/while
  1164.5 74.3 %copy-start.16 = (f32[1,256,1536]{2,1,0:T(8,128)S(1)}, f32[1,256,1536]{2,1,0:T(8,128)}, u32[]{:S(2)}) copy-start(f32[1,256,1536]{2,1,0:T(8,128)} %get-tuple-element.2188) | copy-start | bytes 4718596 | tf_op jit(solution)/shard_map/while
  1242.1 21.2 collective-permute-start
  1263.9 130.3 %copy-start.13 = (bf16[2,256,1536]{2,1,0:T(8,128)(2,1)}, bf16[2,256,1536]{2,1,0:T(8,128)(2,1)S(1)}, u32[]{:S(2)}) copy-start(bf16[2,256,1536]{2,1,0:T(8,128)(2,1)S(1)} %get-tuple-element.2527) | copy-start | bytes 4718596 | tf_op jit(solution)/shard_map/while
  1264.0 162.4 %copy-start.69 = (f32[3,1,2,3,1024]{4,3,2,1,0:T(4,128)}, f32[3,1,2,3,1024]{4,3,2,1,0:T(4,128)S(1)}, u32[]{:S(2)}) copy-start(f32[3,1,2,3,1024]{4,3,2,1,0:T(4,128)S(1)} %get-tuple-element.2535) | copy-start | bytes 221188 | tf_op jit(solution)/shard_map/while
  1264.0 31.6 %all-gather.9.cloned.1.call-start = ((), (), s32[]{:S(2)}) async-start(), calls=%async_computation.10 | async-start | bytes 3932160 | tf_op jit(solution)/shard_map/while/body/eval_jaxpr/all_gather | solution.py:165
  1267.7 123.5 %reduce-scatter.9.cloned.1.call-start = ((), (), s32[]{:S(2)}) async-start(), calls=%async_computation.11 | async-start | bytes 7864320 | tf_op jit(solution)/shard_map/while/body/eval_jaxpr/reduce_scatter | solution.py:169
  1332.8 93.5 %all-gather.11.cloned.1.call-start = ((), (), s32[]{:S(2)}) async-start(), calls=%async_computation.12 | async-start | bytes 3932160 | tf_op jit(solution)/shard_map/while/body/eval_jaxpr/all_gather | solution.py:165
  1397.6 210.8 %reduce-scatter.11.cloned.1.call-start = ((), (), s32[]{:S(2)}) async-start(), calls=%async_computation.13 | async-start | bytes 7864320 | tf_op jit(solution)/shard_map/while/body/eval_jaxpr/reduce_scatter | solution.py:169
  1534.4 74.0 %copy-start.61 = (f32[1536]{0:T(1024)S(1)}, f32[1536]{0:T(1024)}, u32[]{:S(2)}) copy-start(f32[1536]{0:T(1024)} %get-tuple-element.2191) | copy-start | bytes 18436 | tf_op jit(solution)/shard_map/while
  1546.7 64.1 %copy-start.16 = (f32[1,256,1536]{2,1,0:T(8,128)S(1)}, f32[1,256,1536]{2,1,0:T(8,128)}, u32[]{:S(2)}) copy-start(f32[1,256,1536]{2,1,0:T(8,128)} %get-tuple-element.2188) | copy-start | bytes 4718596 | tf_op jit(solution)/shard_map/while
  1610.9 38.0 %copy-start.14 = (bf16[2,256,1536]{2,1,0:T(8,128)(2,1)S(1)}, bf16[2,256,1536]{2,1,0:T(8,128)(2,1)}, u32[]{:S(2)}) copy-start(bf16[2,256,1536]{2,1,0:T(8,128)(2,1)} %copy-done.13) | copy-start | bytes 4718596 | tf_op jit(solution)/shard_map/while
  1610.9 38.0 %copy-start.70 = (f32[3,1,2,3,1024]{4,3,2,1,0:T(4,128)S(1)}, f32[3,1,2,3,1024]{4,3,2,1,0:T(4,128)}, u32[]{:S(2)}) copy-start(f32[3,1,2,3,1024]{4,3,2,1,0:T(4,128)} %copy-done.69) | copy-start | bytes 221188 | tf_op jit(solution)/shard_map/while
  1610.9 38.0 %copy-start.84 = (f32[2,64]{1,0:T(2,128)S(1)}, f32[2,64]{1,0:T(2,128)}, u32[]{:S(2)}) copy-start(f32[2,64]{1,0:T(2,128)} %get-tuple-element.2686) | copy-start | bytes 1540 | tf_op jit(solution)/shard_map/while
  1614.0 34.7 %collective-permute-start = (bf16[1,256,1536]{2,1,0:T(8,128)(2,1)S(1)}, bf16[1,256,1536]{2,1,0:T(8,128)(2,1)S(1)}, u32[]{:S(2)}, u32[]{:S(2)}) collective-permute-start(bf16[1,256,1536]{2,1,0:T(8,128)(2,1)S(1)} %get-tuple-element.2193), channel_id=1, source_target_pairs={{16,0},{17,1},{18,2},{19,3},{20,4},{21,5},{22,6},{23,7},{24,8},{25... | collective-permute-start | bytes 2359304 | tf_op jit(solution)/shard_map/while/body/eval_jaxpr/ppermute | solution.py:18
  1615.4 33.5 %copy-start.86 = (f32[2,64]{1,0:T(2,128)}, f32[2,64]{1,0:T(2,128)S(1)}, u32[]{:S(2)}) copy-start(f32[2,64]{1,0:T(2,128)S(1)} %select_add_fusion.22) | copy-start | bytes 1540 | tf_op jit(solution)/shard_map/while
  1615.4 33.5 %copy-start.76 = (f32[3,384]{1,0:T(4,128)}, f32[3,384]{1,0:T(4,128)S(1)}, u32[]{:S(2)}) copy-start(f32[3,384]{1,0:T(4,128)S(1)} %select_add_fusion.18) | copy-start | bytes 13828 | tf_op jit(solution)/shard_map/while
  1615.5 33.4 %copy-start.73 = (f32[2,1536]{1,0:T(2,128)}, f32[2,1536]{1,0:T(2,128)S(1)}, u32[]{:S(2)}) copy-start(f32[2,1536]{1,0:T(2,128)S(1)} %fusion.260) | copy-start | bytes 36868 | tf_op jit(solution)/shard_map/while
  1649.2 130.7 %copy-start.13 = (bf16[2,256,1536]{2,1,0:T(8,128)(2,1)}, bf16[2,256,1536]{2,1,0:T(8,128)(2,1)S(1)}, u32[]{:S(2)}) copy-start(bf16[2,256,1536]{2,1,0:T(8,128)(2,1)S(1)} %get-tuple-element.2527) | copy-start | bytes 4718596 | tf_op jit(solution)/shard_map/while
  1649.2 162.8 %copy-start.69 = (f32[3,1,2,3,1024]{4,3,2,1,0:T(4,128)}, f32[3,1,2,3,1024]{4,3,2,1,0:T(4,128)S(1)}, u32[]{:S(2)}) copy-start(f32[3,1,2,3,1024]{4,3,2,1,0:T(4,128)S(1)} %get-tuple-element.2535) | copy-start | bytes 221188 | tf_op jit(solution)/shard_map/while
  1649.2 32.0 %all-gather.9.cloned.1.call-start = ((), (), s32[]{:S(2)}) async-start(), calls=%async_computation.10 | async-start | bytes 3932160 | tf_op jit(solution)/shard_map/while/body/eval_jaxpr/all_gather | solution.py:165
  1653.0 123.9 %reduce-scatter.9.cloned.1.call-start = ((), (), s32[]{:S(2)}) async-start(), calls=%async_computation.11 | async-start | bytes 7864320 | tf_op jit(solution)/shard_map/while/body/eval_jaxpr/reduce_scatter | solution.py:169
  1718.4 93.6 %all-gather.11.cloned.1.call-start = ((), (), s32[]{:S(2)}) async-start(), calls=%async_computation.12 | async-start | bytes 3932160 | tf_op jit(solution)/shard_map/while/body/eval_jaxpr/all_gather | solution.py:165
  1783.3 210.8 %reduce-scatter.11.cloned.1.call-start = ((), (), s32[]{:S(2)}) async-start(), calls=%async_computation.13 | async-start | bytes 7864320 | tf_op jit(solution)/shard_map/while/body/eval_jaxpr/reduce_scatter | solution.py:169
  1784.7 27.3 copy-start.45
  1784.7 27.3 copy-start.51
  1920.1 74.0 %copy-start.61 = (f32[1536]{0:T(1024)S(1)}, f32[1536]{0:T(1024)}, u32[]{:S(2)}) copy-start(f32[1536]{0:T(1024)} %get-tuple-element.2191) | copy-start | bytes 18436 | tf_op jit(solution)/shard_map/while
  1932.4 64.1 %copy-start.16 = (f32[1,256,1536]{2,1,0:T(8,128)S(1)}, f32[1,256,1536]{2,1,0:T(8,128)}, u32[]{:S(2)}) copy-start(f32[1,256,1536]{2,1,0:T(8,128)} %get-tuple-element.2188) | copy-start | bytes 4718596 | tf_op jit(solution)/shard_map/while
  1996.5 38.1 %copy-start.14 = (bf16[2,256,1536]{2,1,0:T(8,128)(2,1)S(1)}, bf16[2,256,1536]{2,1,0:T(8,128)(2,1)}, u32[]{:S(2)}) copy-start(bf16[2,256,1536]{2,1,0:T(8,128)(2,1)} %copy-done.13) | copy-start | bytes 4718596 | tf_op jit(solution)/shard_map/while
  1996.5 38.1 %copy-start.70 = (f32[3,1,2,3,1024]{4,3,2,1,0:T(4,128)S(1)}, f32[3,1,2,3,1024]{4,3,2,1,0:T(4,128)}, u32[]{:S(2)}) copy-start(f32[3,1,2,3,1024]{4,3,2,1,0:T(4,128)} %copy-done.69) | copy-start | bytes 221188 | tf_op jit(solution)/shard_map/while
  1996.5 38.1 %copy-start.84 = (f32[2,64]{1,0:T(2,128)S(1)}, f32[2,64]{1,0:T(2,128)}, u32[]{:S(2)}) copy-start(f32[2,64]{1,0:T(2,128)} %get-tuple-element.2686) | copy-start | bytes 1540 | tf_op jit(solution)/shard_map/while
  1999.7 34.6 %collective-permute-start = (bf16[1,256,1536]{2,1,0:T(8,128)(2,1)S(1)}, bf16[1,256,1536]{2,1,0:T(8,128)(2,1)S(1)}, u32[]{:S(2)}, u32[]{:S(2)}) collective-permute-start(bf16[1,256,1536]{2,1,0:T(8,128)(2,1)S(1)} %get-tuple-element.2193), channel_id=1, source_target_pairs={{16,0},{17,1},{18,2},{19,3},{20,4},{21,5},{22,6},{23,7},{24,8},{25... | collective-permute-start | bytes 2359304 | tf_op jit(solution)/shard_map/while/body/eval_jaxpr/ppermute | solution.py:18
  2001.1 33.5 %copy-start.86 = (f32[2,64]{1,0:T(2,128)}, f32[2,64]{1,0:T(2,128)S(1)}, u32[]{:S(2)}) copy-start(f32[2,64]{1,0:T(2,128)S(1)} %select_add_fusion.22) | copy-start | bytes 1540 | tf_op jit(solution)/shard_map/while
  2001.1 33.5 %copy-start.76 = (f32[3,384]{1,0:T(4,128)}, f32[3,384]{1,0:T(4,128)S(1)}, u32[]{:S(2)}) copy-start(f32[3,384]{1,0:T(4,128)S(1)} %select_add_fusion.18) | copy-start | bytes 13828 | tf_op jit(solution)/shard_map/while
  2001.2 33.4 %copy-start.73 = (f32[2,1536]{1,0:T(2,128)}, f32[2,1536]{1,0:T(2,128)S(1)}, u32[]{:S(2)}) copy-start(f32[2,1536]{1,0:T(2,128)S(1)} %fusion.260) | copy-start | bytes 36868 | tf_op jit(solution)/shard_map/while
  2039.7 274.8 %all-reduce.28.cloned.1.call-start = ((), (), s32[]{:S(2)}) async-start(), calls=%async_computation.4 | async-start | bytes 15728640 | tf_op jit(solution)/shard_map/psum | solution.py:444
  2055.9 795.9 %all-reduce.30.cloned.1.call-start = ((), (), s32[]{:S(2)}) async-start(), calls=%async_computation.5 | async-start | bytes 31850496 | tf_op jit(solution)/shard_map/psum | solution.py:440
  (103 other events, 782.0 us)
Sparse Core Ops, SparseCore 0:
  35.2 31.2 all-gather.4
  79.4 85.4 reduce-scatter.4
  170.1 28.5 all-gather.6
  232.3 58.3 reduce-scatter.6
  318.1 29.5 all-gather.4
  360.6 85.4 reduce-scatter.4
  451.9 28.5 all-gather.6
  514.1 58.3 reduce-scatter.6
  599.8 29.5 all-gather.4
  642.3 85.4 reduce-scatter.4
  733.5 28.5 all-gather.6
  795.9 58.3 reduce-scatter.6
  893.9 29.5 all-gather.8
  960.9 58.3 reduce-scatter.8
  1025.8 28.5 all-gather.10
  1108.1 128.4 reduce-scatter.10
  1267.9 27.6 all-gather.8
  1332.9 58.3 reduce-scatter.8
  1397.7 28.5 all-gather.10
  1480.0 128.4 reduce-scatter.10
  1653.1 28.0 all-gather.8
  1718.5 58.3 reduce-scatter.8
  1783.4 28.5 all-gather.10
  1865.6 128.3 reduce-scatter.10
Sparse Core Ops, SparseCore 1:
  2055.9 258.5 all-reduce.27
  2317.6 534.1 all-reduce.29
where the time goes:
time: 2900 us; the launch traced here: 2880 us
  waiting for transfers between devices  1880 us (65%)
  matrix products  429 us (15%)
  local copies, waits for them, and re-layouts  208 us (7%)
  other arithmetic  205 us (7%)
  blocking collectives  64.5 us (2%)
  loops' own time  56.4 us (2%)
    reduce_scatter x12, waiting for transfers between devices, reduce_tokens(): return lax.psum_scatter(values, 'tensor', scatter_dimension=1, tiled=True)  780 us
    psum x1, waiting for transfers between devices, on_device(): lax.psum(ffn_acc[0].astype(jnp.bfloat16), 'dp').astype(jnp.float32)  526 us
    all_gather x12, waiting for transfers between devices, gather_tokens(): return lax.all_gather(values, 'tensor', axis=1, tiled=True)  283 us
    psum x1, waiting for transfers between devices, on_device(): lax.psum(shortened(mixer_acc[:6]), ('section', 'dp'))  168 us
    ppermute x6, waiting for transfers between devices, from_behind(): return lax.ppermute(array, axis, pairs)  126 us
    dot_general x3, matrix products, block_backward(): jnp.einsum('rtd,rtcf->dcf', full_ffn, grad_gu_low, preferred_element_type...  70.6 us
    dot_general x3, matrix products, down_partial(): jnp.einsum('rtd,dcf->rtcf', full_ffn, gate_up_w, preferred_element_type=j...  63.2 us
    add x18, other arithmetic, backward_step(): total + is_valid * term  60.8 us
  transfers between devices with their start and end apart: 32, of which 32 were waited for; matrix products, arithmetic and copies ran while one was open for 11% of the time, Pallas kernels for 0%

commit v1 on v0

v1 whole, which is shorter than its diff:
```python
import jax
import jax.numpy as jnp
from jax import lax
from jax.sharding import PartitionSpec as P

EPSILON = 1e-05
THETA = 1000000.0
NEGATIVE = -1e30
BF = jnp.bfloat16
F32 = jnp.float32


def mm(spec, left, right, kind=F32):
    return jnp.einsum(spec, left, right, preferred_element_type=F32).astype(kind)


def inverse_rms(values):
    return lax.rsqrt(jnp.mean(values * values, axis=-1, keepdims=True) + EPSILON)


def norm(values, gain):
    return (values * inverse_rms(values) * gain).astype(BF)


def norm_back(values, gain, grad):
    scale = inverse_rms(values)
    normed = values * scale
    weighted = grad * gain
    grad_in = scale * (weighted - normed * jnp.mean(weighted * normed, axis=-1, keepdims=True))
    return grad_in, grad * normed


def section_pairs(section, size, function):
    return [
        (section * size + i, section * size + function(i))
        for i in range(size)
        if 0 <= function(i) < size
    ]


def permute(values, section, axis, function):
    pairs = section_pairs(section, lax.axis_size(axis), function)
    return lax.ppermute(values, ("section", axis), pairs)


def pick(values, index, axis):
    return lax.dynamic_index_in_dim(values, index, axis, keepdims=False)


def delay_rows(values, lag):
    widths = ((0, 0), (lag, 0)) + ((0, 0),) * (values.ndim - 2)
    return jnp.pad(values, widths)[:, : values.shape[1]]


def advance_rows(values, lag):
    widths = ((0, 0), (0, lag)) + ((0, 0),) * (values.ndim - 2)
    return jnp.pad(values, widths)[:, lag:]


def lag_masks(seg_ids, kernel_len):
    masks_list = []
    for lag in range(1, kernel_len):
        shifted = jnp.pad(seg_ids, ((0, 0), (lag, 0)), constant_values=-1)[:, : seg_ids.shape[1]]
        masks_list.append((shifted == seg_ids).astype(F32)[..., None])
    return masks_list


def rope_tables(seg_ids, half_dim):
    starts = jnp.sum((seg_ids[:, None, :] < seg_ids[:, :, None]).astype(jnp.int32), axis=2)
    places = jnp.arange(seg_ids.shape[1], dtype=jnp.int32)[None, :] - starts
    freqs = jnp.power(THETA, -(2.0 * jnp.arange(half_dim, dtype=F32)) / (2.0 * half_dim))
    angles = places.astype(F32)[..., None] * freqs
    return (jnp.cos(angles), jnp.sin(angles))


def head_prep(values, gain, cosine, sine):
    normed = values * inverse_rms(values) * gain
    half_dim = values.shape[-1] // 2
    low_half = normed[..., :half_dim]
    high_half = normed[..., half_dim:]
    cos_b = cosine[..., None, :]
    sin_b = sine[..., None, :]
    return jnp.concatenate(
        [low_half * cos_b - high_half * sin_b, high_half * cos_b + low_half * sin_b], axis=-1
    )


def allowed_mask(seg_row, start, block_len):
    length = seg_row.shape[0]
    query_pos = start + jnp.arange(block_len, dtype=jnp.int32)
    key_pos = jnp.arange(length, dtype=jnp.int32)
    seg_query = lax.dynamic_slice_in_dim(seg_row, start, block_len)
    return (key_pos[None, :] <= query_pos[:, None]) & (seg_row[None, :] == seg_query[:, None])


def regroup(blocks):
    moved = jnp.moveaxis(blocks, 0, 2)
    return moved.reshape(moved.shape[:2] + (moved.shape[2] * moved.shape[3],) + moved.shape[4:])


def attend_row(query, keyed, valued, seg_row):
    length = query.shape[2]
    block_len = min(512, length)
    scaling = query.shape[3] ** (-0.5)

    def one_block(index):
        start = index * block_len
        q_block = lax.dynamic_slice_in_dim(query, start, block_len, 2)
        scores = mm("kgqd,ksd->kgqs", q_block, keyed) * scaling
        scores = jnp.where(allowed_mask(seg_row, start, block_len), scores, NEGATIVE)
        largest = jnp.max(scores, axis=-1)
        expon = jnp.exp(scores - largest[..., None])
        totals = jnp.sum(expon, axis=-1)
        probs = (expon / totals[..., None]).astype(BF)
        attended = mm("kgqs,ksd->kgqd", probs, valued, BF)
        return (attended, largest + jnp.log(totals))

    attended, logsum = lax.map(one_block, jnp.arange(length // block_len, dtype=jnp.int32))
    return (regroup(attended), regroup(logsum))


def attend_back(query, keyed, valued, seg_row, logsum, grad_out):
    length = query.shape[2]
    block_len = min(512, length)
    scaling = query.shape[3] ** (-0.5)

    def one_block(carry, index):
        grad_key, grad_val = carry
        start = index * block_len
        q_block = lax.dynamic_slice_in_dim(query, start, block_len, 2)
        g_block = lax.dynamic_slice_in_dim(grad_out, start, block_len, 2)
        l_block = lax.dynamic_slice_in_dim(logsum, start, block_len, 2)
        scores = mm("kgqd,ksd->kgqs", q_block, keyed) * scaling
        scores = jnp.where(allowed_mask(seg_row, start, block_len), scores, NEGATIVE)
        probs = jnp.exp(scores - l_block[..., None])
        probs_low = probs.astype(BF)
        grad_probs = mm("kgqd,ksd->kgqs", g_block, valued)
        inner = jnp.sum(probs * grad_probs, axis=-1, keepdims=True)
        grad_scores = (probs * (grad_probs - inner)).astype(BF)
        grad_query = mm("kgqs,ksd->kgqd", grad_scores, keyed) * scaling
        grad_key = grad_key + mm("kgqs,kgqd->ksd", grad_scores, q_block) * scaling
        grad_val = grad_val + mm("kgqs,kgqd->ksd", probs_low, g_block)
        return ((grad_key, grad_val), grad_query)

    zeros_kv = jnp.zeros(keyed.shape, F32)
    carried, stacked = lax.scan(
        one_block, (zeros_kv, zeros_kv), jnp.arange(length // block_len, dtype=jnp.int32)
    )
    return (regroup(stacked), carried[0], carried[1])


def on_device(
    boundary,
    segments,
    norm_gains,
    qk_gains,
    conv_in,
    conv_kernel,
    conv_out,
    attn_query,
    attn_keyval,
    attn_out,
    ffn_gate_up,
    ffn_down,
):
    is_first = lax.axis_index("section") == 0
    place = lax.axis_index("tensor")
    tensor = lax.axis_size("tensor")
    dp = lax.axis_size("dp")
    core = place % 2
    chip = place // 2
    chips = tensor // 2
    steps = [1 << k for k in range(chips.bit_length() - 1)]
    local = boundary[0]
    rows, seq_local, width = local.shape
    seq = segments.shape[1]
    head_dim = qk_gains.shape[1]
    heads_here = attn_query.shape[1] // head_dim
    kv_here = attn_keyval.shape[2] // head_dim
    groups = heads_here // kv_here
    gains = norm_gains.astype(F32)
    head_gains = qk_gains.astype(F32)
    kernel = conv_kernel.astype(F32)
    hidden = ffn_down.shape[2]
    gate_up_w = ffn_gate_up[0].reshape(width, 2 * hidden)
    down_w = ffn_down[0]
    home = rows * chips * seq_local

    def mate(values, section):
        return permute(values, section, "tensor", lambda i: i ^ 1)

    def chip_gather(values, section):
        held = values[:, None]
        for step in steps:
            other = permute(held, section, "tensor", lambda i: i ^ (2 * step))
            upper = (chip // step) % 2 == 1
            held = jnp.where(
                upper,
                jnp.concatenate([other, held], axis=1),
                jnp.concatenate([held, other], axis=1),
            )
        return held

    def chip_sum(values, section):
        for step in steps:
            values = values + permute(
                values.astype(BF), section, "tensor", lambda i: i ^ (2 * step)
            ).astype(F32)
        return values

    def chip_scatter(values, section):
        for step in reversed(steps):
            halves = values.reshape((rows, 2, step) + values.shape[2:])
            upper = (chip // step) % 2
            kept = pick(halves, upper, 1)
            sent = pick(halves, 1 - upper, 1).astype(BF)
            values = kept + permute(sent, section, "tensor", lambda i: i ^ (2 * step)).astype(F32)
        return values[:, 0]

    def weave(mine, other):
        both = jnp.where(
            core == 0, jnp.stack([mine, other], axis=2), jnp.stack([other, mine], axis=2)
        )
        return both.reshape((rows, seq) + mine.shape[3:])

    def part(full, index):
        return pick(full.reshape((rows, chips, 2, seq_local) + full.shape[2:]), index, 2)

    def core_sum(mine, sent, section):
        return mine + mate(sent, section).astype(F32)

    def when(section, function, *args):
        shapes = jax.eval_shape(function, *args)
        zeros = lambda *unused: jax.tree.map(lambda s: jnp.zeros(s.shape, s.dtype), shapes)
        return lax.cond(is_first if section == 0 else ~is_first, function, zeros, *args)

    def conv_parts(project, masks_list):
        gate_in = project[:, :, 0] * project[:, :, 2]
        running = kernel[0] * gate_in
        for lag in range(1, kernel.shape[0]):
            running = running + kernel[lag] * delay_rows(gate_in, lag) * masks_list[lag - 1]
        return gate_in, running

    def outward(full_in, weight):
        mine = mm("rkte,ed->rktd", part(full_in, core), weight)
        sent = mm("rkte,ed->rktd", part(full_in, 1 - core), weight, BF)
        return mine, sent

    def conv_forward(mine, other):
        full = weave(mine, other)
        project = mm("rtd,dce->rtce", full, conv_in)
        unused, running = conv_parts(project, lag_masks(segments, kernel.shape[0]))
        mixed = (project[:, :, 1] * running).astype(BF)
        return outward(mixed, conv_out) + (project.astype(BF), mixed, full)

    def arrange(query, keyed, valued):
        q_all = query.reshape(rows, seq, kv_here, groups, head_dim).transpose(0, 2, 3, 1, 4)
        return (q_all, keyed.transpose(0, 2, 1, 3), valued.transpose(0, 2, 1, 3))

    def attn_forward(mine, other):
        full = weave(mine, other)
        query_raw = mm("rtd,de->rte", full, attn_query).reshape(rows, seq, heads_here, head_dim)
        keyval_raw = mm("rtd,dce->rtce", full, attn_keyval)
        key_raw = keyval_raw[:, :, 0].reshape(rows, seq, kv_here, head_dim)
        val_raw = keyval_raw[:, :, 1].reshape(rows, seq, kv_here, head_dim)
        cosine, sine = rope_tables(segments, head_dim // 2)
        query = head_prep(query_raw, head_gains[0], cosine, sine).astype(BF)
        keyed = head_prep(key_raw, head_gains[1], cosine, sine).astype(BF)
        q_all, k_all, v_all = arrange(query, keyed, val_raw.astype(BF))
        attended, logsum = lax.map(lambda item: attend_row(*item), (q_all, k_all, v_all, segments))
        flat = attended.transpose(0, 3, 1, 2, 4).reshape(rows, seq, heads_here * head_dim)
        saved = (query_raw, key_raw, q_all, k_all, v_all, logsum, flat, full)
        return outward(flat, attn_out) + saved

    def conv_backward(mine, other, project, mixed, full):
        grad_full = weave(mine, other)
        masks_list = lag_masks(segments, kernel.shape[0])
        project = project.astype(F32)
        gate_in, running = conv_parts(project, masks_list)
        grad_mixed = mm("rtd,ed->rte", grad_full, conv_out)
        grad_c = grad_mixed * running
        grad_run = grad_mixed * project[:, :, 1]
        grad_in = kernel[0] * grad_run
        grad_kernel = [jnp.sum(grad_run * gate_in, axis=(0, 1))]
        for lag in range(1, kernel.shape[0]):
            mask = masks_list[lag - 1]
            grad_in = grad_in + kernel[lag] * advance_rows(grad_run * mask, lag)
            grad_kernel.append(jnp.sum(grad_run * mask * delay_rows(gate_in, lag), axis=(0, 1)))
        grad_low = jnp.stack(
            [grad_in * project[:, :, 2], grad_c, grad_in * project[:, :, 0]], axis=2
        ).astype(BF)
        mine_in = mm("rktce,dce->rktd", part(grad_low, core), conv_in)
        sent_in = mm("rktce,dce->rktd", part(grad_low, 1 - core), conv_in, BF)
        grad_cout = mm("rte,rtd->ed", mixed, grad_full, BF)
        grad_cin = mm("rtd,rtce->dce", full, grad_low, BF)
        return mine_in, sent_in, (grad_cin, jnp.stack(grad_kernel).astype(BF), grad_cout)

    def attn_backward(mine, other, query_raw, key_raw, q_all, k_all, v_all, logsum, flat, full):
        grad_full = weave(mine, other)
        cosine, sine = rope_tables(segments, head_dim // 2)
        unused, query_pull = jax.vjp(
            lambda values, gain: head_prep(values, gain, cosine, sine), query_raw, head_gains[0]
        )
        unused, key_pull = jax.vjp(
            lambda values, gain: head_prep(values, gain, cosine, sine), key_raw, head_gains[1]
        )
        grad_flat = mm("rtd,ed->rte", grad_full, attn_out, BF)
        grad_heads = grad_flat.reshape(rows, seq, kv_here, groups, head_dim).transpose(
            0, 2, 3, 1, 4
        )
        grad_q, grad_k, grad_v = lax.map(
            lambda item: attend_back(*item), (q_all, k_all, v_all, segments, logsum, grad_heads)
        )
        grad_qraw, grad_qgain = query_pull(
            grad_q.transpose(0, 3, 1, 2, 4).reshape(rows, seq, heads_here, head_dim)
        )
        grad_kraw, grad_kgain = key_pull(grad_k.transpose(0, 2, 1, 3))
        query_low = grad_qraw.reshape(rows, seq, heads_here * head_dim).astype(BF)
        kv_low = jnp.stack(
            [
                grad_kraw.reshape(rows, seq, kv_here * head_dim),
                grad_v.transpose(0, 2, 1, 3).reshape(rows, seq, kv_here * head_dim),
            ],
            axis=2,
        ).astype(BF)

        def inward(index):
            return mm("rkte,de->rktd", part(query_low, index), attn_query) + mm(
                "rktce,dce->rktd", part(kv_low, index), attn_keyval
            )

        mine_in = inward(core)
        sent_in = inward(1 - core).astype(BF)
        grad_aout = mm("rte,rtd->ed", flat, grad_full, BF)
        grad_aq = mm("rtd,rte->de", full, query_low, BF)
        grad_akv = mm("rtd,rtce->dce", full, kv_low, BF)
        return (
            mine_in,
            sent_in,
            (grad_aq, grad_akv, grad_aout),
            jnp.stack([grad_qgain, grad_kgain]),
        )

    def flat_tokens(mine, other):
        return jnp.stack([mine, other]).reshape(2 * home, mine.shape[-1])

    def gate_up(both):
        return mm("td,df->tf", both, gate_up_w, BF)

    def activate(gu):
        gate = gu[:, :hidden].astype(F32)
        return (jax.nn.silu(gate) * gu[:, hidden:].astype(F32)).astype(BF)

    def shaped(tokens):
        return tokens.reshape(rows, chips, seq_local, width)

    def ffn_out(act):
        mine = mm("tf,df->td", act[:home], down_w)
        sent = mm("tf,df->td", act[home:], down_w, BF)
        return shaped(mine), shaped(sent)

    def ffn_back(grad_both, gu):
        grad_act = mm("td,df->tf", grad_both, down_w)
        gate = gu[:, :hidden].astype(F32)
        up = gu[:, hidden:].astype(F32)
        sig = jax.nn.sigmoid(gate)
        slope = sig * (1.0 + gate * (1.0 - sig))
        grad_gu = jnp.concatenate([grad_act * up * slope, grad_act * gate * sig], axis=1).astype(BF)
        mine = mm("tf,df->td", grad_gu[:home], gate_up_w)
        sent = mm("tf,df->td", grad_gu[home:], gate_up_w, BF)
        return grad_gu, shaped(mine), shaped(sent)

    def ffn_weights(both, gu, grad_both, grad_gu):
        act = activate(gu)
        grad_down = mm("td,tf->df", grad_both, act, BF)
        grad_up = mm("td,tf->df", both, grad_gu, BF)
        return grad_up, grad_down

    x_home = chip_gather(local, 0).astype(F32)
    cot_home = chip_gather(local, 1)
    cot_mate = mate(cot_home, 1)
    cot_both = flat_tokens(cot_home, cot_mate)

    z_home = norm(x_home, gains[0, 0])
    mine, sent, project, mixed, full1 = when(0, conv_forward, z_home, mate(z_home, 0))
    h1 = x_home + chip_sum(core_sum(mine, sent, 0), 0)
    z_home = norm(h1, gains[0, 1])
    both1 = flat_tokens(z_home, mate(z_home, 0))
    gu1 = gate_up(both1)
    mine, sent = ffn_out(activate(gu1))
    x2_local = pick(h1, chip, 1) + chip_scatter(core_sum(mine, sent, 0), 0)

    crossing = lax.ppermute(x2_local.astype(BF), "section", [(0, 1)])
    x2_home = chip_gather(crossing, 1).astype(F32)
    z_home = norm(x2_home, gains[1, 0])
    mine, sent, *saved = when(1, attn_forward, z_home, mate(z_home, 1))
    h3 = x2_home + chip_sum(core_sum(mine, sent, 1), 1)
    z_home = norm(h3, gains[1, 1])
    both2 = flat_tokens(z_home, mate(z_home, 1))
    gu2 = gate_up(both2)

    grad_gu2, mine, sent = ffn_back(cot_both, gu2)
    dz = chip_sum(core_sum(mine, sent, 1), 1)
    grad_norm, gain_terms = norm_back(h3, gains[1, 1], dz)
    gain_ffn2 = jnp.sum(pick(gain_terms, chip, 1), axis=(0, 1))
    gh3 = cot_home.astype(F32) + grad_norm
    gm_home = gh3.astype(BF)
    mine, sent, attn_grads, head_grads = when(
        1, attn_backward, gm_home, mate(gm_home, 1), *saved
    )
    dz = chip_scatter(core_sum(mine, sent, 1), 1)
    grad_norm, gain_terms = norm_back(pick(x2_home, chip, 1), gains[1, 0], dz)
    gain_mix2 = jnp.sum(gain_terms, axis=(0, 1))
    gx2_local = pick(gh3, chip, 1) + grad_norm

    crossing = lax.ppermute(gx2_local.astype(BF), "section", [(1, 0)])
    g_home = chip_gather(crossing, 0)
    g_both = flat_tokens(g_home, mate(g_home, 0))

    grad_gu1, mine, sent = ffn_back(g_both, gu1)
    late = (both1, gu1, g_both, grad_gu1, both2, gu2, cot_both, grad_gu2)
    grad_up, grad_down, mine_y, sent_y = lax.cond(
        is_first,
        lambda *args: ffn_weights(*args[:4])
        + (jnp.zeros((rows, chips, seq_local, width), F32), jnp.zeros((rows, chips, seq_local, width), BF)),
        lambda *args: ffn_weights(*args[4:]) + ffn_out(activate(args[5])),
        *late,
    )
    full_gu = lax.psum(grad_up, "dp")
    full_down = lax.psum(grad_down, "dp")
    y_local = pick(h3, chip, 1) + chip_scatter(core_sum(mine_y, sent_y, 1), 1)
    dz = chip_sum(core_sum(mine, sent, 0), 0)
    grad_norm, gain_terms = norm_back(h1, gains[0, 1], dz)
    gain_ffn1 = jnp.sum(pick(gain_terms, chip, 1), axis=(0, 1))
    gh1 = g_home.astype(F32) + grad_norm
    gm_home = gh1.astype(BF)
    mine, sent, conv_grads = when(
        0, conv_backward, gm_home, mate(gm_home, 0), project, mixed, full1
    )
    dz = chip_scatter(core_sum(mine, sent, 0), 0)
    grad_norm, gain_terms = norm_back(pick(x_home, chip, 1), gains[0, 0], dz)
    gain_mix1 = jnp.sum(gain_terms, axis=(0, 1))
    gx_local = pick(gh1, chip, 1) + grad_norm

    mixer_sums = jax.tree.map(
        lambda v: v.astype(F32), lax.psum(conv_grads + attn_grads, ("section", "dp"))
    )
    zero = jnp.zeros_like(gain_mix1)
    first_gains = jnp.stack([jnp.stack([gain_mix1, gain_ffn1]), jnp.stack([zero, zero])])
    second_gains = jnp.stack([jnp.stack([zero, zero]), jnp.stack([gain_mix2, gain_ffn2])])
    grad_gains = jnp.where(is_first, first_gains, second_gains)
    grad_gains, grad_heads = lax.psum((grad_gains, head_grads), ("section", "tensor", "dp"))
    boundary_out = jnp.where(is_first, gx_local, y_local)[None]
    return (boundary_out, grad_gains, grad_heads) + mixer_sums + (
        full_gu.astype(F32).reshape(ffn_gate_up.shape),
        full_down.astype(F32)[None],
    )


def solution(mesh):
    placed = (
        P("section", "dp", "tensor", None),
        P("dp", None),
        P(),
        P(),
        P(None, None, "tensor"),
        P(None, "tensor"),
        P("tensor", None),
        P(None, "tensor"),
        P(None, None, "tensor"),
        P("tensor", None),
        P("section", None, None, "tensor"),
        P("section", None, "tensor"),
    )
    return jax.shard_map(
        on_device,
        mesh=mesh,
        in_specs=placed,
        out_specs=(
            P("section", "dp", "tensor", None),
            P(),
            P(),
            P(None, None, "tensor"),
            P(None, "tensor"),
            P("tensor", None),
            P(None, "tensor"),
            P(None, None, "tensor"),
            P("tensor", None),
            P("section", None, None, "tensor"),
            P("section", None, "tensor"),
        ),
        check_vma=False,
    )
```

time: 2900 us -> 2160 us (0.74)
  waiting for transfers between devices: 1880 us -> 1330 us
  matrix products: 429 us -> 306 us
  local copies, waits for them, and re-layouts: 208 us -> 124 us
  starting transfers between devices: 16 us -> 65.9 us
  loops' own time: 56.4 us -> 18.4 us
    reduce_scatter x12 -> x0, waiting for transfers between devices: 780 us -> none  [reduce_tokens(): return lax.psum_scatter(values, 'tensor', scatter_dimension=1, tiled=True)]
    ppermute x6 -> x30, waiting for transfers between devices: 126 us -> 886 us  [the longest x1 586 us: on_device(): crossing = lax.ppermute(gx2_local.astype(BF), 'section', [(1, 0)])]
    all_gather x12 -> x0, waiting for transfers between devices: 283 us -> none  [gather_tokens(): return lax.all_gather(values, 'tensor', axis=1, tiled=True)]
    psum x2, waiting for transfers between devices: 695 us -> 445 us  [the longest x1 245 us: on_device(): lax.psum(conv_grads + attn_grads, ('section', 'dp'))]
    dot_general x39 -> x20, matrix products: 429 us -> 306 us  [mm(): jnp.einsum(spec, left, right, preferred_element_type=F32).astype(kind)]
    squeeze x9 -> x0, local copies, waits for them, and re-layouts: 53.8 us -> none  [backward_step(): saved = jax.tree.map(lambda stacked: stacked[saved_index], saved_stack)]
    ppermute x6 -> x30, starting transfers between devices: 14.1 us -> 65.8 us  [the longest x28 63.1 us: permute(): return lax.ppermute(values, ('section', axis), pairs)]
    another operation x8 -> x4, loops' own time: 56.4 us -> 9.24 us  [when(): lax.cond(is_first if section == 0 else ~is_first, function, zeros, *args)]
  transfers between devices with their start and end apart: 32 -> 32, of which waited for: 32 -> 14; matrix products, arithmetic and copies ran while one was open for 11% -> 11% of each run, Pallas kernels for 0% -> 0%
where the time goes in v1:
time: 2160 us; the launch traced here: 2150 us
  waiting for transfers between devices  1330 us (62%)
  matrix products  306 us (14%)
  other arithmetic  223 us (10%)
  local copies, waits for them, and re-layouts  124 us (6%)
  starting transfers between devices  65.9 us (3%)
  blocking collectives  64 us (3%)
    ppermute x1, waiting for transfers between devices, on_device(): crossing = lax.ppermute(gx2_local.astype(BF), 'section', [(1, 0)])  586 us
    dot_general x20, matrix products, mm(): jnp.einsum(spec, left, right, preferred_element_type=F32).astype(kind)  306 us
    ppermute x28, waiting for transfers between devices, permute(): return lax.ppermute(values, ('section', axis), pairs)  267 us
    psum x1, waiting for transfers between devices, on_device(): lax.psum(conv_grads + attn_grads, ('section', 'dp'))  245 us
    psum x1, waiting for transfers between devices, on_device(): full_gu = lax.psum(grad_up, 'dp')  200 us
    ppermute x28, starting transfers between devices, permute(): return lax.ppermute(values, ('section', axis), pairs)  63.1 us
    psum x1, blocking collectives, on_device(): lax.psum((grad_gains, head_grads), ('section', 'tensor', 'dp'))  44.6 us
  transfers between devices with their start and end apart: 32, of which 14 were waited for; matrix products, arithmetic and copies ran while one was open for 11% of the time, Pallas kernels for 0%

profile of v1, /device:TPU:0, one launch (start us, length us, event | category | flops | bytes accessed | tf_op | source)
XLA Modules:
  0.0 2147.5 jit_solution(5253187860334628724)
XLA Ops:
  7.2 5.0 collective-permute-start.1
  13.6 33.2 %collective-permute-done.1 = bf16[2,1,256,1536]{3,2,0,1:T(8,128)(2,1)S(1)} collective-permute-done((bf16[2,1,256,1536]{3,2,0,1:T(8,128)(2,1)}, bf16[2,1,256,1536]{3,2,0,1:T(8,128)(2,1)S(1)}, u32[]{:S(2)}, u32[]{:S(2)}) %collective-permute-start.1) | collective-permute-done | bytes 1572896 | tf_op jit(solution)/shard_map/ppermute | solution.py:43
  54.1 5.9 collective-permute-done.2
  60.1 33.2 %conditional.6 = (bf16[2,2,256,1536]{3,2,1,0:T(8,128)(2,1)}, bf16[2,1024,3,384]{3,1,2,0:T(8,128)(2,1)}, bf16[2,1024,384]{2,1,0:T(8,128)(2,1)}, bf16[2,1024,1536]{2,1,0:T(8,128)(2,1)}, f32[2,2,256,1536]{3,2,0,1:T(8,128)}) conditional(s32[]{:T(128)} %convert_element_type.359, () %tuple.67, (s32[]{:T(128)}, bf16[2,2,256,1536]{3,2,0,1:T(8,128)(2,1)}, ...), branch_computations={%region_1.2_spmd, %region_2.3_spmd} | conditional | flops 9684918272 | bytes 123918008 | solution.py:235
  68.2 11.8 fusion.244
  82.6 4.6 convolution_convert_fusion.3
  97.8 5.0 collective-permute-done.3
  102.9 4.0 fusion.203
  110.6 68.4 %collective-permute-done.4 = bf16[2,2,256,1536]{3,2,0,1:T(8,128)(2,1)S(1)} collective-permute-done((bf16[2,2,256,1536]{3,2,0,1:T(8,128)(2,1)S(1)}, bf16[2,2,256,1536]{3,2,0,1:T(8,128)(2,1)S(1)}, u32[]{:S(2)}, u32[]{:S(2)}) %collective-permute-start.4) | collective-permute-done | bytes 3145760 | tf_op jit(solution)/shard_map/ppermute | solution.py:43
  179.0 4.7 multiply_reduce_fusion.16
  190.2 5.6 collective-permute-done.5
  197.1 30.1 %convolution_convert_fusion.5 = bf16[2048,3456]{1,0:T(8,128)(2,1)} fusion(bf16[2048,1536]{1,0:T(8,128)(2,1)S(1)} %bitcast.619, bf16[1536,3456]{0,1:T(8,128)(2,1)} %bitcast.656), kind=kOutput, calls=%fused_computation.314 | convolution fusion | flops 21750349824 | bytes 31064064 | tf_op jit(solution)/shard_map/td,df->tf/dot_general | solution.py:14
  227.2 9.7 fusion.164
  236.9 12.3 fusion.209
  251.5 5.5 collective-permute-done.6
  257.0 7.9 convert_add_fusion.8
  271.5 34.7 %collective-permute-done.7 = bf16[2,1,256,1536]{3,2,1,0:T(8,128)(2,1)S(1)} collective-permute-done((bf16[2,1,256,1536]{3,2,1,0:T(8,128)(2,1)S(1)}, bf16[2,1,256,1536]{3,2,1,0:T(8,128)(2,1)S(1)}, u32[]{:S(2)}, u32[]{:S(2)}) %collective-permute-start.7) | collective-permute-done | bytes 1572896 | tf_op jit(solution)/shard_map/ppermute | solution.py:43
  311.2 33.3 %collective-permute-done.8 = bf16[2,256,1536]{2,1,0:T(8,128)(2,1)S(1)} collective-permute-done((bf16[2,256,1536]{2,1,0:T(8,128)(2,1)S(1)}, bf16[2,256,1536]{2,1,0:T(8,128)(2,1)S(1)}, u32[]{:S(2)}, u32[]{:S(2)}) %collective-permute-start.8) | collective-permute-done | bytes 1572896 | tf_op jit(solution)/shard_map/ppermute | solution.py:393
  350.4 19.3 conditional.14
  373.9 4.2 fusion.204
  385.5 5.2 multiply_reduce_fusion.14
  405.5 30.2 %convolution_convert_fusion.4 = bf16[2048,3456]{1,0:T(8,128)(2,1)} fusion(bf16[2048,1536]{1,0:T(8,128)(2,1)S(1)} %bitcast.623, bf16[1536,3456]{0,1:T(8,128)(2,1)} %bitcast.657), kind=kOutput, calls=%fused_computation.313 | convolution fusion | flops 21750349824 | bytes 31064064 | tf_op jit(solution)/shard_map/td,df->tf/dot_general | solution.py:14
  435.7 25.7 %fusion.173 = (bf16[2048,1728]{1,0:T(8,128)(2,1)}, bf16[2048,1728]{1,0:T(8,128)(2,1)}) fusion(bf16[2048,3456]{1,0:T(8,128)(2,1)} %convolution_convert_fusion.4, bf16[2048,1536]{1,0:T(8,128)(2,1)} %bitcast.621, bf16[1,1536,1728]{1,2,0:T(8,128)(2,1)} %param.41), kind=kOutput, calls=%fused_computation.324 | convolution fusion | flops 10924720128 | bytes 39911424 | tf_op jit(solution)/shard_map/td,df->tf/dot_general | solution.py:14
  461.4 17.2 fusion.212
  483.1 15.3 fusion.205
  500.6 9.8 multiply_reduce_fusion.13
  510.5 9.7 fusion.243
  522.5 13.7 conditional.15
  539.2 3.8 convert_add_fusion.4
  550.2 586.3 %collective-permute-done.20 = bf16[2,256,1536]{2,1,0:T(8,128)(2,1)S(1)} collective-permute-done((bf16[2,256,1536]{2,1,0:T(8,128)(2,1)S(1)}, bf16[2,256,1536]{2,1,0:T(8,128)(2,1)S(1)}, u32[]{:S(2)}, u32[]{:S(2)}) %collective-permute-start.20) | collective-permute-done | bytes 1572896 | tf_op jit(solution)/shard_map/ppermute | solution.py:416
  1140.0 33.3 %collective-permute-done.21 = bf16[2,1,256,1536]{3,2,0,1:T(8,128)(2,1)S(1)} collective-permute-done((bf16[2,1,256,1536]{3,2,0,1:T(8,128)(2,1)S(1)}, bf16[2,1,256,1536]{3,2,0,1:T(8,128)(2,1)S(1)}, u32[]{:S(2)}, u32[]{:S(2)}) %collective-permute-start.21) | collective-permute-done | bytes 1572896 | tf_op jit(solution)/shard_map/ppermute | solution.py:43
  1177.7 7.9 copy.171
  1185.7 15.6 pad_maximum_fusion.3
  1207.7 25.5 %fusion.166 = (bf16[2048,1728]{1,0:T(8,128)(2,1)}, bf16[2048,1728]{1,0:T(8,128)(2,1)}) fusion(bf16[2048,3456]{1,0:T(8,128)(2,1)} %convolution_convert_fusion.5, bf16[2048,1536]{1,0:T(8,128)(2,1)} %bitcast.625, bf16[1,1536,1728]{1,2,0:T(8,128)(2,1)} %param.41), kind=kOutput, calls=%fused_computation.317 | convolution fusion | flops 10924720128 | bytes 39911424 | tf_op jit(solution)/shard_map/td,df->tf/dot_general | solution.py:14
  1233.2 15.6 pad_maximum_fusion.4
  1248.8 64.1 %conditional.17 = (bf16[1536,3456]{1,0:T(8,128)(2,1)}, bf16[1536,1728]{0,1:T(8,128)(2,1)}, bf16[2,2,256,1536]{3,2,1,0:T(8,128)(2,1)}, f32[2,2,256,1536]{3,2,0,1:T(8,128)}) conditional(s32[]{:T(128)} %convert_element_type.359, (bf16[2048,1536]{1,0:T(8,128)(2,1)}, bf16[2048,3456]{1,0:T(8,128)(2,1)}, bf16[2048,3456]{1,0:T(8,128)(2,1)}, ...), branch_computations={%region_42.43_spmd, %region_43.44_spmd} | conditional | flops 43516428288 | bytes 209453216
  1257.8 30.9 %fusion.246 = bf16[1536,3456]{1,0:T(8,128)(2,1)} fusion(bf16[2048,1536]{1,0:T(8,128)(2,1)} %get-tuple-element.346, bf16[2048,3456]{1,0:T(8,128)(2,1)} %get-tuple-element.347), kind=kOutput, calls=%fused_computation.463 | convolution fusion | flops 21743271936 | bytes 31064064 | tf_op jit(solution)/shard_map/cond/branch_1_fun/td,tf->df/dot_general | solution.py:14
  1288.7 18.8 convolution_bitcast_fusion.1
  1313.0 14.4 copy.213
  1327.5 16.9 fusion.215
  1347.5 5.6 fusion.183
  1353.2 13.9 fusion.206
  1370.6 69.0 %collective-permute-done.24 = bf16[2,2,256,1536]{3,2,0,1:T(8,128)(2,1)S(1)} collective-permute-done((bf16[2,2,256,1536]{3,2,0,1:T(8,128)(2,1)}, bf16[2,2,256,1536]{3,2,0,1:T(8,128)(2,1)S(1)}, u32[]{:S(2)}, u32[]{:S(2)}) %collective-permute-start.24) | collective-permute-done | bytes 3145760 | tf_op jit(solution)/shard_map/ppermute | solution.py:43
  1441.3 10.9 multiply_reduce_fusion.12
  1452.2 7.9 fusion.242
  1462.0 6.0 collective-permute-done.25
  1468.0 66.6 %conditional.16 = (bf16[2,2,256,1536]{3,2,1,0:T(8,128)(2,1)}, bf16[1536,3,384]{0,2,1:T(8,128)(2,1)S(1)}, bf16[3,384]{1,0:T(4,128)(2,1)}, bf16[384,1536]{0,1:T(8,128)(2,1)}, f32[2,2,256,1536]{3,2,0,1:T(8,128)}) conditional(s32[]{:T(128)} %convert_element_type.359, () %tuple.73, (f32[3,384]{1,0:T(4,128)S(1)}, s32[]{:T(128)}, ...), branch_computations={%region_36.37_spmd, %region_37.41_spmd} | conditional | flops 19374551040 | bytes 225383968 | solution.py:235
  1475.5 5.9 fusion.156
  1486.4 16.0 multiply_reduce_fusion.11
  1503.0 4.0 multiply_convert_fusion.3
  1508.4 10.0 fusion.144
  1521.5 5.7 bitcast_convert_fusion.1
  1527.2 4.2 convolution_bitcast_fusion.5
  1559.1 5.1 convert_add_fusion.1
  1569.2 8.1 convert_add_fusion
  1577.3 4.0 dynamic-slice_convert_fusion
  1586.4 19.4 psum.73
  1606.4 4.3 fusion.225
  1610.8 44.6 %all-reduce.16 = (f32[2,2,1536]{2,1,0:T(2,128)}, f32[2,64]{1,0:T(2,128)}) all-reduce(f32[2,2,1536]{2,1,0:T(2,128)S(1)} %pad_select_fusion, f32[2,64]{1,0:T(2,128)} %get-tuple-element.412), channel_id=1, replica_groups=mesh['section'=2,'tensor'=4,'dp'=4] {'section','tensor','dp'}, use_global_device_ids=true, to_apply=%region_48.49 | all-reduce | flops 6272 | bytes 50176 | tf_op jit(solution)/shard_map/psum | solution.py:452
  1655.4 9.5 bitcast_select_fusion
  1664.9 200.1 %all-reduce.24.cloned.1.call-done = (bf16[1,1536,2,1728]{1,3,2,0:T(8,128)(2,1)}, bf16[1,1536,1728]{1,2,0:T(8,128)(2,1)}) async-done(((bf16[1,1536,2,1728]{1,3,2,0:T(8,128)(2,1)}, bf16[1,1536,1728]{1,2,0:T(8,128)(2,1)}), (bf16[1,1536,2,1728]{1,3,2,0:T(8,128)(2,1)}, bf16[1,1536,1728]{1,2,0:T(8,128)(2,1)})) %all-reduce.24.cloned.1.call-update) | async-done | bytes 15925264 | tf_op jit(solution)/shard_map/psum | solution.py:429
  1865.1 13.0 reshape.584
  1878.1 5.6 broadcast_in_dim.82
  1883.7 244.6 %all-reduce.22.cloned.1.call-done = (bf16[1536,3,384]{2,0,1:T(8,128)(2,1)}, bf16[384,1536]{1,0:T(8,128)(2,1)}, bf16[1536,384]{1,0:T(8,128)(2,1)}, bf16[1536,2,128]{2,1,0:T(2,128)(2,1)}, bf16[384,1536]{1,0:T(8,128)(2,1)}) async-done(((bf16[1536,3,384]{2,0,1:T(8,128)(2,1)}, bf16[384,1536]{1,0:T(8,128)(2,1)}, bf16[1536,384]{1,0:T(8,128)(2,1)}, bf16[1536,2,128]{2,1,0:T(2,128)(2,1)}, ...) | async-done | bytes 7864336 | tf_op jit(solution)/shard_map/psum | solution.py:446
  (320 shorter events, 227.9 us)
Async XLA Ops:
  7.2 42.8 %copy-start.10 = (bf16[1,2,256,1536]{3,2,1,0:T(8,128)(2,1)S(1)}, bf16[1,2,256,1536]{3,2,1,0:T(8,128)(2,1)}, u32[]{:S(2)}) copy-start(bf16[1,2,256,1536]{3,2,1,0:T(8,128)(2,1)} %param.30) | copy-start | bytes 4718596
  7.2 1857.9 %all-reduce.24.cloned.1.call-start = ((), (), s32[]{:S(2)}) async-start(), calls=%async_computation.1 | async-start | bytes 31850496 | tf_op jit(solution)/shard_map/psum | solution.py:429
  7.2 39.6 %collective-permute-start.1 = (bf16[2,1,256,1536]{3,2,0,1:T(8,128)(2,1)}, bf16[2,1,256,1536]{3,2,0,1:T(8,128)(2,1)S(1)}, u32[]{:S(2)}, u32[]{:S(2)}) collective-permute-start(bf16[2,1,256,1536]{3,2,0,1:T(8,128)(2,1)} %bitcast.578), channel_id=1, source_target_pairs={{0,8},{4,12},{8,0},{12,4},{1,9},{5,13},{9,1},{13,5},{2,10},{6,14},... | collective-permute-start | bytes 4718600 | tf_op jit(solution)/shard_map/ppermute | solution.py:43
  13.6 38.5 %copy-start.74 = (f32[1536]{0:T(1024)}, f32[1536]{0:T(1024)S(1)}, u32[]{:S(2)}) copy-start(f32[1536]{0:T(1024)S(1)} %get-tuple-element.605) | copy-start | bytes 18436
  13.6 170.0 %copy-start.71 = (f32[1536]{0:T(1024)}, f32[1536]{0:T(1024)S(1)}, u32[]{:S(2)}) copy-start(f32[1536]{0:T(1024)S(1)} %get-tuple-element.604) | copy-start | bytes 18436
  13.6 332.9 %copy-start.76 = (f32[1536]{0:T(1024)}, f32[1536]{0:T(1024)S(1)}, u32[]{:S(2)}) copy-start(f32[1536]{0:T(1024)S(1)} %get-tuple-element.603) | copy-start | bytes 18436
  46.8 132.1 %copy-start.21 = (bf16[2,1,256,1536]{3,2,0,1:T(8,128)(2,1)}, bf16[2,1,256,1536]{3,2,0,1:T(8,128)(2,1)S(1)}, u32[]{:S(2)}) copy-start(bf16[2,1,256,1536]{3,2,0,1:T(8,128)(2,1)S(1)} %collective-permute-done.1) | copy-start | bytes 4718596
  52.2 7.9 collective-permute-start.2
  95.3 7.6 collective-permute-start.3
  106.9 72.0 %collective-permute-start.4 = (bf16[2,2,256,1536]{3,2,0,1:T(8,128)(2,1)S(1)}, bf16[2,2,256,1536]{3,2,0,1:T(8,128)(2,1)S(1)}, u32[]{:S(2)}, u32[]{:S(2)}) collective-permute-start(bf16[2,2,256,1536]{3,2,0,1:T(8,128)(2,1)S(1)} %fusion.203), channel_id=1, source_target_pairs={{0,8},{4,12},{8,0},{12,4},{1,9},{5,13},{9,1},{13,5},{2,10},{6,14},... | collective-permute-start | bytes 9437192 | tf_op jit(solution)/shard_map/ppermute | solution.py:43
  188.2 7.5 collective-permute-start.5
  197.0 30.2 %copy-start.33 = (bf16[2,2,2,256,1536]{4,3,2,1,0:T(8,128)(2,1)}, bf16[2,2,2,256,1536]{4,3,2,1,0:T(8,128)(2,1)S(1)}, u32[]{:S(2)}) copy-start(bf16[2,2,2,256,1536]{4,3,2,1,0:T(8,128)(2,1)S(1)} %copy.170) | copy-start | bytes 18874372
  236.9 12.3 copy-start.23
  249.3 7.8 collective-permute-start.6
  267.8 38.4 %collective-permute-start.7 = (bf16[2,1,256,1536]{3,2,1,0:T(8,128)(2,1)S(1)}, bf16[2,1,256,1536]{3,2,1,0:T(8,128)(2,1)S(1)}, u32[]{:S(2)}, u32[]{:S(2)}) collective-permute-start(bf16[2,1,256,1536]{3,2,1,0:T(8,128)(2,1)S(1)} %dynamic-slice_convert_fusion.3), channel_id=1, source_target_pairs={{0,8},{4,12},{8,0},{12,4},{1,9},{5,13},{9,1},{13,5},{2,10},{6,14},... | collective-permute-start | bytes 4718600 | tf_op jit(solution)/shard_map/ppermute | solution.py:43
  309.8 34.7 %collective-permute-start.8 = (bf16[2,256,1536]{2,1,0:T(8,128)(2,1)S(1)}, bf16[2,256,1536]{2,1,0:T(8,128)(2,1)S(1)}, u32[]{:S(2)}, u32[]{:S(2)}) collective-permute-start(bf16[2,256,1536]{2,1,0:T(8,128)(2,1)S(1)} %fusion.235), channel_id=1, source_target_pairs={{0,16},{1,17},{2,18},{3,19},{4,20},{5,21},{6,22},{7,23},{8,24},{9,... | collective-permute-start | bytes 4718600 | tf_op jit(solution)/shard_map/ppermute | solution.py:393
  344.5 0.8 collective-permute-start.9
  347.6 2.3 collective-permute-start.10
  373.0 0.9 collective-permute-start.11
  378.1 7.3 collective-permute-start.12
  380.5 0.8 collective-permute-start
  384.4 14.0 collective-permute-start.13
  395.2 7.2 collective-permute-start.14
  405.5 30.2 %copy-start.35 = (bf16[2,2,2,256,1536]{4,3,2,1,0:T(8,128)(2,1)}, bf16[2,2,2,256,1536]{4,3,2,1,0:T(8,128)(2,1)S(1)}, u32[]{:S(2)}) copy-start(bf16[2,2,2,256,1536]{4,3,2,1,0:T(8,128)(2,1)S(1)} %copy.182) | copy-start | bytes 18874372
  461.4 18.4 slice-start.8
  461.4 18.4 slice-start.10
  461.4 18.4 slice-start.9
  461.4 18.4 slice-start.11
  478.9 4.2 collective-permute-start.15
  498.3 2.3 collective-permute-start.16
  510.5 12.1 copy-start.3
  510.5 12.1 copy-start.59
  510.5 12.1 copy-start.88
  520.2 2.3 collective-permute-start.17
  538.3 0.9 collective-permute-start.18
  543.3 2.6 collective-permute-start.19
  548.9 587.6 %collective-permute-start.20 = (bf16[2,256,1536]{2,1,0:T(8,128)(2,1)S(1)}, bf16[2,256,1536]{2,1,0:T(8,128)(2,1)S(1)}, u32[]{:S(2)}, u32[]{:S(2)}) collective-permute-start(bf16[2,256,1536]{2,1,0:T(8,128)(2,1)S(1)} %fusion.233), channel_id=1, source_target_pairs={{16,0},{17,1},{18,2},{19,3},{20,4},{21,5},{22,6},{23,7},{24,8},{25... | collective-permute-start | bytes 4718600 | tf_op jit(solution)/shard_map/ppermute | solution.py:416
  1136.4 64.9 %copy-start.26 = (bf16[2,256,1536]{2,1,0:T(8,128)(2,1)}, bf16[2,256,1536]{2,1,0:T(8,128)(2,1)S(1)}, u32[]{:S(2)}) copy-start(bf16[2,256,1536]{2,1,0:T(8,128)(2,1)S(1)} %collective-permute-done.20) | copy-start | bytes 4718596
  1136.4 36.9 %collective-permute-start.21 = (bf16[2,1,256,1536]{3,2,0,1:T(8,128)(2,1)S(1)}, bf16[2,1,256,1536]{3,2,0,1:T(8,128)(2,1)S(1)}, u32[]{:S(2)}, u32[]{:S(2)}) collective-permute-start(bf16[2,1,256,1536]{3,2,0,1:T(8,128)(2,1)S(1)} %bitcast.599), channel_id=1, source_target_pairs={{0,8},{4,12},{8,0},{12,4},{1,9},{5,13},{9,1},{13,5},{2,10},{6,14},... | collective-permute-start | bytes 4718600 | tf_op jit(solution)/shard_map/ppermute | solution.py:43
  1173.3 28.0 %copy-start.28 = (bf16[2,1,256,1536]{3,2,0,1:T(8,128)(2,1)}, bf16[2,1,256,1536]{3,2,0,1:T(8,128)(2,1)S(1)}, u32[]{:S(2)}) copy-start(bf16[2,1,256,1536]{3,2,0,1:T(8,128)(2,1)S(1)} %collective-permute-done.21) | copy-start | bytes 4718596
  1175.4 26.5 %collective-permute-start.22 = (bf16[2,2,256,1536]{3,2,0,1:T(8,128)(2,1)}, bf16[2,2,256,1536]{3,2,0,1:T(8,128)(2,1)}, u32[]{:S(2)}, u32[]{:S(2)}) collective-permute-start(bf16[2,2,256,1536]{3,2,0,1:T(8,128)(2,1)} %maximum_select_fusion.6), channel_id=1, source_target_pairs={{0,4},{4,0},{8,12},{12,8},{1,5},{5,1},{9,13},{13,9},{2,6},{6,2},{1... | collective-permute-start | bytes 9437192 | tf_op jit(solution)/shard_map/ppermute | solution.py:43
  1257.8 30.9 %copy-start.24 = (bf16[2048,3456]{1,0:T(8,128)(2,1)S(1)}, bf16[2048,3456]{1,0:T(8,128)(2,1)}, u32[]{:S(2)}) copy-start(bf16[2048,3456]{1,0:T(8,128)(2,1)} %get-tuple-element.348) | copy-start | bytes 42467332 | tf_op jit(solution)/shard_map/conditional
  1327.4 800.8 %all-reduce.22.cloned.1.call-start = ((), (), s32[]{:S(2)}) async-start(), calls=%async_computation | async-start | bytes 15728640 | tf_op jit(solution)/shard_map/psum | solution.py:446
  1344.7 8.4 collective-permute-start.23
  1353.1 13.9 copy-start.43
  1353.1 88.1 %copy-start.72 = (f32[1536]{0:T(1024)S(1)}, f32[1536]{0:T(1024)}, u32[]{:S(2)}) copy-start(f32[1536]{0:T(1024)} %copy-done.71) | copy-start | bytes 18436
  1367.0 72.5 %collective-permute-start.24 = (bf16[2,2,256,1536]{3,2,0,1:T(8,128)(2,1)}, bf16[2,2,256,1536]{3,2,0,1:T(8,128)(2,1)S(1)}, u32[]{:S(2)}, u32[]{:S(2)}) collective-permute-start(bf16[2,2,256,1536]{3,2,0,1:T(8,128)(2,1)} %get-tuple-element.765), channel_id=1, source_target_pairs={{0,8},{4,12},{8,0},{12,4},{1,9},{5,13},{9,1},{13,5},{2,10},{6,14},... | collective-permute-start | bytes 9437192 | tf_op jit(solution)/shard_map/ppermute | solution.py:43
  1452.2 15.8 copy-start.60
  1452.2 15.8 copy-start.79
  1460.1 7.9 collective-permute-start.25
  1538.4 20.7 collective-permute-start.26
  1556.7 12.4 collective-permute-start.28
  1559.1 24.1 %slice-start.4 = ((s8[6291456]{0:T(1024)(128)(4,1)}), s8[4194304]{0:T(1024)(128)(4,1)S(1)}, s32[]{:S(2)}) async-start(s8[6291456]{0:T(1024)(128)(4,1)} %bitcast.573), calls=%async_computation.6 | async-start | bytes 8388608
  1559.1 25.1 %slice-start = ((s8[6291456]{0:T(1024)(128)(4,1)}), s8[4194304]{0:T(1024)(128)(4,1)S(1)}, s32[]{:S(2)}) async-start(s8[6291456]{0:T(1024)(128)(4,1)} %bitcast.568), calls=%async_computation.2 | async-start | bytes 8388608
  1565.5 40.9 %collective-permute-start.27 = (bf16[2,1,256,1536]{3,2,0,1:T(8,128)(2,1)}, bf16[2,1,256,1536]{3,2,0,1:T(8,128)(2,1)}, u32[]{:S(2)}, u32[]{:S(2)}) collective-permute-start(bf16[2,1,256,1536]{3,2,0,1:T(8,128)(2,1)} %dynamic-slice_convert_fusion.1), channel_id=1, source_target_pairs={{0,8},{4,12},{8,0},{12,4},{1,9},{5,13},{9,1},{13,5},{2,10},{6,14},... | collective-permute-start | bytes 4718600 | tf_op jit(solution)/shard_map/ppermute | solution.py:43
  1569.1 14.4 slice-start.2
  1569.1 14.4 slice-start.6
  1569.1 14.0 slice-start.5
  1569.1 14.3 slice-start.3
  1569.2 14.3 slice-start.7
  1569.2 15.0 slice-start.1
  1581.4 74.1 %collective-permute-start.29 = (bf16[2,1,256,1536]{3,2,0,1:T(8,128)(2,1)}, bf16[2,1,256,1536]{3,2,0,1:T(8,128)(2,1)}, u32[]{:S(2)}, u32[]{:S(2)}) collective-permute-start(bf16[2,1,256,1536]{3,2,0,1:T(8,128)(2,1)} %dynamic-slice_convert_fusion), channel_id=1, source_target_pairs={{16,24},{20,28},{24,16},{28,20},{17,25},{21,29},{25,17},{29,21},{1... | collective-permute-start | bytes 4718600 | tf_op jit(solution)/shard_map/ppermute | solution.py:43
  1583.9 22.5 %copy-start.75 = (f32[1536]{0:T(1024)S(1)}, f32[1536]{0:T(1024)}, u32[]{:S(2)}) copy-start(f32[1536]{0:T(1024)} %copy-done.74) | copy-start | bytes 18436
  1865.1 13.0 copy-start.37
  (44 other events, 219.0 us)
Sparse Core Ops, SparseCore 0:
  1327.6 537.4 all-reduce.23
  1871.2 257.0 all-reduce.21

commit v2 on v1

--- a/solution.py
+++ b/solution.py
@@ -1,6 +1,10 @@
+import functools
+
 import jax
 import jax.numpy as jnp
 from jax import lax
+from jax.experimental import pallas as pl
+from jax.experimental.pallas import tpu as pltpu
 from jax.sharding import PartitionSpec as P
 
 EPSILON = 1e-05
@@ -8,6 +12,9 @@
 NEGATIVE = -1e30
 BF = jnp.bfloat16
 F32 = jnp.float32
+MESH = pl.DeviceIdType.MESH
+TILE = 64
+VMEM_BYTES = 60 * 1024 * 1024
 
 
 def mm(spec, left, right, kind=F32):
@@ -147,6 +154,460 @@
         one_block, (zeros_kv, zeros_kv), jnp.arange(length // block_len, dtype=jnp.int32)
     )
     return (regroup(stacked), carried[0], carried[1])
+
+
+class Peers:
+    def __init__(self):
+        self.section = lax.axis_index("section")
+        place = lax.axis_index("tensor")
+        core = place % 2
+        self.chip = place // 2
+        self.mate = {"tensor": place + 1 - 2 * core}
+        self.beside = {"tensor": place + 2 - 4 * self.chip}
+        self.across = {"section": 1 - self.section}
+        self.corner = {"section": 1 - self.section, "tensor": place + 2 - 4 * self.chip}
+
+
+def greet(signalled, count):
+    barrier = pltpu.get_barrier_semaphore()
+    for device in signalled:
+        pl.semaphore_signal(barrier, inc=1, device_id=device, device_id_type=MESH)
+    pl.semaphore_wait(barrier, count)
+
+
+def remote(source, target, send, receive, device):
+    return pltpu.make_async_remote_copy(
+        src_ref=source,
+        dst_ref=target,
+        send_sem=send,
+        recv_sem=receive,
+        device_id=device,
+        device_id_type=MESH,
+    )
+
+
+def loop(count, body):
+    lax.fori_loop(0, count, lambda i, unused: (body(i), 0)[1], 0)
+
+
+def tile_rows(index):
+    return pl.ds(pl.multiple_of(index * TILE, TILE), TILE)
+
+
+def home_tile(j, chip, per_chip):
+    each = per_chip // TILE
+    return ((j // each) * 2 + chip) * each + j % each
+
+
+def rms_tile(values):
+    return lax.rsqrt(jnp.mean(values * values, axis=-1, keepdims=True) + EPSILON)
+
+
+def norm_back_tile(values, gain, grad):
+    scale = rms_tile(values)
+    normed = values * scale
+    weighted = grad * gain
+    inner = jnp.mean(weighted * normed, axis=-1, keepdims=True)
+    return scale * (weighted - normed * inner), grad * normed
+
+
+def comm_call(kernel, name, number, inputs, outs, scratch, where):
+    return pl.pallas_call(
+        kernel,
+        name=name,
+        out_shape=outs,
+        in_specs=[pl.BlockSpec(memory_space=space) for space in where],
+        out_specs=tuple(pl.BlockSpec(memory_space=pltpu.VMEM) for unused in outs),
+        scratch_shapes=scratch,
+        compiler_params=pltpu.CompilerParams(
+            collective_id=number, has_side_effects=True, vmem_limit_bytes=VMEM_BYTES
+        ),
+    )(*inputs)
+
+
+def sum_tiles(active, backward, per_chip, *refs):
+    if backward:
+        sent, mine, hidden, grad, gain, out, low, low_mate, gain_out = refs[:9]
+        scratch = refs[9:]
+    else:
+        sent, mine, residual, gain, out, low, low_mate = refs[:7]
+        scratch = refs[7:]
+    from_mate, summed, from_chip, relayed = scratch[:4]
+    mate_s, mate_r, chip_s, chip_r, relay_s, relay_r, low_s, low_r = scratch[4:]
+    peers = Peers()
+    count = mine.shape[0] // TILE
+    pairs = count // 2
+
+    def mate_copy(i):
+        rows = tile_rows(i)
+        return remote(sent.at[rows], from_mate.at[rows], mate_s.at[i], mate_r.at[i], peers.mate)
+
+    def direct(i):
+        rows = tile_rows(i)
+        return remote(summed.at[rows], from_chip.at[rows], chip_s.at[i], chip_r.at[i], peers.beside)
+
+    def detour(p):
+        return remote(
+            summed.at[tile_rows(2 * p)],
+            relayed.at[tile_rows(p)],
+            chip_s.at[2 * p],
+            relay_r.at[p],
+            peers.corner,
+        )
+
+    def back(p):
+        return remote(
+            relayed.at[tile_rows(p)],
+            from_chip.at[tile_rows(2 * p)],
+            relay_s.at[p],
+            chip_r.at[2 * p],
+            peers.across,
+        )
+
+    def low_copy(i):
+        rows = tile_rows(i)
+        return remote(low.at[rows], low_mate.at[rows], low_s.at[i], low_r.at[i], peers.mate)
+
+    @pl.when(peers.section == active)
+    def work():
+        greet([peers.mate, peers.beside, peers.across], 3)
+        loop(count, lambda i: mate_copy(i).start())
+
+        def first(p):
+            for k in range(2):
+                i = 2 * p + k
+                rows = tile_rows(i)
+                mate_copy(i).wait_recv()
+                total = mine[rows, :] + from_mate[rows, :].astype(F32)
+                out[rows, :] = total
+                summed[rows, :] = total.astype(BF)
+                if k == 0:
+                    detour(p).start()
+                else:
+                    direct(i).start()
+
+        loop(pairs, first)
+        if backward:
+            gain_out[...] = jnp.zeros_like(gain_out)
+
+        def second(i):
+            rows = tile_rows(i)
+            direct(i).wait_recv()
+            total = out[rows, :] + from_chip[rows, :].astype(F32)
+            if backward:
+                change, terms = norm_back_tile(hidden[rows, :], gain[...], total)
+                result = grad[rows, :].astype(F32) + change
+                lower = result.astype(BF)
+                ours = ((i * TILE) // per_chip) % 2 == peers.chip
+                added = jnp.sum(terms, axis=0, keepdims=True)
+                gain_out[...] += jnp.where(ours, added, jnp.zeros_like(added))
+            else:
+                result = residual[rows, :].astype(F32) + total
+                lower = (result * rms_tile(result) * gain[...]).astype(BF)
+            out[rows, :] = result
+            low[rows, :] = lower
+            low_copy(i).start()
+
+        loop(count, second)
+
+        def finish(i):
+            mate_copy(i).wait_send()
+            direct(i).wait_send()
+            low_copy(i).wait()
+
+        loop(count, finish)
+
+    @pl.when(peers.section != active)
+    def relay():
+        greet([peers.corner], 1)
+
+        def step(p):
+            detour(p).wait_recv()
+            back(p).start()
+
+        loop(pairs, step)
+        loop(pairs, lambda p: back(p).wait_send())
+
+
+def sum_call(active, number, backward, per_chip, sent, mine, *rest):
+    size, width = mine.shape
+    count = size // TILE
+    full = jax.ShapeDtypeStruct((size, width), F32)
+    half = jax.ShapeDtypeStruct((size, width), BF)
+    outs = (full, half, half)
+    if backward:
+        outs += (jax.ShapeDtypeStruct((1, width), F32),)
+    scratch = [pltpu.VMEM((size, width), BF)] * 3 + [pltpu.VMEM((size // 2, width), BF)]
+    sizes = [count, count, count, count, count // 2, count // 2, count, count]
+    scratch += [pltpu.SemaphoreType.DMA((n,)) for n in sizes]
+    return comm_call(
+        functools.partial(sum_tiles, active, backward, per_chip),
+        "sum_back" if backward else "sum_norm",
+        number,
+        (sent, mine) + rest,
+        outs,
+        scratch,
+        [pl.ANY] + [pltpu.VMEM] * (1 + len(rest)),
+    )
+
+
+def spread_tiles(normed, peers, per_chip, gain, home, low, low_mate, sems, arrived, source):
+    chip_s, chip_r, low_s, low_r = sems
+    count = home.shape[0] // TILE
+    half = count // 2
+
+    def place(j, chip):
+        return home_tile(j, chip, per_chip)
+
+    def chip_copy(j):
+        rows = tile_rows(place(j, peers.chip))
+        return remote(source(j), home.at[rows], chip_s.at[j], chip_r.at[j], peers.beside)
+
+    def chip_wait(j):
+        rows = tile_rows(place(j, 1 - peers.chip))
+        remote(source(j), home.at[rows], chip_s.at[j], chip_r.at[j], peers.beside).wait_recv()
+
+    def low_copy(i, k):
+        rows = tile_rows(i)
+        return remote(low.at[rows], low_mate.at[rows], low_s.at[k], low_r.at[k], peers.mate)
+
+    def lower(i, values):
+        rows = tile_rows(i)
+        wide = values.astype(F32)
+        if normed == "all":
+            wide = wide * rms_tile(wide) * gain[...]
+        elif normed == "first":
+            scale = rms_tile(wide)
+            wide = wide * jnp.where(peers.section == 0, scale, jnp.ones_like(scale)) * gain[...]
+        low[rows, :] = wide.astype(BF)
+
+    def own(j):
+        arrived(j)
+        chip_copy(j).start()
+        i = place(j, peers.chip)
+        values = source(j)[...]
+        home[tile_rows(i), :] = values
+        lower(i, values)
+        low_copy(i, j).start()
+
+    loop(half, own)
+
+    def other(j):
+        chip_wait(j)
+        i = place(j, 1 - peers.chip)
+        lower(i, home[tile_rows(i), :])
+        low_copy(i, half + j).start()
+
+    loop(half, other)
+
+    def finish(j):
+        chip_copy(j).wait_send()
+        low_copy(place(j, peers.chip), j).wait_send()
+        low_copy(place(j, 1 - peers.chip), half + j).wait_send()
+        low_copy(place(j, peers.chip), j).wait_recv()
+        low_copy(place(j, 1 - peers.chip), half + j).wait_recv()
+
+    loop(half, finish)
+
+
+def start_tiles(per_chip, local, gain, home, low, low_mate, *sems):
+    peers = Peers()
+    greet([peers.mate, peers.beside], 2)
+    spread_tiles(
+        "first",
+        peers,
+        per_chip,
+        gain,
+        home,
+        low,
+        low_mate,
+        sems,
+        lambda j: None,
+        lambda j: local.at[tile_rows(j)],
+    )
+
+
+def start_call(number, per_chip, local, gain):
+    size, width = local.shape
+    half = size // TILE
+    out = jax.ShapeDtypeStruct((2 * size, width), BF)
+    return comm_call(
+        functools.partial(start_tiles, per_chip),
+        "start",
+        number,
+        (local, gain),
+        (out, out, out),
+        [pltpu.SemaphoreType.DMA((n,)) for n in (half, half, 2 * half, 2 * half)],
+        [pltpu.VMEM, pltpu.VMEM],
+    )
+
+
+def scatter_steps(peers, per_chip, sent, mine, from_mate, summed, kept, from_chip, sems, finished):
+    mate_s, mate_r, chip_s, chip_r = sems
+    count = mine.shape[0] // TILE
+    half = count // 2
+
+    def place(j, chip):
+        return home_tile(j, chip, per_chip)
+
+    def mate_copy(j, chip, k):
+        rows = tile_rows(place(j, chip))
+        return remote(sent.at[rows], from_mate.at[rows], mate_s.at[k], mate_r.at[k], peers.mate)
+
+    def chip_copy(j):
+        rows = tile_rows(j)
+        return remote(summed.at[rows], from_chip.at[rows], chip_s.at[j], chip_r.at[j], peers.beside)
+
+    loop(half, lambda j: mate_copy(j, 1 - peers.chip, j).start())
+    loop(half, lambda j: mate_copy(j, peers.chip, half + j).start())
+
+    def away(j):
+        mate_copy(j, 1 - peers.chip, j).wait_recv()
+        rows = tile_rows(place(j, 1 - peers.chip))
+        total = mine[rows, :] + from_mate[rows, :].astype(F32)
+        summed[tile_rows(j), :] = total.astype(BF)
+        chip_copy(j).start()
+
+    loop(half, away)
+
+    def keep(j):
+        mate_copy(j, peers.chip, half + j).wait_recv()
+        rows = tile_rows(place(j, peers.chip))
+        kept[tile_rows(j), :] = mine[rows, :] + from_mate[rows, :].astype(F32)
+
+    loop(half, keep)
+
+    def last(j):
+        chip_copy(j).wait_recv()
+        rows = tile_rows(j)
+        finished(j, kept[rows, :] + from_chip[rows, :].astype(F32))
+
+    loop(half, last)
+
+    def finish(j):
+        mate_copy(j, 1 - peers.chip, j).wait_send()
+        mate_copy(j, peers.chip, half + j).wait_send()
+        chip_copy(j).wait_send()
+
+    loop(half, finish)
+
+
+def end_tiles(per_chip, sent, mine, out, from_mate, summed, from_chip, *sems):
+    peers = Peers()
+    greet([peers.mate, peers.beside], 2)
+
+    def finished(j, total):
+        out[tile_rows(j), :] = total
+
+    scatter_steps(peers, per_chip, sent, mine, from_mate, summed, out, from_chip, sems, finished)
+
+
+def end_call(number, per_chip, sent, mine):
+    size, width = mine.shape
+    half = size // TILE // 2
+    return comm_call(
+        functools.partial(end_tiles, per_chip),
+        "end",
+        number,
+        (sent, mine),
+        (jax.ShapeDtypeStruct((size // 2, width), F32),),
+        [pltpu.VMEM((size, width), BF)]
+        + [pltpu.VMEM((size // 2, width), BF)] * 2
+        + [pltpu.SemaphoreType.DMA((n,)) for n in (2 * half, 2 * half, half, half)],
+        [pl.ANY, pltpu.VMEM],
+    )[0]
+
+
+def hop_tiles(source, backward, per_chip, *refs):
+    if backward:
+        sent, mine, values, grad, gain, next_gain, home, low, low_mate, result, gain_out = refs[:11]
+        scratch = refs[11:]
+    else:
+        sent, mine, values, next_gain, home, low, low_mate, result = refs[:8]
+        scratch = refs[8:]
+    from_mate, summed, kept, from_chip, crossing, landed = scratch[:6]
+    scatter_sems = scratch[6:10]
+    spread_sems = scratch[10:14]
+    cross_s, cross_r = scratch[14:]
+    peers = Peers()
+    half = result.shape[0] // TILE
+
+    def cross_copy(j):
+        rows = tile_rows(j)
+        return remote(
+            crossing.at[rows], landed.at[rows], cross_s.at[j], cross_r.at[j], peers.across
+        )
+
+    @pl.when(peers.section == source)
+    def give():
+        greet([peers.mate, peers.beside], 3)
+        if backward:
+            gain_out[...] = jnp.zeros_like(gain_out)
+
+        def finished(j, total):
+            rows = tile_rows(j)
+            own = tile_rows(home_tile(j, peers.chip, per_chip))
+            if backward:
+                change, terms = norm_back_tile(values[own, :].astype(F32), gain[...], total)
+                full = grad[own, :] + change
+                gain_out[...] += jnp.sum(terms, axis=0, keepdims=True)
+            else:
+                full = values[own, :] + total
+            result[rows, :] = full
+            crossing[rows, :] = full.astype(BF)
+            cross_copy(j).start()
+
+        scatter_steps(
+            peers,
+            per_chip,
+            sent,
+            mine,
+            from_mate,
+            summed,
+            kept,
+            from_chip,
+            scatter_sems,
+            finished,
+        )
+        loop(half, lambda j: cross_copy(j).wait_send())
+
+    @pl.when(peers.section != source)
+    def take():
+        greet([peers.mate, peers.beside, peers.across], 2)
+        spread_tiles(
+            None if backward else "all",
+            peers,
+            per_chip,
+            next_gain,
+            home,
+            low,
+            low_mate,
+            spread_sems,
+            lambda j: cross_copy(j).wait_recv(),
+            lambda j: landed.at[tile_rows(j)],
+        )
+
+
+def hop_call(source, number, backward, per_chip, sent, mine, *rest):
+    size, width = mine.shape
+    half = size // TILE // 2
+    out = jax.ShapeDtypeStruct((size, width), BF)
+    outs = (out, out, out, jax.ShapeDtypeStruct((size // 2, width), F32))
+    if backward:
+        outs += (jax.ShapeDtypeStruct((1, width), F32),)
+    scratch = [pltpu.VMEM((size, width), BF), pltpu.VMEM((size // 2, width), BF)]
+    scratch += [pltpu.VMEM((size // 2, width), F32)] + [pltpu.VMEM((size // 2, width), BF)] * 3
+    sizes = [2 * half, 2 * half, half, half, half, half, 2 * half, 2 * half, half, half]
+    scratch += [pltpu.SemaphoreType.DMA((n,)) for n in sizes]
+    return comm_call(
+        functools.partial(hop_tiles, source, backward, per_chip),
+        "hop_back" if backward else "hop",
+        number,
+        (sent, mine) + rest,
+        outs,
+        scratch,
+        [pl.ANY] + [pltpu.VMEM] * (1 + len(rest)),
+    )
 
 
 def on_device(
@@ -376,71 +837,151 @@
         grad_up = mm("td,tf->df", both, grad_gu, BF)
         return grad_up, grad_down
 
-    x_home = chip_gather(local, 0).astype(F32)
-    cot_home = chip_gather(local, 1)
-    cot_mate = mate(cot_home, 1)
-    cot_both = flat_tokens(cot_home, cot_mate)
-
-    z_home = norm(x_home, gains[0, 0])
-    mine, sent, project, mixed, full1 = when(0, conv_forward, z_home, mate(z_home, 0))
-    h1 = x_home + chip_sum(core_sum(mine, sent, 0), 0)
-    z_home = norm(h1, gains[0, 1])
-    both1 = flat_tokens(z_home, mate(z_home, 0))
+    fused = chips == 2 and seq_local % TILE == 0
+    home_shape = (rows, chips, seq_local, width)
+
+    def tokens(values):
+        return values.reshape(-1, width)
+
+    def homed(values):
+        return values.reshape(home_shape)
+
+    def row(gain):
+        return gain.reshape(1, width)
+
+    def spread(own, section, lower):
+        home_values = chip_gather(own, section)
+        low = lower(home_values)
+        return home_values, low, mate(low, section)
+
+    def begin(gain):
+        if fused:
+            gain = jnp.where(is_first, gain, jnp.ones_like(gain))
+            return map(homed, start_call(0, seq_local, tokens(local), row(gain)))
+        first = spread(local, 0, lambda v: norm(v.astype(F32), gain))
+        second = spread(local, 1, lambda v: v)
+        return [jnp.where(is_first, one, two) for one, two in zip(first, second)]
+
+    def sum_norm(section, number, mine, sent, residual, gain):
+        if fused:
+            outs = sum_call(
+                section, number, False, seq_local, tokens(sent), tokens(mine), tokens(residual), row(gain)
+            )
+            return map(homed, outs)
+        hidden_out = residual.astype(F32) + chip_sum(core_sum(mine, sent, section), section)
+        low = norm(hidden_out, gain)
+        return hidden_out, low, mate(low, section)
+
+    def sum_back(section, number, mine, sent, hidden_in, grad, gain):
+        if fused:
+            *outs, terms = sum_call(
+                section,
+                number,
+                True,
+                seq_local,
+                tokens(sent),
+                tokens(mine),
+                tokens(hidden_in),
+                tokens(grad),
+                row(gain),
+            )
+            return *map(homed, outs), terms[0]
+        dz = chip_sum(core_sum(mine, sent, section), section)
+        change, terms = norm_back(hidden_in, gain, dz)
+        grad_in = grad.astype(F32) + change
+        low = grad_in.astype(BF)
+        return grad_in, low, mate(low, section), jnp.sum(pick(terms, chip, 1), axis=(0, 1))
+
+    def hop(number, mine, sent, hidden_in, gain):
+        if fused:
+            *outs, result = hop_call(
+                0, number, False, seq_local, tokens(sent), tokens(mine), tokens(hidden_in), row(gain)
+            )
+            return map(homed, outs)
+        result = pick(hidden_in, chip, 1) + chip_scatter(core_sum(mine, sent, 0), 0)
+        crossing = lax.ppermute(result.astype(BF), "section", [(0, 1)])
+        return spread(crossing, 1, lambda v: norm(v.astype(F32), gain))
+
+    def hop_back(number, mine, sent, values, grad, gain):
+        if fused:
+            *outs, result, terms = hop_call(
+                1,
+                number,
+                True,
+                seq_local,
+                tokens(sent),
+                tokens(mine),
+                tokens(values),
+                tokens(grad),
+                row(gain),
+                row(gain),
+            )
+            return *map(homed, outs), terms[0]
+        dz = chip_scatter(core_sum(mine, sent, 1), 1)
+        change, terms = norm_back(pick(values, chip, 1).astype(F32), gain, dz)
+        result = pick(grad, chip, 1) + change
+        crossing = lax.ppermute(result.astype(BF), "section", [(1, 0)])
+        return *spread(crossing, 0, lambda v: v), jnp.sum(terms, axis=(0, 1))
+
+    def end(number, mine, sent):
+        if fused:
+            out = end_call(number, seq_local, tokens(sent), tokens(mine))
+            return out.reshape(rows, seq_local, width)
+        return jnp.where(
+            is_first,
+            chip_scatter(core_sum(mine, sent, 0), 0),
+            chip_scatter(core_sum(mine, sent, 1), 1),
+        )
+
+    start_home, start_low, start_mate = begin(gains[0, 0])
+    cot_both = flat_tokens(start_home, start_mate)
+    mine, sent, project, mixed, full1 = when(0, conv_forward, start_low, start_mate)
+    h1, z_home, z_mate = sum_norm(0, 1, mine, sent, start_home, gains[0, 1])
+    both1 = flat_tokens(z_home, z_mate)
     gu1 = gate_up(both1)
     mine, sent = ffn_out(activate(gu1))
-    x2_local = pick(h1, chip, 1) + chip_scatter(core_sum(mine, sent, 0), 0)
-
-    crossing = lax.ppermute(x2_local.astype(BF), "section", [(0, 1)])
-    x2_home = chip_gather(crossing, 1).astype(F32)
-    z_home = norm(x2_home, gains[1, 0])
-    mine, sent, *saved = when(1, attn_forward, z_home, mate(z_home, 1))
-    h3 = x2_home + chip_sum(core_sum(mine, sent, 1), 1)
-    z_home = norm(h3, gains[1, 1])
-    both2 = flat_tokens(z_home, mate(z_home, 1))
+
+    x2_home, z_home, z_mate = hop(2, mine, sent, h1, gains[1, 0])
+    mine, sent, *saved = when(1, attn_forward, z_home, z_mate)
+    h3, z_home, z_mate = sum_norm(1, 3, mine, sent, x2_home, gains[1, 1])
+    both2 = flat_tokens(z_home, z_mate)
     gu2 = gate_up(both2)
 
     grad_gu2, mine, sent = ffn_back(cot_both, gu2)
-    dz = chip_sum(core_sum(mine, sent, 1), 1)
-    grad_norm, gain_terms = norm_back(h3, gains[1, 1], dz)
-    gain_ffn2 = jnp.sum(pick(gain_terms, chip, 1), axis=(0, 1))
-    gh3 = cot_home.astype(F32) + grad_norm
-    gm_home = gh3.astype(BF)
-    mine, sent, attn_grads, head_grads = when(
-        1, attn_backward, gm_home, mate(gm_home, 1), *saved
-    )
-    dz = chip_scatter(core_sum(mine, sent, 1), 1)
-    grad_norm, gain_terms = norm_back(pick(x2_home, chip, 1), gains[1, 0], dz)
-    gain_mix2 = jnp.sum(gain_terms, axis=(0, 1))
-    gx2_local = pick(gh3, chip, 1) + grad_norm
-
-    crossing = lax.ppermute(gx2_local.astype(BF), "section", [(1, 0)])
-    g_home = chip_gather(crossing, 0)
-    g_both = flat_tokens(g_home, mate(g_home, 0))
-
+    gh3, gm_home, gm_mate, gain_ffn2 = sum_back(1, 4, mine, sent, h3, start_home, gains[1, 1])
+    mine, sent, attn_grads, head_grads = when(1, attn_backward, gm_home, gm_mate, *saved)
+    g_home, unused, g_mate, gain_mix2 = hop_back(5, mine, sent, x2_home, gh3, gains[1, 0])
+
+    g_both = flat_tokens(g_home, g_mate)
     grad_gu1, mine, sent = ffn_back(g_both, gu1)
     late = (both1, gu1, g_both, grad_gu1, both2, gu2, cot_both, grad_gu2)
-    grad_up, grad_down, mine_y, sent_y = lax.cond(
-        is_first,
-        lambda *args: ffn_weights(*args[:4])
-        + (jnp.zeros((rows, chips, seq_local, width), F32), jnp.zeros((rows, chips, seq_local, width), BF)),
-        lambda *args: ffn_weights(*args[4:]) + ffn_out(activate(args[5])),
-        *late,
+    grad_up, grad_down = lax.cond(
+        is_first, lambda *args: ffn_weights(*args[:4]), lambda *args: ffn_weights(*args[4:]), *late
     )
     full_gu = lax.psum(grad_up, "dp")
     full_down = lax.psum(grad_down, "dp")
-    y_local = pick(h3, chip, 1) + chip_scatter(core_sum(mine_y, sent_y, 1), 1)
-    dz = chip_sum(core_sum(mine, sent, 0), 0)
-    grad_norm, gain_terms = norm_back(h1, gains[0, 1], dz)
-    gain_ffn1 = jnp.sum(pick(gain_terms, chip, 1), axis=(0, 1))
-    gh1 = g_home.astype(F32) + grad_norm
-    gm_home = gh1.astype(BF)
-    mine, sent, conv_grads = when(
-        0, conv_backward, gm_home, mate(gm_home, 0), project, mixed, full1
-    )
-    dz = chip_scatter(core_sum(mine, sent, 0), 0)
-    grad_norm, gain_terms = norm_back(pick(x_home, chip, 1), gains[0, 0], dz)
-    gain_mix1 = jnp.sum(gain_terms, axis=(0, 1))
-    gx_local = pick(gh1, chip, 1) + grad_norm
+    gh1, gm_home, gm_mate, gain_ffn1 = sum_back(0, 6, mine, sent, h1, g_home, gains[0, 1])
+
+    def second_out(*args):
+        shapes = jax.eval_shape(conv_backward, *args[:-1])
+        zeros = jax.tree.map(lambda one: jnp.zeros(one.shape, one.dtype), shapes)
+        return ffn_out(activate(args[-1])) + zeros[2:]
+
+    mine, sent, conv_grads = lax.cond(
+        is_first,
+        lambda *args: conv_backward(*args[:-1]),
+        second_out,
+        gm_home,
+        gm_mate,
+        project,
+        mixed,
+        full1,
+        gu2,
+    )
+    total = end(7, mine, sent)
+    change, terms = norm_back(local.astype(F32), gains[0, 0], total)
+    gain_mix1 = jnp.sum(terms, axis=(0, 1))
+    boundary_out = jnp.where(is_first, pick(gh1, chip, 1) + change, pick(h3, chip, 1) + total)[None]
 
     mixer_sums = jax.tree.map(
         lambda v: v.astype(F32), lax.psum(conv_grads + attn_grads, ("section", "dp"))
@@ -450,7 +991,6 @@
     second_gains = jnp.stack([jnp.stack([zero, zero]), jnp.stack([gain_mix2, gain_ffn2])])
     grad_gains = jnp.where(is_first, first_gains, second_gains)
     grad_gains, grad_heads = lax.psum((grad_gains, head_grads), ("section", "tensor", "dp"))
-    boundary_out = jnp.where(is_first, gx_local, y_local)[None]
     return (boundary_out, grad_gains, grad_heads) + mixer_sums + (
         full_gu.astype(F32).reshape(ffn_gate_up.shape),
         full_down.astype(F32)[None],

time: 2160 us -> 2020 us (0.935)
  Pallas kernels: 0 us -> 810 us
  waiting for transfers between devices: 1330 us -> 552 us
  other arithmetic: 223 us -> 117 us
  starting transfers between devices: 65.9 us -> 0.08 us
    ppermute x30 -> x0, waiting for transfers between devices: 886 us -> none  [the longest x1 586 us: on_device(): crossing = lax.ppermute(gx2_local.astype(BF), 'section', [(1, 0)])]
    pallas_call x0 -> x8, Pallas kernels: none -> 810 us  [comm_call(): pl.pallas_call(kernel, name=name, out_shape=outs, in_specs=[pl.BlockSpec(...]
    psum x1, waiting for transfers between devices: 200 us -> 526 us  [on_device(): full_gu = lax.psum(grad_up, 'dp')]
    psum x1, waiting for transfers between devices: 245 us -> 25.9 us  [on_device(): lax.psum(conv_grads + attn_grads, ('section', 'dp'))]
    ppermute x30 -> x0, starting transfers between devices: 65.8 us -> none  [the longest x28 63.1 us: permute(): return lax.ppermute(values, ('section', axis), pairs)]
    convert_element_type x12 -> x0, other arithmetic: 45 us -> none  [the longest x4 10.8 us: norm(): return (values * inverse_rms(values) * gain).astype(BF)]
    reduce_sum x6 -> x1, other arithmetic: 29.2 us -> 3.38 us  [on_device(): gain_mix1 = jnp.sum(terms, axis=(0, 1))]
    select_n x1 -> x2, local copies, waits for them, and re-layouts: 3.39 us -> 27.3 us  [weave(): jnp.where(core == 0, jnp.stack([mine, other], axis=2), jnp.stack([other,...]
  transfers between devices with their start and end apart: 32 -> 2, of which waited for: 14 -> 2; matrix products, arithmetic and copies ran while one was open for 11% -> 7% of each run, Pallas kernels for 0% -> 2%
where the time goes in v2:
time: 2020 us; the launch traced here: 2000 us
  Pallas kernels  810 us (40%)
  waiting for transfers between devices  552 us (27%)
  matrix products  304 us (15%)
  other arithmetic  117 us (6%)
  local copies, waits for them, and re-layouts  117 us (6%)
  blocking collectives  62.6 us (3%)
  loops' own time  28.2 us (1%)
    pallas_call x8, Pallas kernels, comm_call(): pl.pallas_call(kernel, name=name, out_shape=outs, in_specs=[pl.BlockSpec(...  810 us
    psum x1, waiting for transfers between devices, on_device(): full_gu = lax.psum(grad_up, 'dp')  526 us
    dot_general x20, matrix products, mm(): jnp.einsum(spec, left, right, preferred_element_type=F32).astype(kind)  304 us
    psum x1, blocking collectives, on_device(): lax.psum((grad_gains, head_grads), ('section', 'tensor', 'dp'))  42.5 us
  transfers between devices with their start and end apart: 2, of which 2 were waited for; matrix products, arithmetic and copies ran while one was open for 7% of the time, Pallas kernels for 2%

profile of v2, /device:TPU:0, one launch (start us, length us, event | category | flops | bytes accessed | tf_op | source)
XLA Modules:
  0.0 2004.3 jit_solution(11665245362223893271)
XLA Ops:
  9.9 43.8 %start.1 = (bf16[1024,1536]{1,0:T(8,128)(2,1)}, bf16[1024,1536]{1,0:T(8,128)(2,1)}, bf16[1024,1536]{1,0:T(8,128)(2,1)S(1)}) custom-call(bf16[512,1536]{1,0:T(8,128)(2,1)} %bitcast.504, f32[1,1536]{1,0:T(1,128)} %get-tuple-element.834.gain), custom_call_target="tpu_custom_call" | custom-call | tf_op jit(solution)/shard_map/start/pallas_call | solution.py:215
  55.4 32.3 %conditional.11 = (bf16[2,1024,3,384]{3,1,2,0:T(8,128)(2,1)}, bf16[2,1024,384]{2,1,0:T(8,128)(2,1)}, bf16[2,1024,1536]{2,1,0:T(8,128)(2,1)}, f32[1024,1536]{1,0:T(8,128)}, bf16[1024,1536]{1,0:T(8,128)(2,1)}) conditional(s32[]{:T(128)} %convert_element_type.255, () %tuple.85, (s32[]{:T(128)}, bf16[1024,1536]{1,0:T(8,128)(2,1)}, ...), branch_computations={%region_0.1_spmd, %region_1.2_spmd} | conditional | flops 9684918272 | bytes 87774920 | solution.py:696
  55.4 7.0 maximum_select_fusion.2
  62.4 11.9 fusion.226
  77.4 4.6 convolution_convert_fusion.3
  83.2 4.5 fusion.230
  87.7 55.9 %sum_norm.2 = (f32[1024,1536]{1,0:T(8,128)}, bf16[1024,1536]{1,0:T(8,128)(2,1)}, bf16[1024,1536]{1,0:T(8,128)(2,1)}) custom-call(bf16[1024,1536]{1,0:T(8,128)(2,1)} %get-tuple-element.424.refs_0_, f32[1024,1536]{1,0:T(8,128)} %get-tuple-element.425.refs_1_, bf16[1024,1536]{1,0:T(8,128)(2,1)} %get-tuple-element.421.refs_2_.refs_3_, ...), custom_call_target="tpu_custom_call" | custom-call | tf_op jit(solution)/shard_map/sum_norm/pallas_call | solution.py:215
  143.5 3.6 pad_maximum_fusion.6
  147.1 26.6 %convolution_convert_fusion.5 = bf16[2048,3456]{0,1:T(8,128)(2,1)S(1)} fusion(bf16[2048,1536]{1,0:T(8,128)(2,1)S(1)} %bitcast.519, bf16[1536,3456]{0,1:T(8,128)(2,1)} %bitcast.568), kind=kOutput, calls=%fused_computation.306 | convolution fusion | flops 21750349824 | bytes 31064064 | tf_op jit(solution)/shard_map/td,df->tf/dot_general | solution.py:21
  173.8 5.0 fusion.162
  178.8 7.8 fusion.195.refs_1_
  186.6 7.3 fusion.201.refs_0_
  193.9 53.0 %hop.1 = (bf16[1024,1536]{1,0:T(8,128)(2,1)}, bf16[1024,1536]{1,0:T(8,128)(2,1)}, bf16[1024,1536]{1,0:T(8,128)(2,1)}, f32[512,1536]{1,0:T(8,128)}) custom-call(bf16[1024,1536]{1,0:T(8,128)(2,1)} %fusion.201.refs_0_, f32[1024,1536]{1,0:T(8,128)} %fusion.195.refs_1_, f32[1024,1536]{1,0:T(8,128)} %get-tuple-element.428.refs_2_, ...), custom_call_target="tpu_custom_call" | custom-call | tf_op jit(solution)/shard_map/hop/pallas_call | solution.py:215
  247.0 29.3 %conditional.12 = (f32[2,1024,6,64]{1,3,2,0:T(8,128)S(1)}, f32[2,1024,2,64]{1,3,2,0:T(8,128)}, bf16[2,2,3,1024,64]{3,4,2,1,0:T(8,128)(2,1)}, bf16[2,2,1024,64]{2...) conditional(s32[]{:T(128)} %convert_element_type.253, () %tuple.84, ...), branch_computations={%region_2.3_spmd, %region_3.13_spmd} | conditional | flops 7317241344 | bytes 174266000 | solution.py:696
  261.0 3.0 broadcast.361
  264.0 3.5 reshape.382
  276.3 161.8 %sum_norm.3 = (f32[1024,1536]{1,0:T(8,128)}, bf16[1024,1536]{1,0:T(8,128)(2,1)}, bf16[1024,1536]{1,0:T(8,128)(2,1)}) custom-call(bf16[1024,1536]{1,0:T(8,128)(2,1)} %get-tuple-element.431.refs_0_, f32[1024,1536]{1,0:T(8,128)} %get-tuple-element.432.refs_1_, bf16[1024,1536]{1,0:T(8,128)(2,1)} %get-tuple-element.433.refs_2_, ...), custom_call_target="tpu_custom_call" | custom-call | tf_op jit(solution)/shard_map/sum_norm/pallas_call | solution.py:215
  438.1 3.4 pad_maximum_fusion.7
  441.5 28.4 %convolution_convert_fusion.4 = bf16[2048,3456]{0,1:T(8,128)(2,1)} fusion(bf16[2048,1536]{1,0:T(8,128)(2,1)S(1)} %bitcast.521, bf16[1536,3456]{0,1:T(8,128)(2,1)} %bitcast.569), kind=kOutput, calls=%fused_computation.305 | convolution fusion | flops 21750349824 | bytes 31064064 | tf_op jit(solution)/shard_map/td,df->tf/dot_general | solution.py:21
  470.0 3.2 pad_maximum_fusion.5
  473.1 26.2 %fusion.173 = (bf16[2048,1728]{0,1:T(8,128)(2,1)}, bf16[2048,1728]{0,1:T(8,128)(2,1)}) fusion(bf16[2048,3456]{0,1:T(8,128)(2,1)} %convolution_convert_fusion.4, bf16[2048,1536]{1,0:T(8,128)(2,1)} %bitcast.523, bf16[1,1536,1728]{1,2,0:T(8,128)(2,1)} %param.41), kind=kOutput, calls=%fused_computation.318 | convolution fusion | flops 10924720128 | bytes 39911424 | tf_op jit(solution)/shard_map/td,df->tf/dot_general | solution.py:21
  499.4 18.9 fusion.191.refs_1_
  518.3 16.2 fusion.204.refs_0_
  534.5 56.6 %sum_back.2 = (f32[1024,1536]{1,0:T(8,128)}, bf16[1024,1536]{1,0:T(8,128)(2,1)S(1)}, bf16[1024,1536]{1,0:T(8,128)(2,1)}, f32[1,1536]{1,0:T(1,128)}) custom-call(bf16[1024,1536]{1,0:T(8,128)(2,1)} %fusion.204.refs_0_, f32[1024,1536]{1,0:T(8,128)} %fusion.191.refs_1_, f32[1024,1536]{1,0:T(8,128)} %get-tuple-element.436.refs_2_, ...), custom_call_target="tpu_custom_call" | custom-call | tf_op jit(solution)/shard_map/sum_back/pallas_call | solution.py:215
  591.1 16.4 conditional.13
  591.1 3.5 reshape.387
  607.5 338.1 %hop_back.1 = (bf16[1024,1536]{1,0:T(8,128)(2,1)}, bf16[1024,1536]{1,0:T(8,128)(2,1)}, bf16[1024,1536]{1,0:T(8,128)(2,1)}, f32[512,1536]{1,0:T(8,128)}, f32[1,1536]{1,0:T(1,128)}) custom-call(bf16[1024,1536]{1,0:T(8,128)(2,1)} %get-tuple-element.447.refs_0_, f32[1024,1536]{1,0:T(8,128)} %get-tuple-element.448.refs_1_, ...), custom_call_target="tpu_custom_call" | custom-call | tf_op jit(solution)/shard_map/hop_back/pallas_call | solution.py:215
  945.6 3.4 pad_maximum_fusion.8
  949.1 25.3 %fusion.180 = (bf16[2048,1728]{0,1:T(8,128)(2,1)}, bf16[2048,1728]{0,1:T(8,128)(2,1)}) fusion(bf16[2048,3456]{0,1:T(8,128)(2,1)} %copy-done.6, bf16[2048,1536]{1,0:T(8,128)(2,1)S(1)} %bitcast.527, bf16[1,1536,1728]{1,2,0:T(8,128)(2,1)} %param.41), kind=kOutput, calls=%fused_computation.325 | convolution fusion | flops 10924720128 | bytes 39911424 | tf_op jit(solution)/shard_map/td,df->tf/dot_general | solution.py:21
  974.4 18.8 fusion.185.refs_1_
  993.2 16.4 fusion.207.refs_0_
  1009.6 7.9 copy.182
  1017.5 57.5 %sum_back.3 = (f32[1024,1536]{1,0:T(8,128)}, bf16[1024,1536]{1,0:T(8,128)(2,1)}, bf16[1024,1536]{1,0:T(8,128)(2,1)}, f32[1,1536]{1,0:T(1,128)}) custom-call(bf16[1024,1536]{1,0:T(8,128)(2,1)} %fusion.207.refs_0_, f32[1024,1536]{1,0:T(8,128)} %fusion.185.refs_1_, f32[1024,1536]{1,0:T(8,128)} %get-tuple-element.428.refs_2_, ...), custom_call_target="tpu_custom_call" | custom-call | tf_op jit(solution)/shard_map/sum_back/pallas_call | solution.py:215
  1075.0 92.6 %conditional.14 = (bf16[1536,3,384]{0,2,1:T(8,128)(2,1)S(1)}, bf16[3,384]{1,0:T(4,128)(2,1)}, bf16[384,1536]{0,1:T(8,128)(2,1)}, f32[1024,1536]{1,0:T(8,128)}, bf16[1024,1536]{1,0:T(8,128)(2,1)}) conditional(s32[]{:T(128)} %convert_element_type.255, (bf16[2048,3456]{0,1:T(8,128)(2,1)}, bf16[1536,1728]{1,0:T(8,128)(2,1)}) %tuple.252, ...), branch_computations={%region_28.29_spmd, %region_29.33_spmd} | conditional | flops 19374551040 | bytes 250549984 | solution.py:970
  1075.5 8.4 maximum_select_fusion.3
  1083.8 16.3 copy.170
  1100.2 11.0 select_n.133
  1111.1 3.0 copy_convert_fusion
  1115.4 10.0 multiply_reduce_fusion.11
  1125.4 4.9 multiply_convert_fusion.3
  1135.3 3.1 constant_dynamic-slice_fusion.9
  1138.7 6.2 convolution_bitcast_fusion.5
  1145.0 5.6 bitcast_convert_fusion.1
  1151.2 10.3 fusion.144
  1161.6 5.9 fusion.156
  1167.7 3.6 copy.192
  1178.4 3.0 copy.195
  1181.6 12.4 pad_maximum_fusion.4
  1193.9 12.3 pad_maximum_fusion.3
  1206.3 76.3 %conditional.15 = (bf16[1536,3456]{1,0:T(8,128)(2,1)}, bf16[1536,1728]{0,1:T(8,128)(2,1)}) conditional(s32[]{:T(128)} %convert_element_type.255, (bf16[2048,1536]{1,0:T(8,128)(2,1)}, bf16[2048,3456]{0,1:T(8,128)(2,1)}, bf16[2048,3456]{0,1:T(8,128)(2,1)}, bf16[2048,1536]{1,0:T(8,128)(2,1)}) %tuple.250, (bf16[2048,1536]{1,0:T(8,128)(2,1)}, ...), branch_computations={%region_43.44_spmd, %region_44.45_spmd} | conditional | flops 32643219456 | bytes 85655568
  1211.8 18.0 copy.200
  1229.8 21.2 %convolution_bitcast_fusion.1 = bf16[1536,1728]{0,1:T(8,128)(2,1)} fusion(bf16[2048,1536]{1,0:T(8,128)(2,1)} %get-tuple-element.358, bf16[2048,3456]{1,0:T(8,128)(2,1)} %copy.200), kind=kOutput, calls=%fused_computation.83 | convolution fusion | flops 10899947520 | bytes 26279936 | tf_op jit(solution)/shard_map/cond/branch_1_fun/td,tf->df/dot_general | solution.py:21
  1251.1 31.3 %fusion.228 = bf16[1536,3456]{1,0:T(8,128)(2,1)} fusion(bf16[2048,1536]{1,0:T(8,128)(2,1)} %get-tuple-element.355, bf16[2048,3456]{0,1:T(8,128)(2,1)} %get-tuple-element.681), kind=kOutput, calls=%fused_computation.382 | convolution fusion | flops 21743271936 | bytes 31064064 | tf_op jit(solution)/shard_map/cond/branch_1_fun/td,tf->df/dot_general | solution.py:21
  1282.6 14.4 copy.201
  1298.9 43.5 %end.1 = f32[512,1536]{1,0:T(8,128)} custom-call(bf16[1024,1536]{1,0:T(8,128)(2,1)} %get-tuple-element.458.sent, f32[1024,1536]{1,0:T(8,128)} %get-tuple-element.459.mine), custom_call_target="tpu_custom_call" | custom-call | tf_op jit(solution)/shard_map/end/pallas_call | solution.py:215
  1342.4 3.4 multiply_reduce_fusion.12
  1345.8 20.0 psum.73
  1366.5 42.5 %all-reduce.16 = (f32[2,2,1536]{2,1,0:T(2,128)}, f32[2,64]{1,0:T(2,128)}) all-reduce(f32[2,2,1536]{2,1,0:T(2,128)S(1)} %pad_select_fusion, f32[2,64]{1,0:T(2,128)} %get-tuple-element.463), channel_id=1, replica_groups=mesh['section'=2,'tensor'=4,'dp'=4] {'section','tensor','dp'}, use_global_device_ids=true, to_apply=%region_35.36 | all-reduce | flops 6272 | bytes 50176 | tf_op jit(solution)/shard_map/psum | solution.py:993
  1409.1 6.1 fusion.217
  1415.2 25.9 %all-reduce.22.cloned.1.call-done = (bf16[1536,3,384]{2,0,1:T(8,128)(2,1)}, bf16[384,1536]{1,0:T(8,128)(2,1)}, bf16[1536,384]{1,0:T(8,128)(2,1)}, bf16[1536,2,128]{2,1,0:T(2,128)(2,1)}, bf16[384,1536]{1,0:T(8,128)(2,1)}) async-done(((bf16[1536,3,384]{2,0,1:T(8,128)(2,1)}, bf16[384,1536]{1,0:T(8,128)(2,1)}, bf16[1536,384]{1,0:T(8,128)(2,1)}, bf16[1536,2,128]{2,1,0:T(2,128)(2,1)}, ...) | async-done | bytes 7864336 | tf_op jit(solution)/shard_map/psum | solution.py:987
  1441.1 5.6 convert_element_type.270
  1453.1 525.6 %all-reduce.24.cloned.1.call-done = (bf16[1,1536,2,1728]{1,3,2,0:T(8,128)(2,1)}, bf16[1,1536,1728]{1,2,0:T(8,128)(2,1)}) async-done(((bf16[1,1536,2,1728]{1,3,2,0:T(8,128)(2,1)}, bf16[1,1536,1728]{1,2,0:T(8,128)(2,1)}), (bf16[1,1536,2,1728]{1,3,2,0:T(8,128)(2,1)}, bf16[1,1536,1728]{1,2,0:T(8,128)(2,1)})) %all-reduce.24.cloned.1.call-update) | async-done | bytes 15925264 | tf_op jit(solution)/shard_map/psum | solution.py:961
  1978.7 13.0 reshape.413
  1991.7 5.6 broadcast_in_dim.81
  (141 shorter events, 45.9 us)
Async XLA Ops:
  7.2 1433.9 %all-reduce.22.cloned.1.call-start = ((), (), s32[]{:S(2)}) async-start(), calls=%async_computation | async-start | bytes 15728640 | tf_op jit(solution)/shard_map/psum | solution.py:987
  9.9 43.8 %copy-start.60 = (f32[3,384]{1,0:T(4,128)}, f32[3,384]{1,0:T(4,128)S(1)}, u32[]{:S(2)}) copy-start(f32[3,384]{1,0:T(4,128)S(1)} %convert_element_type.256) | copy-start | bytes 13828
  53.7 1.7 copy-start.10
  55.4 7.0 copy-start.67
  74.3 0.7 copy-start.51
  74.6 2.8 copy-start.41
  143.5 35.3 %slice-start.4 = ((s8[5308416]{0:T(1024)(128)(4,1)}), s8[4194304]{0:T(1024)(128)(4,1)S(1)}, s32[]{:S(2)}) async-start(s8[5308416]{0:T(1024)(128)(4,1)} %bitcast.536), calls=%async_computation.6 | async-start | bytes 8388608
  147.1 26.6 %copy-start.23 = (bf16[2,2,2,256,1536]{4,3,2,1,0:T(8,128)(2,1)}, bf16[2,2,2,256,1536]{4,3,2,1,0:T(8,128)(2,1)S(1)}, u32[]{:S(2)}) copy-start(bf16[2,2,2,256,1536]{4,3,2,1,0:T(8,128)(2,1)S(1)} %pad_maximum_fusion.6) | copy-start | bytes 18874372
  147.1 31.7 %slice-start.5 = ((s8[5308416]{0:T(1024)(128)(4,1)}), s8[1114112]{0:T(1024)(128)(4,1)S(1)}, s32[]{:S(2)}) async-start(s8[5308416]{0:T(1024)(128)(4,1)} %bitcast.536), calls=%async_computation.7 | async-start | bytes 2228224
  173.7 5.0 copy-start.6
  186.6 7.3 copy-start.69
  193.9 53.0 %copy-start.65 = (f32[2,64]{1,0:T(2,128)}, f32[2,64]{1,0:T(2,128)S(1)}, u32[]{:S(2)}) copy-start(f32[2,64]{1,0:T(2,128)S(1)} %convert_element_type.262) | copy-start | bytes 1540
  193.9 53.0 %copy-start.49 = (s32[2,1024]{1,0:T(2,128)S(1)}, s32[2,1024]{1,0:T(2,128)}, u32[]{:S(2)}) copy-start(s32[2,1024]{1,0:T(2,128)} %param.31) | copy-start | bytes 24580
  276.3 161.8 %copy-start.4 = (f32[2,1024,6,64]{1,3,2,0:T(8,128)}, f32[2,1024,6,64]{1,3,2,0:T(8,128)S(1)}, u32[]{:S(2)}) copy-start(f32[2,1024,6,64]{1,3,2,0:T(8,128)S(1)} %get-tuple-element.443) | copy-start | bytes 9437188
  441.5 28.5 %copy-start.24 = (bf16[2,2,2,256,1536]{4,3,2,1,0:T(8,128)(2,1)}, bf16[2,2,2,256,1536]{4,3,2,1,0:T(8,128)(2,1)S(1)}, u32[]{:S(2)}) copy-start(bf16[2,2,2,256,1536]{4,3,2,1,0:T(8,128)(2,1)S(1)} %pad_maximum_fusion.7) | copy-start | bytes 18874372
  441.5 28.5 %copy-start.7 = (bf16[1024,1536]{1,0:T(8,128)(2,1)S(1)}, bf16[1024,1536]{1,0:T(8,128)(2,1)}, u32[]{:S(2)}) copy-start(bf16[1024,1536]{1,0:T(8,128)(2,1)} %get-tuple-element.421.refs_2_.refs_3_) | copy-start | bytes 9437188
  441.5 28.4 %copy-start.11 = (bf16[1024,1536]{1,0:T(8,128)(2,1)S(1)}, bf16[1024,1536]{1,0:T(8,128)(2,1)}, u32[]{:S(2)}) copy-start(bf16[1024,1536]{1,0:T(8,128)(2,1)} %copy-done.10) | copy-start | bytes 9437188
  499.4 18.9 copy-start.14
  499.4 18.9 copy-start.15
  949.1 25.3 %copy-start.25 = (bf16[2,2,2,256,1536]{4,3,2,1,0:T(8,128)(2,1)}, bf16[2,2,2,256,1536]{4,3,2,1,0:T(8,128)(2,1)S(1)}, u32[]{:S(2)}) copy-start(bf16[2,2,2,256,1536]{4,3,2,1,0:T(8,128)(2,1)S(1)} %pad_maximum_fusion.8) | copy-start | bytes 18874372
  974.4 18.8 copy-start.16
  974.4 18.8 copy-start.17
  1017.5 57.5 %copy-start.50 = (s32[2,1024]{1,0:T(2,128)S(1)}, s32[2,1024]{1,0:T(2,128)}, u32[]{:S(2)}) copy-start(s32[2,1024]{1,0:T(2,128)} %param.31) | copy-start | bytes 24580
  1017.5 57.5 %copy-start.61 = (f32[3,384]{1,0:T(4,128)S(1)}, f32[3,384]{1,0:T(4,128)}, u32[]{:S(2)}) copy-start(f32[3,384]{1,0:T(4,128)} %copy-done.60) | copy-start | bytes 13828
  1114.1 1.3 copy-start.42
  1130.3 5.0 copy-start.21
  1130.3 2.5 copy-start.38
  1130.9 7.5 copy-start.26
  1135.3 3.4 copy-start.68
  1145.0 6.3 copy-start.22
  1145.0 6.3 copy-start.27
  1145.0 6.3 copy-start.39
  1145.0 16.6 slice-start.2
  1151.2 10.3 slice-start.3
  1181.5 797.1 %all-reduce.24.cloned.1.call-start = ((), (), s32[]{:S(2)}) async-start(), calls=%async_computation.1 | async-start | bytes 31850496 | tf_op jit(solution)/shard_map/psum | solution.py:961
  1297.0 1.4 copy-start.9
  1298.8 43.6 %copy-start.59 = (f32[1536]{0:T(1024)S(1)}, f32[1536]{0:T(1024)}, u32[]{:S(2)}) copy-start(f32[1536]{0:T(1024)} %get-tuple-element.830) | copy-start | bytes 18436
  1298.8 67.6 %copy-start.62 = (f32[1,1536]{1,0:T(1,128)S(1)}, f32[1,1536]{1,0:T(1,128)}, u32[]{:S(2)}) copy-start(f32[1,1536]{1,0:T(1,128)} %get-tuple-element.462) | copy-start | bytes 18436
  1298.8 67.6 %copy-start.63 = (f32[1,1536]{1,0:T(1,128)S(1)}, f32[1,1536]{1,0:T(1,128)}, u32[]{:S(2)}) copy-start(f32[1,1536]{1,0:T(1,128)} %get-tuple-element.461) | copy-start | bytes 18436
  1298.9 67.6 %copy-start.64 = (f32[1,1536]{1,0:T(1,128)S(1)}, f32[1,1536]{1,0:T(1,128)}, u32[]{:S(2)}) copy-start(f32[1,1536]{1,0:T(1,128)} %get-tuple-element.460) | copy-start | bytes 18436
  1342.4 66.7 %copy-start.8 = (f32[512,1536]{1,0:T(8,128)S(1)}, f32[512,1536]{1,0:T(8,128)}, u32[]{:S(2)}) copy-start(f32[512,1536]{1,0:T(8,128)} %end.1) | copy-start | bytes 9437188
  1441.1 5.6 copy-start.45
  1441.1 7.3 copy-start.44
  1441.1 8.8 copy-start.43
  1446.7 5.0 copy-start.54
  1978.6 13.0 copy-start.30
Sparse Core Ops, SparseCore 0:
  1181.6 259.4 all-reduce.21
  1444.3 534.2 all-reduce.23

commit v3 on v2

v3 whole, which is shorter than its diff:
```python
import functools

import jax
import jax.numpy as jnp
from jax import lax
from jax.experimental import pallas as pl
from jax.experimental.pallas import tpu as pltpu
from jax.sharding import PartitionSpec as P

EPSILON = 1e-05
THETA = 1000000.0
NEGATIVE = -1e30
BF = jnp.bfloat16
F32 = jnp.float32
MESH = pl.DeviceIdType.MESH
TILE = 64
VMEM_BYTES = 60 * 1024 * 1024


def mm(spec, left, right, kind=F32):
    return jnp.einsum(spec, left, right, preferred_element_type=F32).astype(kind)


def inverse_rms(values):
    return lax.rsqrt(jnp.mean(values * values, axis=-1, keepdims=True) + EPSILON)


def norm(values, gain):
    return (values * inverse_rms(values) * gain).astype(BF)


def norm_back(values, gain, grad):
    scale = inverse_rms(values)
    normed = values * scale
    weighted = grad * gain
    grad_in = scale * (weighted - normed * jnp.mean(weighted * normed, axis=-1, keepdims=True))
    return grad_in, grad * normed


def section_pairs(section, size, function):
    return [
        (section * size + i, section * size + function(i))
        for i in range(size)
        if 0 <= function(i) < size
    ]


def permute(values, section, axis, function):
    pairs = section_pairs(section, lax.axis_size(axis), function)
    return lax.ppermute(values, ("section", axis), pairs)


def pick(values, index, axis):
    return lax.dynamic_index_in_dim(values, index, axis, keepdims=False)


def delay_rows(values, lag):
    widths = ((0, 0), (lag, 0)) + ((0, 0),) * (values.ndim - 2)
    return jnp.pad(values, widths)[:, : values.shape[1]]


def advance_rows(values, lag):
    widths = ((0, 0), (0, lag)) + ((0, 0),) * (values.ndim - 2)
    return jnp.pad(values, widths)[:, lag:]


def lag_masks(seg_ids, kernel_len):
    masks_list = []
    for lag in range(1, kernel_len):
        shifted = jnp.pad(seg_ids, ((0, 0), (lag, 0)), constant_values=-1)[:, : seg_ids.shape[1]]
        masks_list.append((shifted == seg_ids).astype(F32)[..., None])
    return masks_list


def rope_tables(seg_ids, half_dim):
    starts = jnp.sum((seg_ids[:, None, :] < seg_ids[:, :, None]).astype(jnp.int32), axis=2)
    places = jnp.arange(seg_ids.shape[1], dtype=jnp.int32)[None, :] - starts
    freqs = jnp.power(THETA, -(2.0 * jnp.arange(half_dim, dtype=F32)) / (2.0 * half_dim))
    angles = places.astype(F32)[..., None] * freqs
    return (jnp.cos(angles), jnp.sin(angles))


class Peers:
    def __init__(self):
        self.section = lax.axis_index("section")
        place = lax.axis_index("tensor")
        self.core = place % 2
        self.chip = place // 2
        self.mate = {"tensor": place + 1 - 2 * self.core}
        self.beside = {"tensor": place + 2 - 4 * self.chip}
        self.across = {"section": 1 - self.section}
        self.corner = {"section": 1 - self.section, "tensor": place + 2 - 4 * self.chip}


def greet(signalled, count):
    barrier = pltpu.get_barrier_semaphore()
    for device in signalled:
        pl.semaphore_signal(barrier, inc=1, device_id=device, device_id_type=MESH)
    pl.semaphore_wait(barrier, count)


def remote(source, target, send, receive, device):
    return pltpu.make_async_remote_copy(
        src_ref=source,
        dst_ref=target,
        send_sem=send,
        recv_sem=receive,
        device_id=device,
        device_id_type=MESH,
    )


def loop(count, body):
    lax.fori_loop(0, count, lambda i, unused: (body(i), 0)[1], 0)


def tile_rows(index):
    return pl.ds(pl.multiple_of(index * TILE, TILE), TILE)


def home_tile(j, chip, per_chip):
    each = per_chip // TILE
    return ((j // each) * 2 + chip) * each + j % each


def rms_tile(values):
    return lax.rsqrt(jnp.mean(values * values, axis=-1, keepdims=True) + EPSILON)


def norm_back_tile(values, gain, grad):
    scale = rms_tile(values)
    normed = values * scale
    weighted = grad * gain
    inner = jnp.mean(weighted * normed, axis=-1, keepdims=True)
    return scale * (weighted - normed * inner), grad * normed


def comm_call(kernel, name, number, inputs, outs, scratch, where, micros=52):
    return pl.pallas_call(
        kernel,
        name=name,
        out_shape=outs,
        in_specs=[pl.BlockSpec(memory_space=space) for space in where],
        out_specs=tuple(pl.BlockSpec(memory_space=pltpu.VMEM) for unused in outs),
        scratch_shapes=scratch,
        cost_estimate=estimate(micros),
        compiler_params=pltpu.CompilerParams(
            collective_id=number, has_side_effects=True, vmem_limit_bytes=VMEM_BYTES
        ),
    )(*inputs)


def full_tile(i, core, per_chip):
    each = per_chip // TILE
    return ((i // each) * 2 + core) * each + i % each


def sum_tiles(active, backward, per_chip, *refs):
    if backward:
        part, hidden, grad, gain, out, full, gain_out = refs[:7]
        scratch = refs[7:]
    else:
        part, residual, gain, out, full, home_low = refs[:6]
        scratch = refs[6:]
    mine, from_mate, summed, from_chip, relayed = scratch[:5]
    own_s, mate_s, mate_r, chip_s, chip_r, relay_s, relay_r, low_s, low_r = scratch[5:]
    peers = Peers()
    count = mine.shape[0] // TILE
    pairs = count // 2

    def own_rows(i):
        return tile_rows(full_tile(i, peers.core, per_chip))

    def own_copy(i):
        return pltpu.make_async_copy(part.at[own_rows(i)], mine.at[tile_rows(i)], own_s.at[i])

    def mate_copy(i):
        theirs = tile_rows(full_tile(i, 1 - peers.core, per_chip))
        target = from_mate.at[tile_rows(i)]
        return remote(part.at[theirs], target, mate_s.at[i], mate_r.at[i], peers.mate)

    def direct(i):
        rows = tile_rows(i)
        return remote(summed.at[rows], from_chip.at[rows], chip_s.at[i], chip_r.at[i], peers.beside)

    def detour(p):
        return remote(
            summed.at[tile_rows(2 * p)],
            relayed.at[tile_rows(p)],
            chip_s.at[2 * p],
            relay_r.at[p],
            peers.corner,
        )

    def back(p):
        return remote(
            relayed.at[tile_rows(p)],
            from_chip.at[tile_rows(2 * p)],
            relay_s.at[p],
            chip_r.at[2 * p],
            peers.across,
        )

    def low_copy(i):
        rows = own_rows(i)
        return remote(full.at[rows], full.at[rows], low_s.at[i], low_r.at[i], peers.mate)

    def low_wait(i):
        rows = tile_rows(full_tile(i, 1 - peers.core, per_chip))
        remote(full.at[rows], full.at[rows], low_s.at[i], low_r.at[i], peers.mate).wait_recv()

    @pl.when(peers.section == active)
    def work():
        loop(count, lambda i: own_copy(i).start())
        greet([peers.mate, peers.beside, peers.across], 3)
        loop(count, lambda i: mate_copy(i).start())

        def first(p):
            for k in range(2):
                i = 2 * p + k
                rows = tile_rows(i)
                own_copy(i).wait()
                mate_copy(i).wait_recv()
                total = mine[rows, :].astype(F32) + from_mate[rows, :].astype(F32)
                out[rows, :] = total
                summed[rows, :] = total.astype(BF)
                if k == 0:
                    detour(p).start()
                else:
                    direct(i).start()

        loop(pairs, first)
        if backward:
            gain_out[...] = jnp.zeros_like(gain_out)

        def second(i):
            rows = tile_rows(i)
            direct(i).wait_recv()
            total = out[rows, :] + from_chip[rows, :].astype(F32)
            if backward:
                change, terms = norm_back_tile(hidden[rows, :], gain[...], total)
                result = grad[rows, :].astype(F32) + change
                lower = result.astype(BF)
                ours = ((i * TILE) // per_chip) % 2 == peers.chip
                added = jnp.sum(terms, axis=0, keepdims=True)
                gain_out[...] += jnp.where(ours, added, jnp.zeros_like(added))
            else:
                result = residual[rows, :].astype(F32) + total
                lower = (result * rms_tile(result) * gain[...]).astype(BF)
            out[rows, :] = result
            full[own_rows(i), :] = lower
            if not backward:
                home_low[rows, :] = lower
            low_copy(i).start()

        loop(count, second)

        def finish(i):
            mate_copy(i).wait_send()
            direct(i).wait_send()
            low_copy(i).wait_send()
            low_wait(i)

        loop(count, finish)

    @pl.when(peers.section != active)
    def relay():
        greet([peers.corner], 1)

        def step(p):
            detour(p).wait_recv()
            back(p).start()

        loop(pairs, step)
        if not backward:

            def keep(i):
                home_low[tile_rows(i), :] = residual[tile_rows(i), :].astype(BF)

            loop(count, keep)
        loop(pairs, lambda p: back(p).wait_send())


def sum_call(active, number, backward, per_chip, part, *rest):
    size, width = part.shape
    size //= 2
    count = size // TILE
    outs = (
        jax.ShapeDtypeStruct((size, width), F32),
        jax.ShapeDtypeStruct((2 * size, width), BF),
    )
    outs += (jax.ShapeDtypeStruct((1, width), F32) if backward else jax.ShapeDtypeStruct((size, width), BF),)
    scratch = [pltpu.VMEM((size, width), BF)] * 4 + [pltpu.VMEM((size // 2, width), BF)]
    sizes = [count, count, count, count, count, count // 2, count // 2, count, count]
    scratch += [pltpu.SemaphoreType.DMA((n,)) for n in sizes]
    return comm_call(
        functools.partial(sum_tiles, active, backward, per_chip),
        "sum_back" if backward else "sum_norm",
        number,
        (part,) + rest,
        outs,
        scratch,
        [pl.ANY] + [pltpu.VMEM] * len(rest),
    )


def spread_tiles(normed, peers, per_chip, gain, home, full, sems, arrived, source):
    chip_s, chip_r, low_s, low_r = sems
    half = home.shape[0] // TILE // 2

    def place(j, chip):
        return home_tile(j, chip, per_chip)

    def chip_copy(j):
        rows = tile_rows(place(j, peers.chip))
        return remote(source(j), home.at[rows], chip_s.at[j], chip_r.at[j], peers.beside)

    def chip_wait(j):
        rows = tile_rows(place(j, 1 - peers.chip))
        remote(source(j), home.at[rows], chip_s.at[j], chip_r.at[j], peers.beside).wait_recv()

    def low_copy(i, k, core):
        rows = tile_rows(full_tile(i, core, per_chip))
        return remote(full.at[rows], full.at[rows], low_s.at[k], low_r.at[k], peers.mate)

    def lower(i, values):
        wide = values.astype(F32)
        if normed == "all":
            wide = wide * rms_tile(wide) * gain[...]
        elif normed == "first":
            scale = rms_tile(wide)
            wide = wide * jnp.where(peers.section == 0, scale, jnp.ones_like(scale)) * gain[...]
        full[tile_rows(full_tile(i, peers.core, per_chip)), :] = wide.astype(BF)

    def own(j):
        arrived(j)
        chip_copy(j).start()
        i = place(j, peers.chip)
        values = source(j)[...]
        home[tile_rows(i), :] = values
        lower(i, values)
        low_copy(i, j, peers.core).start()

    loop(half, own)

    def other(j):
        chip_wait(j)
        i = place(j, 1 - peers.chip)
        lower(i, home[tile_rows(i), :])
        low_copy(i, half + j, peers.core).start()

    loop(half, other)

    def finish(j):
        chip_copy(j).wait_send()
        low_copy(place(j, peers.chip), j, peers.core).wait_send()
        low_copy(place(j, 1 - peers.chip), half + j, peers.core).wait_send()
        low_copy(place(j, peers.chip), j, 1 - peers.core).wait_recv()
        low_copy(place(j, 1 - peers.chip), half + j, 1 - peers.core).wait_recv()

    loop(half, finish)


def start_tiles(per_chip, local, gain, home, full, *sems):
    peers = Peers()
    greet([peers.mate, peers.beside], 2)
    spread_tiles(
        "first",
        peers,
        per_chip,
        gain,
        home,
        full,
        sems,
        lambda j: None,
        lambda j: local.at[tile_rows(j)],
    )


def start_call(number, per_chip, local, gain):
    size, width = local.shape
    half = size // TILE
    outs = (
        jax.ShapeDtypeStruct((2 * size, width), BF),
        jax.ShapeDtypeStruct((4 * size, width), BF),
    )
    return comm_call(
        functools.partial(start_tiles, per_chip),
        "start",
        number,
        (local, gain),
        outs,
        [pltpu.SemaphoreType.DMA((n,)) for n in (half, half, 2 * half, 2 * half)],
        [pltpu.VMEM, pltpu.VMEM],
    )


def scatter_steps(peers, per_chip, parts, mine, from_mate, summed, from_chip, sems, finished):
    own_s, mate_s, mate_r, chip_s, chip_r = sems
    half = mine.shape[0] // TILE // 2

    def rows_of(j, chip, core):
        return tile_rows(full_tile(home_tile(j, chip, per_chip), core, per_chip))

    def slot(j, k):
        return tile_rows(half * k + j)

    def chip_of(k):
        return 1 - peers.chip if k == 0 else peers.chip

    def own_copy(j, k, part=parts[0]):
        source = part.at[rows_of(j, chip_of(k), peers.core)]
        return pltpu.make_async_copy(source, mine.at[slot(j, k)], own_s.at[half * k + j])

    def mate_copy(j, k, part=parts[0]):
        source = part.at[rows_of(j, chip_of(k), 1 - peers.core)]
        index = half * k + j
        target = from_mate.at[slot(j, k)]
        return remote(source, target, mate_s.at[index], mate_r.at[index], peers.mate)

    def chip_copy(j):
        rows = tile_rows(j)
        return remote(summed.at[rows], from_chip.at[rows], chip_s.at[j], chip_r.at[j], peers.beside)

    def begin(part):
        for k in range(2):
            loop(half, lambda j: own_copy(j, k, part).start())
            loop(half, lambda j: mate_copy(j, k, part).start())

    if len(parts) == 1:
        begin(parts[0])
    else:
        for section, part in enumerate(parts):
            pl.when(peers.section == section)(functools.partial(begin, part))

    def both(j, k):
        own_copy(j, k).wait()
        mate_copy(j, k).wait_recv()
        return mine[slot(j, k), :].astype(F32) + from_mate[slot(j, k), :].astype(F32)

    def away(j):
        summed[tile_rows(j), :] = both(j, 0).astype(BF)
        chip_copy(j).start()

    loop(half, away)

    def last(j):
        total = both(j, 1)
        chip_copy(j).wait_recv()
        finished(j, total + from_chip[tile_rows(j), :].astype(F32))

    loop(half, last)

    def finish(j):
        mate_copy(j, 0).wait_send()
        mate_copy(j, 1).wait_send()
        chip_copy(j).wait_send()

    loop(half, finish)


def scatter_scratch(size, width):
    half = size // TILE // 2
    buffers = [pltpu.VMEM((size, width), BF)] * 2 + [pltpu.VMEM((size // 2, width), BF)] * 2
    counts = (2 * half, 2 * half, 2 * half, half, half)
    return buffers + [pltpu.SemaphoreType.DMA((n,)) for n in counts]


def end_tiles(per_chip, first, second, out, *scratch):
    peers = Peers()
    greet([peers.mate, peers.beside], 2)

    def finished(j, total):
        out[tile_rows(j), :] = total

    scatter_steps(peers, per_chip, (first, second), *scratch[:4], scratch[4:], finished)


def end_call(number, per_chip, first, second):
    size, width = first.shape
    size //= 2
    return comm_call(
        functools.partial(end_tiles, per_chip),
        "end",
        number,
        (first, second),
        (jax.ShapeDtypeStruct((size // 2, width), F32),),
        scatter_scratch(size, width),
        [pl.ANY, pl.ANY],
    )[0]


def hop_tiles(source, backward, per_chip, *refs):
    if backward:
        part, values, grad, gain, next_gain, home, full, gain_out = refs[:8]
        scratch = refs[8:]
    else:
        part, values, next_gain, home, full = refs[:5]
        scratch = refs[5:]
    crossing, landed, cross_s, cross_r = scratch[:4]
    spread_sems = scratch[4:8]
    buffers = scratch[8:12]
    scatter_sems = scratch[12:]
    peers = Peers()
    half = crossing.shape[0] // TILE

    def cross_copy(j):
        rows = tile_rows(j)
        return remote(
            crossing.at[rows], landed.at[rows], cross_s.at[j], cross_r.at[j], peers.across
        )

    @pl.when(peers.section == source)
    def give():
        greet([peers.mate, peers.beside], 3)
        if backward:
            gain_out[...] = jnp.zeros_like(gain_out)

        def finished(j, total):
            own = tile_rows(home_tile(j, peers.chip, per_chip))
            if backward:
                change, terms = norm_back_tile(values[own, :].astype(F32), gain[...], total)
                result = grad[own, :] + change
                gain_out[...] += jnp.sum(terms, axis=0, keepdims=True)
            else:
                result = values[own, :] + total
            crossing[tile_rows(j), :] = result.astype(BF)
            cross_copy(j).start()

        scatter_steps(peers, per_chip, (part,), *buffers, scatter_sems, finished)
        loop(half, lambda j: cross_copy(j).wait_send())

    @pl.when(peers.section != source)
    def take():
        greet([peers.mate, peers.beside, peers.across], 2)
        spread_tiles(
            None if backward else "all",
            peers,
            per_chip,
            next_gain,
            home,
            full,
            spread_sems,
            lambda j: cross_copy(j).wait_recv(),
            lambda j: landed.at[tile_rows(j)],
        )


def hop_call(source, number, backward, per_chip, part, *rest):
    size, width = part.shape
    size //= 2
    half = size // TILE // 2
    outs = (
        jax.ShapeDtypeStruct((size, width), BF),
        jax.ShapeDtypeStruct((2 * size, width), BF),
    )
    if backward:
        outs += (jax.ShapeDtypeStruct((1, width), F32),)
    scratch = [pltpu.VMEM((size // 2, width), BF)] * 2
    scratch += [pltpu.SemaphoreType.DMA((n,)) for n in (half, half, half, half, 2 * half, 2 * half)]
    return comm_call(
        functools.partial(hop_tiles, source, backward, per_chip),
        "hop_back" if backward else "hop",
        number,
        (part,) + rest,
        outs,
        scratch + scatter_scratch(size, width),
        [pl.ANY] + [pltpu.VMEM] * len(rest),
    )


def silu_parts(gu):
    lanes = gu.shape[1] // 2
    gate = gu[:, :lanes].astype(F32)
    up = gu[:, lanes:].astype(F32)
    return gate, up, 1.0 / (1.0 + jnp.exp(-gate))


def load_up(up_w, up_v, sems):
    hidden = up_w.shape[1]
    lanes = up_v.shape[0] // 2
    copies = [
        pltpu.make_async_copy(up_w.at[c], up_v.at[pl.ds(c * lanes, hidden)], sems.at[c])
        for c in range(2)
    ]
    for c, copy in enumerate(copies):
        copy.start()
        if lanes > hidden:
            up_v[c * lanes + hidden : (c + 1) * lanes, :] = jnp.zeros(
                (lanes - hidden, up_v.shape[1]), BF
            )
    return copies


def load_down(down_w, down_v, sems):
    hidden = down_w.shape[0]
    lanes = down_v.shape[0]
    copy = pltpu.make_async_copy(down_w, down_v.at[pl.ds(0, hidden)], sems.at[2])
    copy.start()
    if lanes > hidden:
        down_v[hidden:, :] = jnp.zeros((lanes - hidden, down_v.shape[1]), BF)
    return [copy]


def wait_all(copies):
    for copy in copies:
        copy.wait()


def only(active, run):
    if active is None:
        run()
    else:
        pl.when(lax.axis_index("section") == active)(run)


def stream(body, grid, inputs, outs):
    def spec(item):
        ref, rows, place = item
        return pl.BlockSpec((rows, ref.shape[1]), lambda *g: (place(*g), 0))

    pltpu.emit_pipeline(
        body,
        grid=grid,
        in_specs=[spec(item) for item in inputs],
        out_specs=[spec(item) for item in outs],
    )(*[item[0] for item in inputs + outs])


def gate_up_body(up_v):
    def body(z_t, gu_t):
        gu_t[...] = dot(z_t[...], up_v[...], (1, 1)).astype(BF)

    return body


def ffn_tiles(active, tile, with_down, *refs):
    if with_down:
        full, up_w, down_w, gu, part, up_v, down_v, sems = refs
    else:
        full, up_w, gu, up_v, sems = refs

    def run():
        copies = load_up(up_w, up_v, sems)
        if with_down:
            copies += load_down(down_w, down_v, sems)
        wait_all(copies)

        def body(z_t, gu_t, part_t):
            low = dot(z_t[...], up_v[...], (1, 1)).astype(BF)
            gu_t[...] = low
            gate, up, sig = silu_parts(low)
            act = (gate * sig * up).astype(BF)
            part_t[...] = dot(act, down_v[...], (1, 0)).astype(BF)

        here = lambda i: i
        grid = (full.shape[0] // tile,)
        if with_down:
            stream(body, grid, [(full, tile, here)], [(gu, tile, here), (part, tile, here)])
        else:
            stream(gate_up_body(up_v), grid, [(full, tile, here)], [(gu, tile, here)])

    only(active, run)


def down_tiles(active, tile, gu, down_w, *refs):
    part, down_v, sems = refs[-3:]

    def run():
        wait_all(load_down(down_w, down_v, sems))

        def body(gu_t, part_t):
            gate, up, sig = silu_parts(gu_t[...])
            part_t[...] = dot((gate * sig * up).astype(BF), down_v[...], (1, 0)).astype(BF)

        here = lambda i: i
        stream(body, (gu.shape[0] // tile,), [(gu, tile, here)], [(part, tile, here)])

    only(active, run)


def back_body(up_v, down_v):
    def body(g_t, gu_t, grad_t, act_t, *part_t):
        grad_act = dot(g_t[...], down_v[...], (1, 1))
        gate, up, sig = silu_parts(gu_t[...])
        silu = gate * sig
        act_t[...] = (silu * up).astype(BF)
        slope = sig + silu * (1.0 - sig)
        lanes = gate.shape[1]
        grad_t[:, :lanes] = (grad_act * up * slope).astype(BF)
        grad_t[:, lanes:] = (grad_act * silu).astype(BF)
        if part_t:
            part_t[0][...] = dot(grad_t[...], up_v[...], (1, 0)).astype(BF)

    return body


def ffn_back_tiles(active, tile, shards, *refs):
    grad, gu, up_w, down_w = refs[:4]
    up_v, down_v, sems = refs[-3:]
    outs = refs[-4 - (4 if shards > 1 else 2) : -3]

    def run():
        wait_all(load_up(up_w, up_v, sems) + load_down(down_w, down_v, sems))
        body = back_body(up_v, down_v)
        part = outs[-1]
        if shards == 1:
            here = lambda i: i
            items = [(out, tile, here) for out in outs]
            grid = (grad.shape[0] // tile,)
            stream(body, grid, [(grad, tile, here), (gu, tile, here)], items)
            return
        core = lax.axis_index("tensor") % 2
        spot = lax.axis_index("dp")
        count = grad.shape[0] // tile // 2
        for half in range(2):
            chosen = core if half == 0 else 1 - core
            here = lambda i: 2 * i + chosen
            there = lambda i: spot * count + i
            stream(
                body,
                (count,),
                [(grad, tile, here), (gu, tile, here)],
                [(outs[half], tile, there), (outs[2 + half], tile, there), (part, tile, here)],
            )

    only(active, run)


def others_up_tiles(active, tile, shards, source, up_w, *refs):
    out, up_v, sems = refs[-3:]

    def run():
        wait_all(load_up(up_w, up_v, sems))
        spot = lax.axis_index("dp")
        count = source.shape[0] // tile // shards
        place = lambda k, i: ((spot + 1 + k) % shards) * count + i
        items = [(source, tile, place)], [(out, tile, place)]
        stream(gate_up_body(up_v), (shards - 1, count), *items)

    only(active, run)


def others_back_tiles(tile, shards, first, second, down_w, gu, unused, grad_gu, act, down_v, sems):
    wait_all(load_down(down_w, down_v, sems))
    spot = lax.axis_index("dp")
    count = first.shape[0] // tile // shards
    place = lambda k, i: ((spot + 1 + k) % shards) * count + i

    def run(grad):
        stream(
            back_body(None, down_v),
            (shards - 1, count),
            [(grad, tile, place), (gu, tile, place)],
            [(grad_gu, tile, place), (act, tile, place)],
        )

    only(0, lambda: run(first))
    only(1, lambda: run(second))


def ffn_pallas(kernel, name, inputs, outs, weights, micros, aliases=None):
    return pl.pallas_call(
        kernel,
        name=name,
        out_shape=tuple(jax.ShapeDtypeStruct(shape, BF) for shape in outs),
        in_specs=[pl.BlockSpec(memory_space=pl.ANY)] * len(inputs),
        out_specs=tuple(pl.BlockSpec(memory_space=pl.ANY) for unused in outs),
        scratch_shapes=[pltpu.VMEM(shape, BF) for shape in weights]
        + [pltpu.SemaphoreType.DMA((3,))],
        input_output_aliases=aliases or {},
        cost_estimate=estimate(micros),
        compiler_params=pltpu.CompilerParams(vmem_limit_bytes=VMEM_BYTES),
    )(*inputs)


def estimate(micros):
    return pl.CostEstimate(flops=0, bytes_accessed=int(micros * 3.3e6), transcendentals=0)


def weight_shapes(up_w):
    lanes = padded(up_w.shape[1])
    return (2 * lanes, up_w.shape[2]), (lanes, up_w.shape[2])


def ffn_call(active, tile, full, up_w, down_w):
    up, down = weight_shapes(up_w)
    gu = (full.shape[0], up[0])
    if down_w is None:
        kernel = functools.partial(ffn_tiles, active, tile, False)
        return ffn_pallas(kernel, "gate_up", (full, up_w), (gu,), (up,), 30)[0]
    kernel = functools.partial(ffn_tiles, active, tile, True)
    return ffn_pallas(kernel, "ffn", (full, up_w, down_w), (gu, full.shape), (up, down), 44)


def down_call(active, tile, gu, down_w, *earlier):
    rows, lanes = gu.shape
    return ffn_pallas(
        functools.partial(down_tiles, active, tile),
        "down",
        (gu, down_w) + earlier,
        ((rows, down_w.shape[1]),),
        ((lanes // 2, down_w.shape[1]),),
        20,
    )[0]


def ffn_back_call(active, tile, shards, grad, gu, up_w, down_w, into=()):
    up, down = weight_shapes(up_w)
    if shards == 1:
        outs = ((grad.shape[0], up[0]), (grad.shape[0], down[0]))
    else:
        rows = grad.shape[0] // 2 * shards
        outs = ((rows, up[0]),) * 2 + ((rows, down[0]),) * 2
    return ffn_pallas(
        functools.partial(ffn_back_tiles, active, tile, shards),
        "ffn_back",
        (grad, gu, up_w, down_w) + tuple(into),
        outs + (grad.shape,),
        (up, down),
        48,
        {4 + i: i for i in range(len(into))},
    )


def others_up_call(active, tile, shards, source, up_w, into, *earlier):
    return ffn_pallas(
        functools.partial(others_up_tiles, active, tile, shards),
        "others_up",
        (source, up_w, into) + earlier,
        (into.shape,),
        (weight_shapes(up_w)[0],),
        42,
        {2: 0},
    )[0]


def others_back_call(tile, shards, first, second, down_w, gu, act):
    return ffn_pallas(
        functools.partial(others_back_tiles, tile, shards),
        "others_back",
        (first, second, down_w, gu, act),
        (gu.shape, act.shape),
        ((act.shape[1], down_w.shape[1]),),
        32,
        {3: 0, 4: 1},
    )


def hold_call(values, *others):
    if not others:
        return values
    return pl.pallas_call(
        lambda *refs: None,
        name="hold",
        out_shape=jax.ShapeDtypeStruct(values.shape, values.dtype),
        in_specs=[pl.BlockSpec(memory_space=pl.ANY)] * (1 + len(others)),
        out_specs=pl.BlockSpec(memory_space=pl.ANY),
        input_output_aliases={0: 0},
        cost_estimate=estimate(1),
        compiler_params=pltpu.CompilerParams(has_side_effects=True),
    )(values, *others)


def total_tiles(values, out, held, landed, sends, receives):
    peers = Peers()
    spot = lax.axis_index("dp")
    partners = [
        peers.mate,
        peers.beside,
        peers.across,
        {"dp": spot + 1 - 2 * (spot % 2)},
        {"dp": spot + 2 - 4 * (spot // 2)},
    ]
    greet(partners, len(partners))
    held[0] = values[...]
    for i, partner in enumerate(partners):
        copy = remote(held.at[i], landed.at[i], sends.at[i], receives.at[i], partner)
        copy.start()
        copy.wait()
        held[i + 1] = held[i] + landed[i]
    out[...] = held[len(partners)]


def total_call(number, values):
    count = 5
    return comm_call(
        total_tiles,
        "total",
        number,
        (values,),
        (jax.ShapeDtypeStruct(values.shape, F32),),
        [
            pltpu.VMEM((count + 1,) + values.shape, F32),
            pltpu.VMEM((count,) + values.shape, F32),
            pltpu.SemaphoreType.DMA((count,)),
            pltpu.SemaphoreType.DMA((count,)),
        ],
        [pltpu.VMEM],
    )[0]


def rotated(values):
    half = values.shape[-1] // 2
    return jnp.concatenate([-values[:, half:], values[:, :half]], axis=-1)


def dot(left, right, dims):
    return lax.dot_general(left, right, ((dims[:1], dims[1:]), ((), ())), preferred_element_type=F32)


def attend_tiles(groups, size, block, raw, cosine, sine, seg_col, seg_row, gains, out, probs, totals, turned, heads):
    length = raw.shape[1]
    cos_t = cosine[0]
    sin_t = sine[0]
    scaling = size ** (-0.5)

    def prepared(values, gain):
        normed = values * rms_tile(values) * gain
        return normed * cos_t + rotated(normed) * sin_t

    for g in range(groups):
        lanes = slice(g * size, (g + 1) * size)
        query = (prepared(raw[0, :, lanes], gains[0:1, :]).astype(BF) * scaling).astype(BF)
        heads[g] = query
        turned[0, :, lanes] = query
    lanes = slice(groups * size, (groups + 1) * size)
    keyed = prepared(raw[0, :, lanes], gains[1:2, :]).astype(BF)
    turned[0, :, lanes] = keyed
    lanes = slice((groups + 1) * size, (groups + 2) * size)
    valued = raw[0, :, lanes].astype(BF)
    turned[0, :, lanes] = valued
    ones = (lax.broadcasted_iota(jnp.int32, (length, size), 1) == 0).astype(BF)
    widened = jnp.concatenate([valued, ones], axis=1)
    used = (groups + 2) * size
    if used < turned.shape[2]:
        turned[0, :, used:] = jnp.zeros((length, turned.shape[2] - used), BF)
    for i in range(length // block):
        rows = slice(i * block, (i + 1) * block)
        span = (i + 1) * block
        query_pos = i * block + lax.broadcasted_iota(jnp.int32, (block, span), 0)
        key_pos = lax.broadcasted_iota(jnp.int32, (block, span), 1)
        allowed = (key_pos <= query_pos) & (seg_col[0, rows, :] == seg_row[0, :, :span])

        def head(g):
            scores = dot(heads[g, rows, :], keyed[:span], (1, 1))
            expon = jnp.exp(jnp.where(allowed, scores, NEGATIVE)).astype(BF)
            probs[0, 0, g, rows, :span] = expon
            summed = dot(expon, widened[:span], (1, 0))
            total = summed[:, size : size + 1]
            totals[0, 0, g, rows, :] = total
            heads[g, rows, :] = (summed[:, :size] * (1.0 / total)).astype(BF)

        for g in range(groups):
            head(g)
    for g in range(groups):
        out[0, :, g * size : (g + 1) * size] = heads[g]
    if groups * size < out.shape[2]:
        out[0, :, groups * size :] = jnp.zeros((length, out.shape[2] - groups * size), BF)


def attend_back_tiles(
    groups, size, block, raw, turned, probs, totals, out, grad_out, cosine, sine, gains, grad_raw, grad_gains, heads, grads, inner, query_grad, key_grad, val_grad
):
    length = raw.shape[1]
    cos_t = cosine[0]
    sin_t = sine[0]
    scaling = size ** (-0.5)

    @pl.when((pl.program_id(0) == 0) & (pl.program_id(1) == 0))
    def clear():
        grad_gains[...] = jnp.zeros_like(grad_gains)

    blocks = length // block
    for g in range(groups):
        lanes = slice(g * size, (g + 1) * size)
        shared = (grad_out[0, :, lanes].astype(F32) * (1.0 / totals[0, 0, g])).astype(BF)
        mean = jnp.sum(shared.astype(F32) * out[0, :, lanes].astype(F32), axis=-1, keepdims=True)
        for i in range(blocks):
            rows = slice(i * block, (i + 1) * block)
            into = slice(g * block, (g + 1) * block)
            heads[i, into, :] = turned[0, rows, lanes]
            grads[i, into, :] = shared[rows]
            inner[i, into, :] = mean[rows]
    keyed = turned[0, :, groups * size : (groups + 1) * size]
    valued = turned[0, :, (groups + 1) * size : (groups + 2) * size]
    key_grad[...] = jnp.zeros_like(key_grad)
    val_grad[...] = jnp.zeros_like(val_grad)
    for i in range(blocks):
        rows = slice(i * block, (i + 1) * block)
        span = (i + 1) * block
        low = jnp.concatenate([probs[0, 0, g, rows, :span] for g in range(groups)], axis=0)
        grad_probs = dot(grads[i], valued[:span], (1, 1))
        grad_scores = (low.astype(F32) * (grad_probs - inner[i])).astype(BF)
        back_q = dot(grad_scores, keyed[:span], (1, 0)) * scaling
        for g in range(groups):
            query_grad[g, rows, :] = back_q[g * block : (g + 1) * block]
        key_grad[:, :span] += dot(heads[i], grad_scores, (0, 0))
        val_grad[:, :span] += dot(grads[i], low, (0, 0))

    def back(values, gain, grad, which):
        grad = grad * cos_t - rotated(grad) * sin_t
        change, terms = norm_back_tile(values, gain, grad)
        grad_gains[which : which + 1, :] += jnp.sum(terms, axis=0, keepdims=True)
        return change.astype(BF)

    for g in range(groups):
        lanes = slice(g * size, (g + 1) * size)
        grad_raw[0, :, lanes] = back(raw[0, :, lanes], gains[0:1, :], query_grad[g], 0)
    lanes = slice(groups * size, (groups + 1) * size)
    grad_raw[0, :, lanes] = back(raw[0, :, lanes], gains[1:2, :], key_grad[...].T, 1)
    lanes = slice((groups + 1) * size, (groups + 2) * size)
    grad_raw[0, :, lanes] = val_grad[...].T.astype(BF)
    used = (groups + 2) * size
    if used < grad_raw.shape[2]:
        grad_raw[0, :, used:] = jnp.zeros((length, grad_raw.shape[2] - used), BF)


def attend_call(groups, size, kv_heads, raw, cosine, sine, segments, gains):
    rows, length, lanes = raw.shape
    lanes //= kv_heads
    out_lanes = padded(groups * size)
    block = min(256, length)
    whole = lambda r, k: (r, 0, 0)
    part = lambda r, k: (r, 0, k)
    return pl.pallas_call(
        functools.partial(attend_tiles, groups, size, block),
        name="attend",
        grid=(rows, kv_heads),
        in_specs=[
            pl.BlockSpec((1, length, lanes), part),
            pl.BlockSpec((1, length, size), whole),
            pl.BlockSpec((1, length, size), whole),
            pl.BlockSpec((1, length, 1), whole),
            pl.BlockSpec((1, 1, length), whole),
            pl.BlockSpec((2, size), lambda r, k: (0, 0)),
        ],
        out_specs=(
            pl.BlockSpec((1, length, out_lanes), part),
            pl.BlockSpec((1, 1, groups, length, length), lambda r, k: (r, k, 0, 0, 0)),
            pl.BlockSpec((1, 1, groups, length, 1), lambda r, k: (r, k, 0, 0, 0)),
            pl.BlockSpec((1, length, lanes), part),
        ),
        out_shape=(
            jax.ShapeDtypeStruct((rows, length, kv_heads * out_lanes), BF),
            jax.ShapeDtypeStruct((rows, kv_heads, groups, length, length), BF),
            jax.ShapeDtypeStruct((rows, kv_heads, groups, length, 1), F32),
            jax.ShapeDtypeStruct((rows, length, kv_heads * lanes), BF),
        ),
        scratch_shapes=[pltpu.VMEM((groups, length, size), BF)],
        cost_estimate=estimate(27),
        compiler_params=pltpu.CompilerParams(vmem_limit_bytes=VMEM_BYTES),
    )(raw, cosine, sine, segments[:, :, None], segments[:, None, :], gains)


def attend_back_call(groups, size, kv_heads, raw, turned, probs, totals, out, grad_out, cosine, sine, gains):
    rows, length, lanes = raw.shape
    lanes //= kv_heads
    out_lanes = padded(groups * size)
    block = min(256, length)
    whole = lambda r, k: (r, 0, 0)
    part = lambda r, k: (r, 0, k)
    fixed = lambda r, k: (0, 0)
    return pl.pallas_call(
        functools.partial(attend_back_tiles, groups, size, block),
        name="attend_back",
        grid=(rows, kv_heads),
        in_specs=[
            pl.BlockSpec((1, length, lanes), part),
            pl.BlockSpec((1, length, lanes), part),
            pl.BlockSpec((1, 1, groups, length, length), lambda r, k: (r, k, 0, 0, 0)),
            pl.BlockSpec((1, 1, groups, length, 1), lambda r, k: (r, k, 0, 0, 0)),
            pl.BlockSpec((1, length, out_lanes), part),
            pl.BlockSpec((1, length, out_lanes), part),
            pl.BlockSpec((1, length, size), whole),
            pl.BlockSpec((1, length, size), whole),
            pl.BlockSpec((2, size), fixed),
        ],
        out_specs=(
            pl.BlockSpec((1, length, lanes), part),
            pl.BlockSpec((2, size), fixed),
        ),
        out_shape=(
            jax.ShapeDtypeStruct((rows, length, kv_heads * lanes), BF),
            jax.ShapeDtypeStruct((2, size), F32),
        ),
        scratch_shapes=[
            pltpu.VMEM((length // block, groups * block, size), BF),
            pltpu.VMEM((length // block, groups * block, size), BF),
            pltpu.VMEM((length // block, groups * block, 1), F32),
            pltpu.VMEM((groups, length, size), F32),
            pltpu.VMEM((size, length), F32),
            pltpu.VMEM((size, length), F32),
        ],
        cost_estimate=estimate(43),
        compiler_params=pltpu.CompilerParams(vmem_limit_bytes=VMEM_BYTES),
    )(raw, turned, probs, totals, out, grad_out, cosine, sine, gains)


def padded(lanes):
    return (lanes + 127) // 128 * 128


def on_device(
    boundary,
    segments,
    norm_gains,
    qk_gains,
    conv_in,
    conv_kernel,
    conv_out,
    attn_query,
    attn_keyval,
    attn_out,
    ffn_gate_up,
    ffn_down,
):
    is_first = lax.axis_index("section") == 0
    place = lax.axis_index("tensor")
    chips = lax.axis_size("tensor") // 2
    core = place % 2
    chip = place // 2
    steps = [1 << k for k in range(chips.bit_length() - 1)]
    local = boundary[0]
    rows, seq_local, width = local.shape
    seq = segments.shape[1]
    head_dim = qk_gains.shape[1]
    kv_here = attn_keyval.shape[2] // head_dim
    groups = attn_query.shape[1] // head_dim // kv_here
    hidden = ffn_down.shape[2]
    dp = lax.axis_size("dp")
    channels = conv_out.shape[0]
    gains = norm_gains.astype(F32)
    head_gains = qk_gains.astype(F32)
    kernel = conv_kernel.astype(F32)
    up_w = ffn_gate_up[0].transpose(1, 2, 0)
    down_w = ffn_down[0].T
    conv_in_w = conv_in.reshape(width, 3 * channels)
    home_shape = (rows, chips, seq_local, width)
    fused = chips == 2 and dp == 4 and seq_local % TILE == 0

    def mate(values, section):
        return permute(values, section, "tensor", lambda i: i ^ 1)

    def chip_gather(values, section):
        held = values[:, None]
        for step in steps:
            other = permute(held, section, "tensor", lambda i: i ^ (2 * step))
            upper = (chip // step) % 2 == 1
            held = jnp.where(
                upper,
                jnp.concatenate([other, held], axis=1),
                jnp.concatenate([held, other], axis=1),
            )
        return held

    def chip_sum(values, section):
        for step in steps:
            values = values + permute(
                values.astype(BF), section, "tensor", lambda i: i ^ (2 * step)
            ).astype(F32)
        return values

    def chip_scatter(values, section):
        for step in reversed(steps):
            halves = values.reshape((rows, 2, step) + values.shape[2:])
            upper = (chip // step) % 2
            kept = pick(halves, upper, 1)
            sent = pick(halves, 1 - upper, 1).astype(BF)
            values = kept + permute(sent, section, "tensor", lambda i: i ^ (2 * step)).astype(F32)
        return values[:, 0]

    def share(mine, section):
        other = mate(mine, section)
        both = jnp.where(
            core == 0, jnp.stack([mine, other], axis=2), jnp.stack([other, mine], axis=2)
        )
        return both.reshape(rows * seq, width)

    def core_sum(part, section):
        parts = part.reshape(rows, chips, 2, seq_local, width)
        return pick(parts, core, 2).astype(F32) + mate(pick(parts, 1 - core, 2), section).astype(F32)

    def tokens(values):
        return values.reshape(-1, width)

    def homed(values):
        return values.reshape(home_shape)

    def row(gain):
        return gain.reshape(1, width)

    def begin(gain):
        if fused:
            gain = jnp.where(is_first, gain, jnp.ones_like(gain))
            home, full = start_call(0, seq_local, tokens(local), row(gain))
            return homed(home), full
        first = chip_gather(local, 0)
        second = chip_gather(local, 1)
        return (
            jnp.where(is_first, first, second),
            jnp.where(is_first, share(norm(first.astype(F32), gain), 0), share(second, 1)),
        )

    def sum_norm(section, number, part, residual, gain):
        if fused:
            out, full, low = sum_call(
                section, number, False, seq_local, part, tokens(residual), row(gain)
            )
            return homed(out), full, low
        out = residual.astype(F32) + chip_sum(core_sum(part, section), section)
        return out, share(norm(out, gain), section), None

    def sum_back(section, number, part, hidden_in, grad, gain):
        if fused:
            out, full, terms = sum_call(
                section,
                number,
                True,
                seq_local,
                part,
                tokens(hidden_in),
                tokens(grad),
                row(gain),
            )
            return homed(out), full, terms[0]
        dz = chip_sum(core_sum(part, section), section)
        change, terms = norm_back(hidden_in, gain, dz)
        out = grad.astype(F32) + change
        return out, share(out.astype(BF), section), jnp.sum(pick(terms, chip, 1), axis=(0, 1))

    def hop(number, part, hidden_in, gain):
        if fused:
            home, full = hop_call(
                0, number, False, seq_local, part, tokens(hidden_in), row(gain)
            )
            return homed(home), full
        result = pick(hidden_in, chip, 1) + chip_scatter(core_sum(part, 0), 0)
        home = chip_gather(lax.ppermute(result.astype(BF), "section", [(0, 1)]), 1)
        return home, share(norm(home.astype(F32), gain), 1)

    def hop_back(number, part, values, grad, gain):
        if fused:
            home, full, terms = hop_call(
                1,
                number,
                True,
                seq_local,
                part,
                tokens(values),
                tokens(grad),
                row(gain),
                row(gain),
            )
            return homed(home), full, terms[0]
        dz = chip_scatter(core_sum(part, 1), 1)
        change, terms = norm_back(pick(values, chip, 1).astype(F32), gain, dz)
        result = pick(grad, chip, 1) + change
        home = chip_gather(lax.ppermute(result.astype(BF), "section", [(1, 0)]), 0)
        return home, share(home, 0), jnp.sum(terms, axis=(0, 1))

    def end(number, first, second):
        if fused:
            return end_call(number, seq_local, first, second).reshape(rows, seq_local, width)
        return jnp.where(
            is_first,
            chip_scatter(core_sum(first, 0), 0),
            chip_scatter(core_sum(second, 1), 1),
        )

    def either(first, first_args, second, second_args):
        def zeros(function, args):
            shapes = jax.eval_shape(function, *args)
            return jax.tree.map(lambda one: jnp.zeros(one.shape, one.dtype), shapes)

        return lax.cond(
            is_first,
            lambda one, two: (first(*one), zeros(second, two)),
            lambda one, two: (zeros(first, one), second(*two)),
            first_args,
            second_args,
        )

    def nothing():
        return ()

    def by_row(values):
        return values.reshape(rows, seq, values.shape[-1])

    def conv_parts(project, masks_list):
        gate_in = project[..., :channels] * project[..., 2 * channels :]
        running = kernel[0] * gate_in
        for lag in range(1, kernel.shape[0]):
            running = running + kernel[lag] * delay_rows(gate_in, lag) * masks_list[lag - 1]
        return gate_in, running

    def conv_forward(full):
        project = by_row(mm("td,de->te", full, conv_in_w))
        unused, running = conv_parts(project, lag_masks(segments, kernel.shape[0]))
        mixed = (project[..., channels : 2 * channels] * running).astype(BF).reshape(-1, channels)
        return mm("te,ed->td", mixed, conv_out, BF), project.astype(BF), mixed

    def conv_backward(grad_full, project, mixed, full):
        masks_list = lag_masks(segments, kernel.shape[0])
        project = project.astype(F32)
        gate_in, running = conv_parts(project, masks_list)
        grad_mixed = by_row(mm("td,ed->te", grad_full, conv_out))
        grad_c = grad_mixed * running
        grad_run = grad_mixed * project[..., channels : 2 * channels]
        grad_in = kernel[0] * grad_run
        grad_kernel = [jnp.sum(grad_run * gate_in, axis=(0, 1))]
        for lag in range(1, kernel.shape[0]):
            mask = masks_list[lag - 1]
            grad_in = grad_in + kernel[lag] * advance_rows(grad_run * mask, lag)
            grad_kernel.append(jnp.sum(grad_run * mask * delay_rows(gate_in, lag), axis=(0, 1)))
        grad_low = jnp.concatenate(
            [grad_in * project[..., 2 * channels :], grad_c, grad_in * project[..., :channels]],
            axis=-1,
        )
        grad_low = grad_low.astype(BF).reshape(-1, 3 * channels)
        part = mm("te,de->td", grad_low, conv_in_w, BF)
        grad_cout = mm("te,td->ed", mixed, grad_full, BF)
        grad_cin = mm("td,te->de", full, grad_low, BF)
        taps = jnp.stack(grad_kernel).astype(BF)
        each = [grad_cin[:, i * channels : (i + 1) * channels] for i in range(3)]
        grad_cout = jnp.concatenate([grad_cout, jnp.pad(taps, ((0, 16 - taps.shape[0]), (0, width - channels)))])
        return part, each + [grad_cout]

    def by_kv(values, axis):
        shape = values.shape[:axis] + (kv_here, -1) + values.shape[axis + 1 :]
        return values.reshape(shape)

    def attn_setup():
        keyval = [by_kv(attn_keyval[:, i], 1) for i in range(2)]
        into = jnp.concatenate([by_kv(attn_query, 1)] + keyval, axis=2)
        used = into.shape[2]
        into = jnp.pad(into, ((0, 0), (0, 0), (0, padded(used) - used)))
        out = by_kv(attn_out, 0)
        used = out.shape[1]
        out = jnp.pad(out, ((0, 0), (0, padded(used) - used), (0, 0)))
        cosine, sine = rope_tables(segments, head_dim // 2)
        twice = lambda table: jnp.concatenate([table, table], axis=-1)
        return into.reshape(width, -1), out.reshape(-1, width), twice(cosine), twice(sine)

    def attn_forward(full, into, outof, cosine, sine):
        raw = by_row(mm("td,de->te", full, into))
        out, probs, totals, turned = attend_call(
            groups, head_dim, kv_here, raw, cosine, sine, segments, head_gains
        )
        flat = out.reshape(rows * seq, -1)
        return mm("te,ed->td", flat, outof, BF), raw, turned, probs, totals, out

    def attn_backward(grad_full, raw, turned, probs, totals, out, into, outof, cosine, sine):
        grad_out = by_row(mm("td,ed->te", grad_full, outof, BF))
        grad_raw, grad_gains = attend_back_call(
            groups,
            head_dim,
            kv_here,
            raw,
            turned,
            probs,
            totals,
            out,
            grad_out,
            cosine,
            sine,
            head_gains,
        )
        grad_raw = grad_raw.reshape(rows * seq, -1)
        return mm("te,de->td", grad_raw, into, BF), grad_raw, grad_gains

    def attn_weights(full, grad_raw, out, grad_full):
        grad_into = by_kv(mm("td,te->de", full, grad_raw, BF), 1)
        grad_out = by_kv(mm("te,td->ed", out.reshape(rows * seq, -1), grad_full, BF), 0)
        cut = groups * head_dim
        grad_keyval = [
            grad_into[:, :, cut + i * head_dim : cut + (i + 1) * head_dim].reshape(width, -1)
            for i in range(2)
        ]
        return (
            grad_into[:, :, :cut].reshape(attn_query.shape),
            jnp.stack(grad_keyval, axis=1),
            grad_out[:, :cut].reshape(attn_out.shape),
        )

    shards = dp if fused else 1

    def weights(full, grad_gu, grad_full, act):
        grad_up = sum(mm("tf,td->fd", one, two) for one, two in zip(grad_gu, full))
        grad_down = sum(mm("tf,td->fd", one, two) for one, two in zip(act, grad_full))
        return grad_up.reshape(2, -1, width)[:, :hidden], grad_down[:hidden]

    def choose(function, first_args, second_args):
        return lax.cond(
            is_first,
            lambda one, two: function(*one),
            lambda one, two: function(*two),
            first_args,
            second_args,
        )

    def gather_shards(home_tokens):
        return lax.all_gather(home_tokens, "dp", axis=0, tiled=True)

    def with_mate(mine, sections, *others):
        size = lax.axis_size("tensor")
        pairs = [p for one in sections for p in section_pairs(one, size, lambda i: i ^ 1)]
        mine = hold_call(mine, *others)
        return mine, lax.ppermute(mine, ("section", "tensor"), pairs)

    def after(values, *others):
        return lax.optimization_barrier((values, others))[0]

    start_home, start_full = begin(gains[0, 0])
    (part, project, mixed), setup = either(conv_forward, (start_full,), attn_setup, ())
    h1, full1, low1 = sum_norm(0, 1, part, start_home, gains[0, 1])
    if fused:
        all_a = gather_shards(low1)
    gu1, part = ffn_call(0, seq_local, full1, up_w, down_w)

    x2_home, z3 = hop(2, part, h1, gains[1, 0])
    unused, (part, *saved) = either(nothing, (), attn_forward, (z3,) + setup)
    h3, full2, low2 = sum_norm(1, 3, part, x2_home, gains[1, 1])
    if fused:
        all_b = gather_shards(low2)
    gu2 = ffn_call(1, seq_local, full2, up_w, None)

    *kept2, part = ffn_back_call(1, seq_local, shards, start_full, gu2, up_w, down_w)
    if fused:
        all_a = with_mate(all_a, (0, 1), gu2)
        kept2[0] = others_up_call(0, seq_local, dp, all_a[0], up_w, kept2[0])
        part = hold_call(part, kept2[0])
    gh3, gm3, gain_ffn2 = sum_back(1, 4, part, h3, start_home, gains[1, 1])
    if fused:
        kept2[1] = others_up_call(0, seq_local, dp, all_a[1], up_w, kept2[1], gm3)
        gm3 = hold_call(gm3, kept2[1])
    unused, (part, grad_raw, head_grads) = either(
        nothing, (), attn_backward, (gm3, *saved) + setup
    )
    g_home, g_full, gain_mix2 = hop_back(5, part, x2_home, gh3, gains[1, 0])
    if fused:
        all_c = gather_shards(tokens(g_home))

    *kept1, part = ffn_back_call(
        0, seq_local, shards, g_full, gu1, up_w, down_w, kept2 if fused else ()
    )
    part_out = down_call(1, seq_local, gu2, down_w, g_home)
    late = (hold_call(z3, part_out), grad_raw, saved[-1], gm3)
    unused, attn_grads = either(nothing, (), attn_weights, late)
    part = hold_call(part, attn_grads[0])
    if fused:
        all_b = with_mate(all_b, (1,), part_out)
        kept1[0] = others_up_call(1, seq_local, dp, all_b[0], up_w, kept1[0], attn_grads[0])
        part = hold_call(part, kept1[0])
    gh1, gm1, gain_ffn1 = sum_back(0, 6, part, h1, g_home, gains[0, 1])
    (part, conv_grads), unused = either(
        conv_backward, (gm1, project, mixed, start_full), nothing, ()
    )
    if fused:
        kept1[1] = others_up_call(1, seq_local, dp, all_b[1], up_w, kept1[1], gm1)
        part_out = hold_call(part_out, kept1[1])
    total = end(7, part, part_out)
    change, terms = norm_back(local.astype(F32), gains[0, 0], total)
    gain_mix1 = jnp.sum(terms, axis=(0, 1))
    boundary_out = jnp.where(is_first, pick(gh1, chip, 1) + change, pick(h3, chip, 1) + total)[None]

    if fused:
        all_c = with_mate(all_c, (0,), total)
        for half in range(2):
            kept1[half], kept1[2 + half] = others_back_call(
                seq_local,
                dp,
                all_c[half],
                all_a[half],
                down_w,
                kept1[half],
                kept1[2 + half],
            )
        grad_up, grad_down = choose(
            weights,
            (all_a, kept1[:2], all_c, kept1[2:]),
            (all_b, kept1[:2], all_a, kept1[2:]),
        )
    else:
        grad_up, grad_down = choose(
            weights,
            ((full1,), kept1[:1], (g_full,), kept1[1:]),
            ((full2,), kept2[:1], (start_full,), kept2[1:]),
        )
        grad_up, grad_down = lax.psum((grad_up.astype(BF), grad_down.astype(BF)), "dp")
    full_gu = grad_up.astype(F32).transpose(2, 0, 1)[None]
    full_down = grad_down.astype(F32).T[None]

    zero = jnp.zeros_like(gain_mix1)
    first_gains = jnp.concatenate([gain_mix1, gain_ffn1, zero, zero])
    second_gains = jnp.concatenate([zero, zero, gain_mix2, gain_ffn2])
    small = jnp.concatenate([jnp.where(is_first, first_gains, second_gains), head_grads.reshape(-1)])
    if fused:
        small = total_call(11, hold_call(small.reshape(1, -1), grad_down))[0]
    else:
        small = lax.psum(small, ("section", "tensor", "dp"))
    mixer_sums = lax.psum(tuple(conv_grads) + tuple(attn_grads), ("section", "dp"))
    mixer_sums = [hold_call(v, small) for v in mixer_sums]
    *sum_cin, sum_cout, sum_aq, sum_akv, sum_aout = [v.astype(F32) for v in mixer_sums]
    sum_kernel = sum_cout[channels : channels + conv_kernel.shape[0], :channels]
    sum_cin = jnp.stack(sum_cin).transpose(1, 0, 2)
    sum_cout = sum_cout[:channels]

    cut = 4 * width
    return (
        boundary_out,
        small[:cut].reshape(norm_gains.shape),
        small[cut:].reshape(qk_gains.shape),
        sum_cin,
        sum_kernel,
        sum_cout,
        sum_aq,
        sum_akv,
        sum_aout,
        full_gu,
        full_down,
    )


def solution(mesh):
    placed = (
        P("section", "dp", "tensor", None),
        P("dp", None),
        P(),
        P(),
        P(None, None, "tensor"),
        P(None, "tensor"),
        P("tensor", None),
        P(None, "tensor"),
        P(None, None, "tensor"),
        P("tensor", None),
        P("section", None, None, "tensor"),
        P("section", None, "tensor"),
    )
    def within(*args):
        with jax.sharding.use_abstract_mesh(mesh.abstract_mesh):
            return mapped(*args)

    mapped = jax.shard_map(
        on_device,
        mesh=mesh,
        in_specs=placed,
        out_specs=(
            P("section", "dp", "tensor", None),
            P(),
            P(),
            P(None, None, "tensor"),
            P(None, "tensor"),
            P("tensor", None),
            P(None, "tensor"),
            P(None, None, "tensor"),
            P("tensor", None),
            P("section", None, None, "tensor"),
            P("section", None, "tensor"),
        ),
        check_vma=False,
    )
    return within
```

time: 2020 us -> 1190 us (0.59)
  waiting for transfers between devices: 552 us -> 14.7 us
  matrix products: 304 us -> 223 us
  blocking collectives: 62.6 us -> 0 us
  other arithmetic: 117 us -> 55.2 us
  local copies, waits for them, and re-layouts: 117 us -> 80.3 us
  Pallas kernels: 810 us -> 779 us
    psum x2 -> x1, waiting for transfers between devices: 552 us -> 0.01 us  [on_device(): lax.psum(tuple(conv_grads) + tuple(attn_grads), ('section', 'dp'))]
    pallas_call x8 -> x9, Pallas kernels: 810 us -> 524 us  [comm_call(): pl.pallas_call(kernel, name=name, out_shape=outs, in_specs=[pl.BlockSpec(...]
    pallas_call x0 -> x28, Pallas kernels: none -> 255 us  [the longest x11 255 us: ffn_pallas(): pl.pallas_call(kernel, name=name, out_shape=tuple((jax.ShapeDtypeStruct(s...]
    dot_general x20 -> x10, matrix products: 304 us -> 223 us  [mm(): jnp.einsum(spec, left, right, preferred_element_type=F32).astype(kind)]
    psum x2 -> x0, blocking collectives: 62.6 us -> none  [the longest x1 42.5 us: on_device(): lax.psum((grad_gains, head_grads), ('section', 'tensor', 'dp'))]
    select_n x2 -> x0, local copies, waits for them, and re-layouts: 27.3 us -> none  [weave(): jnp.where(core == 0, jnp.stack([mine, other], axis=2), jnp.stack([other,...]
    concatenate x2, other arithmetic: 24.7 us -> 1.12 us  [the longest x1 1.11 us: conv_backward(): jnp.concatenate([grad_cout, jnp.pad(taps, ((0, 16 - taps.shape[0]), (0, w...]
    slice x0 -> x6, local copies, waits for them, and re-layouts: none -> 22.5 us  [the longest x1 16.2 us: weights(): return (grad_up.reshape(2, -1, width)[:, :hidden], grad_down[:hidden])]
  transfers between devices with their start and end apart: 2 -> 7, of which waited for: 2 -> 1; matrix products, arithmetic and copies ran while one was open for 7% -> 25% of each run, Pallas kernels for 2% -> 57%
where the time goes in v3:
time: 1190 us; the launch traced here: 1180 us
  Pallas kernels  779 us (65%)
  matrix products  223 us (19%)
  local copies, waits for them, and re-layouts  80.3 us (7%)
  other arithmetic  55.2 us (5%)
  waiting for transfers between devices  14.7 us (1%)
  between operations  14.6 us (1%)
    pallas_call x9, Pallas kernels, comm_call(): pl.pallas_call(kernel, name=name, out_shape=outs, in_specs=[pl.BlockSpec(...  524 us
    pallas_call x11, Pallas kernels, ffn_pallas(): pl.pallas_call(kernel, name=name, out_shape=tuple((jax.ShapeDtypeStruct(s...  255 us
    dot_general x10, matrix products, mm(): jnp.einsum(spec, left, right, preferred_element_type=F32).astype(kind)  223 us
    another operation x17, local copies, waits for them, and re-layouts, within(): return mapped(*args)  31.7 us
  transfers between devices with their start and end apart: 7, of which 1 were waited for; matrix products, arithmetic and copies ran while one was open for 25% of the time, Pallas kernels for 57%

profile of v3, /device:TPU:0, one launch (start us, length us, event | category | flops | bytes accessed | tf_op | source)
XLA Modules:
  0.0 1183.4 jit_solution(9319426047513326823)
XLA Ops:
  9.2 6.2 copy.80
  15.4 44.7 %start.1 = (bf16[1024,1536]{1,0:T(8,128)(2,1)}, bf16[2048,1536]{1,0:T(8,128)(2,1)}) custom-call(bf16[512,1536]{1,0:T(8,128)(2,1)} %bitcast.134, f32[1,1536]{1,0:T(1,128)} %get-tuple-element.406.gain), custom_call_target="tpu_custom_call" | custom-call | bytes 171600000 | tf_op jit(solution)/shard_map/start/pallas_call | solution.py:139
  60.1 28.2 %conditional.6 = (bf16[2048,1536]{1,0:T(8,128)(2,1)}, bf16[2,1024,1152]{2,1,0:T(8,128)(2,1)}, bf16[2048,384]{1,0:T(8,128)(2,1)}, bf16[1536,768]{1,0:T(8,128)(2,1...) conditional(s32[]{:T(128)} %convert_element_type.123, ...), branch_computations={%region_0.2_spmd, %region_2.3_spmd} | conditional | flops 9677053952 | bytes 69523032 | solution.py:1276
  60.7 11.5 fusion.48
  72.6 2.3 fusion.10
  74.9 6.7 convolution_convert_fusion.5
  81.6 2.8 convert_element_type.100
  84.4 1.6 broadcast.150
  88.3 54.8 %sum_norm.2 = (f32[1024,1536]{1,0:T(8,128)}, bf16[2048,1536]{1,0:T(8,128)(2,1)}, bf16[1024,1536]{1,0:T(8,128)(2,1)}) custom-call(bf16[2048,1536]{1,0:T(8,128)(2,1)} %get-tuple-element.244.refs_0_, bf16[1024,1536]{1,0:T(8,128)(2,1)} %get-tuple-element.245.refs_1_.refs_2_, f32[1,1536]{1,0:T(1,128)} %get-tuple-element.405.refs_2_.refs_3_), custom_call_target="tpu_custom_call" | custom-call | bytes 171600000 | tf_op jit(solution)/shard_map/sum_norm/pallas_call | solution.py:139
  143.8 44.6 %ffn.1 = (bf16[2048,3584]{1,0:T(8,128)(2,1)}, bf16[2048,1536]{1,0:T(8,128)(2,1)}) custom-call(bf16[2048,1536]{1,0:T(8,128)(2,1)} %get-tuple-element.246.refs_0_, bf16[2,1728,1536]{2,1,0:T(8,128)(2,1)} %bitcast.110, bf16[1728,1536]{1,0:T(8,128)(2,1)} %bitcast.118), custom_call_target="tpu_custom_call" | custom-call | bytes 145200000 | tf_op jit(solution)/shard_map/ffn/pallas_call | solution.py:763
  188.4 50.6 %hop.1 = (bf16[1024,1536]{1,0:T(8,128)(2,1)}, bf16[2048,1536]{1,0:T(8,128)(2,1)}) custom-call(bf16[2048,1536]{1,0:T(8,128)(2,1)} %get-tuple-element.247.refs_0_, f32[1024,1536]{1,0:T(8,128)} %get-tuple-element.248.refs_1_, f32[1,1536]{1,0:T(1,128)} %get-tuple-element.404.refs_2_.refs_3_.refs_4_), custom_call_target="tpu_custom_call" | custom-call | bytes 171600000 | tf_op jit(solution)/shard_map/hop/pallas_call | solution.py:139
  239.0 21.7 %conditional.7 = (bf16[2048,1536]{1,0:T(8,128)(2,1)}, f32[2,1024,768]{2,1,0:T(8,128)}, bf16[2,1024,768]{2,1,0:T(8,128)(2,1)}, bf16[2,2,3,1024,1024]{4,3,2,1,0:T(...) conditional(s32[]{:T(128)} %convert_element_type.123, (bf16[2048,1536]{1,0:T(8,128)(2,1)}, ...), branch_computations={%region_3.4_spmd, %region_4.5_spmd} | conditional | flops 8056209408 | bytes 114036496 | solution.py:1276
  239.2 8.7 broadcast.156
  247.9 3.1 broadcast.153
  251.0 3.1 broadcast.154
  254.1 3.3 broadcast.157
  257.4 1.9 broadcast.155
  260.7 85.9 %sum_norm.3 = (f32[1024,1536]{1,0:T(8,128)}, bf16[2048,1536]{1,0:T(8,128)(2,1)}, bf16[1024,1536]{1,0:T(8,128)(2,1)}) custom-call(bf16[2048,1536]{1,0:T(8,128)(2,1)} %get-tuple-element.254.refs_0_, bf16[1024,1536]{1,0:T(8,128)(2,1)} %get-tuple-element.255.refs_1_, f32[1,1536]{1,0:T(1,128)} %get-tuple-element.403.refs_2_.refs_3_), custom_call_target="tpu_custom_call" | custom-call | bytes 171600000 | tf_op jit(solution)/shard_map/sum_norm/pallas_call | solution.py:139
  346.8 14.6 %all-gather.4.cloned.1.call-done.refs_0_ = bf16[4096,1536]{1,0:T(8,128)(2,1)} async-done(((bf16[1024,1536]{1,0:T(8,128)(2,1)}), bf16[4096,1536]{1,0:T(8,128)(2,1)}) %all-gather.4.cloned.1.call-update) | async-done | bytes 12582928 | tf_op jit(solution)/shard_map/all_gather | solution.py:1403
  361.5 43.7 %others_up.4.refs_1_.refs_4_ = bf16[4096,3584]{1,0:T(8,128)(2,1)} custom-call(bf16[4096,1536]{1,0:T(8,128)(2,1)} %hold.17.source.second, bf16[2,1728,1536]{2,1,0:T(8,128)(2,1)} %bitcast.113, bf16[4096,3584]{1,0:T(8,128)(2,1)} %get-tuple-element.259.refs_0_), custom_call_target="tpu_custom_call", output_to_operand_aliasing={{}: (2, {})} | custom-call | bytes 138600000 | tf_op jit(solution)/shard_map/others_up/pallas_call | solution.py:763
  405.2 80.3 %sum_back.2 = (f32[1024,1536]{1,0:T(8,128)}, bf16[2048,1536]{1,0:T(8,128)(2,1)}, f32[1,1536]{1,0:T(1,128)}) custom-call(bf16[2048,1536]{1,0:T(8,128)(2,1)} %hold.18.refs_0_, f32[1024,1536]{1,0:T(8,128)} %get-tuple-element.260.refs_1_, bf16[1024,1536]{1,0:T(8,128)(2,1)} %get-tuple-element.245.refs_1_.refs_2_, f32[1,1536]{1,0:T(1,128)} %get-tuple-element.403.refs_2_.refs_3_), custom_call_target="tpu_custom_call" | custom-call | bytes 171600000 | tf_op jit(solution)/shard_map/sum_back/pallas_call | solution.py:139
  485.5 43.6 %others_up.5.refs_1_.refs_5_ = bf16[4096,3584]{1,0:T(8,128)(2,1)} custom-call(bf16[4096,1536]{1,0:T(8,128)(2,1)} %collective-permute-done.source.second, bf16[2,1728,1536]{2,1,0:T(8,128)(2,1)} %bitcast.114, bf16[4096,3584]{1,0:T(8,128)(2,1)} %get-tuple-element.262.refs_0_, ...), custom_call_target="tpu_custom_call", output_to_operand_aliasing={{}: (2, {})} | custom-call | bytes 138600000 | tf_op jit(solution)/shard_map/others_up/pallas_call | solution.py:763
  529.1 5.4 conditional.8
  529.5 3.1 broadcast.159
  532.6 1.9 broadcast.160
  534.5 74.6 %hop_back.1 = (bf16[1024,1536]{1,0:T(8,128)(2,1)}, bf16[2048,1536]{1,0:T(8,128)(2,1)}, f32[1,1536]{1,0:T(1,128)}) custom-call(bf16[2048,1536]{1,0:T(8,128)(2,1)} %get-tuple-element.268.refs_0_, bf16[1024,1536]{1,0:T(8,128)(2,1)} %get-tuple-element.255.refs_1_, f32[1024,1536]{1,0:T(8,128)} %get-tuple-element.269.refs_2_, ...), custom_call_target="tpu_custom_call" | custom-call | bytes 171600000 | tf_op jit(solution)/shard_map/hop_back/pallas_call | solution.py:139
  609.3 5.2 collective-permute-start.1
  614.5 2.3 copy-done.24
  618.2 53.0 %ffn_back.3 = (bf16[4096,3584]{1,0:T(8,128)(2,1)}, bf16[4096,3584]{1,0:T(8,128)(2,1)}, bf16[4096,1792]{1,0:T(8,128)(2,1)}, bf16[4096,1792]{1,0:T(8,128)(2,1)}, bf16[2048,1536]{1,0:T(8,128)(2,1)}) custom-call(bf16[2048,1536]{1,0:T(8,128)(2,1)} %get-tuple-element.270.refs_0_, ...), custom_call_target="tpu_custom_call", output_to_operand_aliasing={{0}: (4, {}), {1}: (5, {}), {2}: (6, {}), {3}: (7, {})} | custom-call | bytes 158400000 | tf_op jit(solution)/shard_map/ffn_back/pallas_call | solution.py:763
  671.2 71.9 %sum_back.3 = (f32[1024,1536]{1,0:T(8,128)}, bf16[2048,1536]{1,0:T(8,128)(2,1)}, f32[1,1536]{1,0:T(1,128)}) custom-call(bf16[2048,1536]{1,0:T(8,128)(2,1)} %hold.23.refs_0_, f32[1024,1536]{1,0:T(8,128)} %get-tuple-element.248.refs_1_, bf16[1024,1536]{1,0:T(8,128)(2,1)} %get-tuple-element.275.refs_2_, f32[1,1536]{1,0:T(1,128)} %get-tuple-element.405.refs_2_.refs_3_), custom_call_target="tpu_custom_call" | custom-call | bytes 171600000 | tf_op jit(solution)/shard_map/sum_back/pallas_call | solution.py:139
  743.1 51.3 %conditional.10 = (bf16[2048,1536]{1,0:T(8,128)(2,1)}, bf16[1536,384]{0,1:T(8,128)(2,1)}, bf16[1536,384]{0,1:T(8,128)(2,1)}, bf16[1536,384]{0,1:T(8,128)(2,1)}, bf16[400,1536]{1,0:T(8,128)(2,1)}) conditional(s32[]{:T(128)} %convert_element_type.123, () %tuple.64, (f32[3,384]{1,0:T(4,128)S(1)}, bf16[2048,1536]{1,0:T(8,128)(2,1)}, ...), branch_computations={%region_10.11_spmd, %region_11.15_spmd} | conditional | flops 19388383232 | bytes 179522720 | solution.py:1276
  743.2 3.0 convert_element_type.106
  746.5 2.5 copy-done.5
  749.0 5.1 fusion.49
  754.2 5.3 multiply_reduce_fusion.2
  759.5 6.0 convolution_convert_fusion.8
  766.6 2.3 multiply_convert_fusion.2
  770.8 9.9 fusion.13
  780.7 1.9 fusion.40
  784.0 10.1 convolution_convert_fusion.7
  794.5 40.7 %end.1 = f32[512,1536]{1,0:T(8,128)} custom-call(bf16[2048,1536]{1,0:T(8,128)(2,1)} %get-tuple-element.284.first, bf16[2048,1536]{1,0:T(8,128)(2,1)} %hold.24.second), custom_call_target="tpu_custom_call" | custom-call | bytes 171600000 | tf_op jit(solution)/shard_map/end/pallas_call | solution.py:139
  835.2 1.9 collective-permute-start.2
  837.1 2.4 copy.87
  839.6 2.4 copy.88
  842.0 2.4 copy.89
  844.3 1.8 copy.91
  846.2 1.9 fusion.29
  848.6 2.3 multiply_reduce_fusion.3
  851.5 6.8 fusion.34
  858.3 34.9 %others_back.2 = (bf16[4096,3584]{1,0:T(8,128)(2,1)}, bf16[4096,1792]{1,0:T(8,128)(2,1)}) custom-call(bf16[4096,1536]{1,0:T(8,128)(2,1)} %hold.25.first, bf16[4096,1536]{1,0:T(8,128)(2,1)} %hold.17.source.second, bf16[1728,1536]{1,0:T(8,128)(2,1)} %bitcast.122, ...), custom_call_target="tpu_custom_call", output_to_operand_aliasing={{0}: (3, {}), {1}: (4, {})} | custom-call | bytes 105600000 | tf_op jit(solution)/shard_map/others_back/pallas_call | solution.py:763
  893.2 35.4 %others_back.3 = (bf16[4096,3584]{1,0:T(8,128)(2,1)}, bf16[4096,1792]{1,0:T(8,128)(2,1)}) custom-call(bf16[4096,1536]{1,0:T(8,128)(2,1)} %collective-permute-done.2.first, bf16[4096,1536]{1,0:T(8,128)(2,1)} %collective-permute-done.source.second, bf16[1728,1536]{1,0:T(8,128)(2,1)} %bitcast.123, ...), custom_call_target="tpu_custom_call", output_to_operand_aliasing={{0}: (3, {}), {1}: (4, {})} | custom-call | bytes 105600000 | tf_op jit(solution)/shard_map/others_back/pallas_call | solution.py:763
  928.6 206.9 %conditional.11 = (f32[2,1728,1536]{2,1,0:T(8,128)}, f32[1728,1536]{1,0:T(8,128)}) conditional(s32[]{:T(128)} %convert_element_type.123, (bf16[4096,3584]{1,0:T(8,128)(2,1)}, bf16[4096,1536]{1,0:T(8,128)(2,1)}, bf16[4096,3584]{1,0:T(8,128)(2,1)}, bf16[4096,1536]{1,0:T(8,128)(2,1)}, bf16[4096,1792]{1,0:T(8,128)(2,1)}, ...), branch_computations={%region_17.18_spmd, %region_18.19_spmd} | conditional | flops 135299629056 | bytes 388890816 | solution.py:1394
  936.0 56.1 %fusion.45 = f32[3584,1536]{1,0:T(8,128)} fusion(bf16[4096,3584]{1,0:T(8,128)(2,1)} %get-tuple-element.163, bf16[4096,1536]{1,0:T(8,128)(2,1)} %get-tuple-element.164), kind=kOutput, calls=%fused_computation.119 | convolution fusion | flops 45097156608 | bytes 63963136 | tf_op jit(solution)/shard_map/cond/branch_1_fun/tf,td->fd/dot_general | solution.py:21
  992.1 56.5 %convolution_add_fusion.1 = f32[3584,1536]{1,0:T(8,128)} fusion(f32[3584,1536]{1,0:T(8,128)} %fusion.45, bf16[4096,3584]{1,0:T(8,128)(2,1)} %get-tuple-element.165, bf16[4096,1536]{1,0:T(8,128)(2,1)} %get-tuple-element.166), kind=kOutput, calls=%fused_computation.21 | convolution fusion | flops 45102661632 | bytes 85983232 | tf_op jit(solution)/shard_map/cond/branch_1_fun/tf,td->fd/dot_general | solution.py:21
  1048.6 16.2 %slice.159 = f32[2,1728,1536]{2,1,0:T(8,128)} slice(f32[2,1792,1536]{2,1,0:T(8,128)} %bitcast.136), slice={[0:2], [0:1728], [0:1536]} | slice | bytes 42467328 | tf_op jit(solution)/shard_map/cond/branch_1_fun/slice | solution.py:1391
  1064.9 28.6 %fusion.46 = f32[1792,1536]{1,0:T(8,128)} fusion(bf16[4096,1792]{1,0:T(8,128)(2,1)S(1)} %bitcast.127, bf16[4096,1536]{1,0:T(8,128)(2,1)} %get-tuple-element.168), kind=kOutput, calls=%fused_computation.120 | convolution fusion | flops 22548578304 | bytes 38273024 | tf_op jit(solution)/shard_map/cond/branch_1_fun/tf,td->fd/dot_general | solution.py:21
  1093.5 32.1 %fusion.47 = f32[1792,1536]{1,0:T(8,128)} fusion(bf16[4096,1792]{1,0:T(8,128)(2,1)} %get-tuple-element.169, bf16[4096,1536]{1,0:T(8,128)(2,1)} %get-tuple-element.170), kind=kOutput, calls=%fused_computation.121 | convolution fusion | flops 22548578304 | bytes 38273024 | tf_op jit(solution)/shard_map/cond/branch_1_fun/tf,td->fd/dot_general | solution.py:21
  1125.6 9.7 slice_add_fusion.1
  1135.5 20.7 %total.1 = f32[1,6272]{1,0:T(1,128)} custom-call(f32[1,6272]{1,0:T(1,128)} %hold.26.values), custom_call_target="tpu_custom_call" | custom-call | bytes 171600000 | tf_op jit(solution)/shard_map/total/pallas_call | solution.py:139
  1157.7 3.0 slice.176
  1162.0 3.0 convert_element_type.132
  1165.0 2.4 convert_element_type.131
  1167.4 2.8 convert_element_type.130
  1171.9 4.8 convert_bitcast_fusion
  (145 shorter events, 20.2 us)
Async XLA Ops:
  7.2 354.3 %all-gather.4.cloned.1.call-start = ((), (), s32[]{:S(2)}) async-start(), calls=%async_computation | async-start | bytes 15728640 | tf_op jit(solution)/shard_map/all_gather | solution.py:1403
  9.2 6.2 copy-start.23
  9.2 50.9 %copy-start.13 = (bf16[1536,384]{1,0:T(8,128)(2,1)S(1)}, bf16[1536,384]{1,0:T(8,128)(2,1)}, u32[]{:S(2)}) copy-start(bf16[1536,384]{1,0:T(8,128)(2,1)} %param.31) | copy-start | bytes 3538948
  9.2 50.9 %copy-start.14 = (s32[2,1024]{1,0:T(2,128)S(1)}, s32[2,1024]{1,0:T(2,128)}, u32[]{:S(2)}) copy-start(s32[2,1024]{1,0:T(2,128)} %param.25) | copy-start | bytes 24580
  15.4 44.7 %copy-start.18 = (f32[3,384]{1,0:T(4,128)}, f32[3,384]{1,0:T(4,128)S(1)}, u32[]{:S(2)}) copy-start(f32[3,384]{1,0:T(4,128)S(1)} %convert_element_type.125) | copy-start | bytes 13828
  72.6 2.3 copy-start.26
  143.1 0.7 copy-start.29
  143.2 466.1 %all-gather.6.cloned.1.call-start = ((), (), s32[]{:S(2)}) async-start(), calls=%async_computation.1 | async-start | bytes 15728640 | tf_op jit(solution)/shard_map/all_gather | solution.py:1403
  188.4 50.6 %copy-start.4 = (f32[2,1024,64]{2,1,0:T(8,128)S(1)}, f32[2,1024,64]{2,1,0:T(8,128)}, u32[]{:S(2)}) copy-start(f32[2,1024,64]{2,1,0:T(8,128)} %get-tuple-element.252) | copy-start | bytes 1572868
  346.7 488.5 %all-gather.8.cloned.1.call-start = ((), (), s32[]{:S(2)}) async-start(), calls=%async_computation.2 | async-start | bytes 15728640 | tf_op jit(solution)/shard_map/all_gather | solution.py:1403
  361.4 124.1 %collective-permute-start = (bf16[4096,1536]{1,0:T(8,128)(2,1)}, bf16[4096,1536]{1,0:T(8,128)(2,1)}, u32[]{:S(2)}, u32[]{:S(2)}) collective-permute-start(bf16[4096,1536]{1,0:T(8,128)(2,1)} %hold.17.source.second), channel_id=1, source_target_pairs={{0,4},{4,0},{8,12},{12,8},{16,20},{20,16},{24,28},{28,24},{1,5},{5... | collective-permute-start | bytes 37748744 | tf_op jit(solution)/shard_map/ppermute | solution.py:1409
  534.5 74.6 %copy-start.27 = (f32[2,64]{1,0:T(2,128)}, f32[2,64]{1,0:T(2,128)S(1)}, u32[]{:S(2)}) copy-start(f32[2,64]{1,0:T(2,128)S(1)} %get-tuple-element.289) | copy-start | bytes 1540
  609.1 548.5 %all-reduce.16.cloned.1.call-start = ((), (), s32[]{:S(2)}) async-start(), calls=%async_computation.3 | async-start | bytes 15826944 | tf_op jit(solution)/shard_map/psum | solution.py:1502
  609.3 185.1 %collective-permute-start.1 = (bf16[4096,1536]{1,0:T(8,128)(2,1)}, bf16[4096,1536]{1,0:T(8,128)(2,1)}, u32[]{:S(2)}, u32[]{:S(2)}) collective-permute-start(bf16[4096,1536]{1,0:T(8,128)(2,1)} %hold.22.source), channel_id=1, source_target_pairs={{16,20},{20,16},{24,28},{28,24},{17,21},{21,17},{25,29},{29,25},{1... | collective-permute-start | bytes 37748744 | tf_op jit(solution)/shard_map/ppermute | solution.py:1409
  614.5 2.3 copy-start.24
  618.1 53.0 %copy-start.9 = (bf16[1536,2,128]{0,2,1:T(8,128)(2,1)}, bf16[1536,2,128]{0,2,1:T(8,128)(2,1)S(1)}, u32[]{:S(2)}) copy-start(bf16[1536,2,128]{0,2,1:T(8,128)(2,1)S(1)} %get-tuple-element.301) | copy-start | bytes 2359300
  618.1 53.0 %copy-start.1 = (bf16[1536,384]{1,0:T(8,128)(2,1)}, bf16[1536,384]{1,0:T(8,128)(2,1)S(1)}, u32[]{:S(2)}) copy-start(bf16[1536,384]{1,0:T(8,128)(2,1)S(1)} %get-tuple-element.362.refs_1_) | copy-start | bytes 3538948
  671.2 71.9 %copy-start.15 = (s32[2,1024]{1,0:T(2,128)S(1)}, s32[2,1024]{1,0:T(2,128)}, u32[]{:S(2)}) copy-start(s32[2,1024]{1,0:T(2,128)} %param.25) | copy-start | bytes 24580
  671.2 71.9 %copy-start.19 = (f32[3,384]{1,0:T(4,128)S(1)}, f32[3,384]{1,0:T(4,128)}, u32[]{:S(2)}) copy-start(f32[3,384]{1,0:T(4,128)} %copy-done.18) | copy-start | bytes 13828
  671.2 71.9 %copy-start.25 = (bf16[384,1536]{1,0:T(8,128)(2,1)S(1)}, bf16[384,1536]{1,0:T(8,128)(2,1)}, u32[]{:S(2)}) copy-start(bf16[384,1536]{1,0:T(8,128)(2,1)} %param.30) | copy-start | bytes 3538948
  746.2 2.8 copy-start.5
  768.9 1.4 copy-start.11
  768.9 1.9 copy-start.12
  780.7 3.3 copy-start.8
  835.2 58.0 %collective-permute-start.2 = (bf16[4096,1536]{1,0:T(8,128)(2,1)}, bf16[4096,1536]{1,0:T(8,128)(2,1)}, u32[]{:S(2)}, u32[]{:S(2)}) collective-permute-start(bf16[4096,1536]{1,0:T(8,128)(2,1)} %hold.25.first), channel_id=1, source_target_pairs={{0,4},{4,0},{8,12},{12,8},{1,5},{5,1},{9,13},{13,9},{2,6},{6,2},{1... | collective-permute-start | bytes 37748744 | tf_op jit(solution)/shard_map/ppermute | solution.py:1409
  837.1 7.2 copy-start.10
  846.1 2.0 copy-start.20
  846.1 2.1 copy-start.22
  846.1 2.1 copy-start.21
  846.1 2.2 copy-start.28
  846.1 2.4 copy-start
  846.2 2.4 copy-start.17
  936.0 128.9 %slice-start.3 = ((s8[14680064]{0:T(1024)(128)(4,1)}), s8[2097152]{0:T(1024)(128)(4,1)S(1)}, s32[]{:S(2)}) async-start(s8[14680064]{0:T(1024)(128)(4,1)} %bitcast.126), calls=%async_computation.7 | async-start | bytes 4194304 | tf_op jit(solution)/shard_map/cond
  936.0 128.9 %slice-start.4 = ((s8[14680064]{0:T(1024)(128)(4,1)}), s8[4194304]{0:T(1024)(128)(4,1)S(1)}, s32[]{:S(2)}) async-start(s8[14680064]{0:T(1024)(128)(4,1)} %bitcast.126), calls=%async_computation.8 | async-start | bytes 8388608 | tf_op jit(solution)/shard_map/cond
  992.1 72.8 %slice-start.5 = ((s8[14680064]{0:T(1024)(128)(4,1)}), s8[4194304]{0:T(1024)(128)(4,1)S(1)}, s32[]{:S(2)}) async-start(s8[14680064]{0:T(1024)(128)(4,1)} %bitcast.126), calls=%async_computation.9 | async-start | bytes 8388608 | tf_op jit(solution)/shard_map/cond
  992.1 72.8 %slice-start.6 = ((s8[14680064]{0:T(1024)(128)(4,1)}), s8[4194304]{0:T(1024)(128)(4,1)S(1)}, s32[]{:S(2)}) async-start(s8[14680064]{0:T(1024)(128)(4,1)} %bitcast.126), calls=%async_computation.10 | async-start | bytes 8388608 | tf_op jit(solution)/shard_map/cond
  1093.5 32.1 %copy-start.3 = (f32[1792,1536]{1,0:T(8,128)S(1)}, f32[1792,1536]{1,0:T(8,128)}, u32[]{:S(2)}) copy-start(f32[1792,1536]{1,0:T(8,128)} %fusion.46) | copy-start | bytes 33030148 | tf_op jit(solution)/shard_map/cond
  1157.7 4.3 copy-start.16
  1170.2 1.3 copy-start.7
  1170.2 1.6 copy-start.6
Sparse Core Ops, SparseCore 0:
  143.3 218.1 all-gather.3
  363.0 216.3 all-gather.5
  609.3 217.8 all-gather.7
  846.3 262.1 all-reduce.15

commit v4 on v3

--- a/solution.py
+++ b/solution.py
@@ -15,6 +15,7 @@
 MESH = pl.DeviceIdType.MESH
 TILE = 64
 VMEM_BYTES = 60 * 1024 * 1024
+WEIGHT_BYTES = 62 * 1024 * 1024
 
 
 def mm(spec, left, right, kind=F32):
@@ -135,13 +136,15 @@
     return scale * (weighted - normed * inner), grad * normed
 
 
-def comm_call(kernel, name, number, inputs, outs, scratch, where, micros=52):
+def comm_call(kernel, name, number, inputs, outs, scratch, where, micros=52, to=None):
     return pl.pallas_call(
         kernel,
         name=name,
         out_shape=outs,
         in_specs=[pl.BlockSpec(memory_space=space) for space in where],
-        out_specs=tuple(pl.BlockSpec(memory_space=pltpu.VMEM) for unused in outs),
+        out_specs=tuple(
+            pl.BlockSpec(memory_space=space) for space in to or [pltpu.VMEM] * len(outs)
+        ),
         scratch_shapes=scratch,
         cost_estimate=estimate(micros),
         compiler_params=pltpu.CompilerParams(
@@ -157,14 +160,22 @@
 
 def sum_tiles(active, backward, per_chip, *refs):
     if backward:
-        part, hidden, grad, gain, out, full, gain_out = refs[:7]
+        part, gain, hidden_in, grad_in, out_to, full, gain_out = refs[:7]
+        hidden, grad = refs[7:9]
+        loads = [(hidden_in, hidden), (grad_in, grad)]
+        scratch = refs[9:]
+    else:
+        part, gain, residual_in, out_to, full, home_low = refs[:6]
+        residual = refs[6]
+        loads = [(residual_in, residual)]
         scratch = refs[7:]
-    else:
-        part, residual, gain, out, full, home_low = refs[:6]
-        scratch = refs[6:]
-    mine, from_mate, summed, from_chip, relayed = scratch[:5]
-    own_s, mate_s, mate_r, chip_s, chip_r, relay_s, relay_r, low_s, low_r = scratch[5:]
+    out, low, mine, from_mate, summed, from_chip, relayed = scratch[:7]
+    own_s, mate_s, mate_r, chip_s, chip_r, relay_s, relay_r, low_s, low_r = scratch[7:16]
+    load_s, out_s, full_s, home_s = scratch[16:]
     peers = Peers()
+    loads = [
+        pltpu.make_async_copy(one, two, load_s.at[k]) for k, (one, two) in enumerate(loads)
+    ]
     count = mine.shape[0] // TILE
     pairs = count // 2
 
@@ -202,16 +213,29 @@
         )
 
     def low_copy(i):
-        rows = own_rows(i)
-        return remote(full.at[rows], full.at[rows], low_s.at[i], low_r.at[i], peers.mate)
+        source = low.at[tile_rows(i)]
+        return remote(source, full.at[own_rows(i)], low_s.at[i], low_r.at[i], peers.mate)
+
+    def stores(i):
+        rows = tile_rows(i)
+        copies = [
+            pltpu.make_async_copy(out.at[rows], out_to.at[rows], out_s.at[i]),
+            pltpu.make_async_copy(low.at[rows], full.at[own_rows(i)], full_s.at[i]),
+        ]
+        if not backward:
+            copies.append(pltpu.make_async_copy(low.at[rows], home_low.at[rows], home_s.at[i]))
+        return copies
 
     def low_wait(i):
         rows = tile_rows(full_tile(i, 1 - peers.core, per_chip))
-        remote(full.at[rows], full.at[rows], low_s.at[i], low_r.at[i], peers.mate).wait_recv()
+        source = low.at[tile_rows(i)]
+        remote(source, full.at[rows], low_s.at[i], low_r.at[i], peers.mate).wait_recv()
 
     @pl.when(peers.section == active)
     def work():
         loop(count, lambda i: own_copy(i).start())
+        for copy in loads:
+            copy.start()
         greet([peers.mate, peers.beside, peers.across], 3)
         loop(count, lambda i: mate_copy(i).start())
 
@@ -230,6 +254,8 @@
                     direct(i).start()
 
         loop(pairs, first)
+        for copy in loads:
+            copy.wait()
         if backward:
             gain_out[...] = jnp.zeros_like(gain_out)
 
@@ -248,10 +274,10 @@
                 result = residual[rows, :].astype(F32) + total
                 lower = (result * rms_tile(result) * gain[...]).astype(BF)
             out[rows, :] = result
-            full[own_rows(i), :] = lower
-            if not backward:
-                home_low[rows, :] = lower
+            low[rows, :] = lower
             low_copy(i).start()
+            for copy in stores(i):
+                copy.start()
 
         loop(count, second)
 
@@ -260,6 +286,8 @@
             direct(i).wait_send()
             low_copy(i).wait_send()
             low_wait(i)
+            for copy in stores(i):
+                copy.wait()
 
         loop(count, finish)
 
@@ -273,11 +301,12 @@
 
         loop(pairs, step)
         if not backward:
-
-            def keep(i):
-                home_low[tile_rows(i), :] = residual[tile_rows(i), :].astype(BF)
-
-            loop(count, keep)
+            for copy in loads:
+                copy.start()
+                copy.wait()
+            copy = pltpu.make_async_copy(residual, home_low, home_s.at[0])
+            copy.start()
+            copy.wait()
         loop(pairs, lambda p: back(p).wait_send())
 
 
@@ -290,8 +319,12 @@
         jax.ShapeDtypeStruct((2 * size, width), BF),
     )
     outs += (jax.ShapeDtypeStruct((1, width), F32) if backward else jax.ShapeDtypeStruct((size, width), BF),)
-    scratch = [pltpu.VMEM((size, width), BF)] * 4 + [pltpu.VMEM((size // 2, width), BF)]
+    part, gain, *others = (part,) + rest
+    scratch = [pltpu.VMEM((size, width), one.dtype) for one in others]
+    scratch += [pltpu.VMEM((size, width), F32)] + [pltpu.VMEM((size, width), BF)] * 5
+    scratch += [pltpu.VMEM((size // 2, width), BF)]
     sizes = [count, count, count, count, count, count // 2, count // 2, count, count]
+    sizes += [2, count, count, count]
     scratch += [pltpu.SemaphoreType.DMA((n,)) for n in sizes]
     return comm_call(
         functools.partial(sum_tiles, active, backward, per_chip),
@@ -300,12 +333,13 @@
         (part,) + rest,
         outs,
         scratch,
-        [pl.ANY] + [pltpu.VMEM] * len(rest),
+        [pl.ANY, pltpu.VMEM] + [pl.ANY] * len(others),
+        to=[pl.ANY] * 2 + [pltpu.VMEM if backward else pl.ANY],
     )
 
 
-def spread_tiles(normed, peers, per_chip, gain, home, full, sems, arrived, source):
-    chip_s, chip_r, low_s, low_r = sems
+def spread_tiles(normed, peers, per_chip, gain, home, full, low, sems, arrived, source):
+    chip_s, chip_r, low_s, low_r, full_s = sems
     half = home.shape[0] // TILE // 2
 
     def place(j, chip):
@@ -321,7 +355,11 @@
 
     def low_copy(i, k, core):
         rows = tile_rows(full_tile(i, core, per_chip))
-        return remote(full.at[rows], full.at[rows], low_s.at[k], low_r.at[k], peers.mate)
+        return remote(low.at[tile_rows(i)], full.at[rows], low_s.at[k], low_r.at[k], peers.mate)
+
+    def store(i):
+        rows = tile_rows(full_tile(i, peers.core, per_chip))
+        return pltpu.make_async_copy(low.at[tile_rows(i)], full.at[rows], full_s.at[i])
 
     def lower(i, values):
         wide = values.astype(F32)
@@ -330,7 +368,8 @@
         elif normed == "first":
             scale = rms_tile(wide)
             wide = wide * jnp.where(peers.section == 0, scale, jnp.ones_like(scale)) * gain[...]
-        full[tile_rows(full_tile(i, peers.core, per_chip)), :] = wide.astype(BF)
+        low[tile_rows(i), :] = wide.astype(BF)
+        store(i).start()
 
     def own(j):
         arrived(j)
@@ -357,11 +396,13 @@
         low_copy(place(j, 1 - peers.chip), half + j, peers.core).wait_send()
         low_copy(place(j, peers.chip), j, 1 - peers.core).wait_recv()
         low_copy(place(j, 1 - peers.chip), half + j, 1 - peers.core).wait_recv()
+        store(place(j, peers.chip)).wait()
+        store(place(j, 1 - peers.chip)).wait()
 
     loop(half, finish)
 
 
-def start_tiles(per_chip, local, gain, home, full, *sems):
+def start_tiles(per_chip, local, gain, home, full, low, *sems):
     peers = Peers()
     greet([peers.mate, peers.beside], 2)
     spread_tiles(
@@ -371,6 +412,7 @@
         gain,
         home,
         full,
+        low,
         sems,
         lambda j: None,
         lambda j: local.at[tile_rows(j)],
@@ -390,12 +432,14 @@
         number,
         (local, gain),
         outs,
-        [pltpu.SemaphoreType.DMA((n,)) for n in (half, half, 2 * half, 2 * half)],
+        [pltpu.VMEM((2 * size, width), BF)]
+        + [pltpu.SemaphoreType.DMA((n,)) for n in (half, half, 2 * half, 2 * half, 2 * half)],
         [pltpu.VMEM, pltpu.VMEM],
+        to=[pltpu.VMEM, pl.ANY],
     )
 
 
-def scatter_steps(peers, per_chip, parts, mine, from_mate, summed, from_chip, sems, finished):
+def scatter_steps(peers, per_chip, parts, mine, from_mate, summed, from_chip, sems, finished, ready=None):
     own_s, mate_s, mate_r, chip_s, chip_r = sems
     half = mine.shape[0] // TILE // 2
 
@@ -443,6 +487,8 @@
         chip_copy(j).start()
 
     loop(half, away)
+    if ready:
+        ready()
 
     def last(j):
         total = both(j, 1)
@@ -492,15 +538,22 @@
 
 def hop_tiles(source, backward, per_chip, *refs):
     if backward:
-        part, values, grad, gain, next_gain, home, full, gain_out = refs[:8]
-        scratch = refs[8:]
+        part, gain, values_in, grad_in, home, full, gain_out = refs[:7]
+        values, grad = refs[7:9]
+        loads = [(values_in, values), (grad_in, grad)]
+        scratch = refs[9:]
     else:
-        part, values, next_gain, home, full = refs[:5]
-        scratch = refs[5:]
-    crossing, landed, cross_s, cross_r = scratch[:4]
-    spread_sems = scratch[4:8]
-    buffers = scratch[8:12]
-    scatter_sems = scratch[12:]
+        part, gain, values_in, home, full = refs[:5]
+        values = refs[5]
+        loads = [(values_in, values)]
+        scratch = refs[6:]
+    load_s, low, crossing, landed, cross_s, cross_r = scratch[:6]
+    spread_sems = scratch[6:11]
+    buffers = scratch[11:15]
+    scatter_sems = scratch[15:]
+    loads = [
+        pltpu.make_async_copy(one, two, load_s.at[k]) for k, (one, two) in enumerate(loads)
+    ]
     peers = Peers()
     half = crossing.shape[0] // TILE
 
@@ -512,9 +565,15 @@
 
     @pl.when(peers.section == source)
     def give():
+        for copy in loads:
+            copy.start()
         greet([peers.mate, peers.beside], 3)
         if backward:
             gain_out[...] = jnp.zeros_like(gain_out)
+
+        def ready():
+            for copy in loads:
+                copy.wait()
 
         def finished(j, total):
             own = tile_rows(home_tile(j, peers.chip, per_chip))
@@ -527,7 +586,7 @@
             crossing[tile_rows(j), :] = result.astype(BF)
             cross_copy(j).start()
 
-        scatter_steps(peers, per_chip, (part,), *buffers, scatter_sems, finished)
+        scatter_steps(peers, per_chip, (part,), *buffers, scatter_sems, finished, ready)
         loop(half, lambda j: cross_copy(j).wait_send())
 
     @pl.when(peers.section != source)
@@ -537,9 +596,10 @@
             None if backward else "all",
             peers,
             per_chip,
-            next_gain,
+            gain,
             home,
             full,
+            low,
             spread_sems,
             lambda j: cross_copy(j).wait_recv(),
             lambda j: landed.at[tile_rows(j)],
@@ -556,8 +616,12 @@
     )
     if backward:
         outs += (jax.ShapeDtypeStruct((1, width), F32),)
-    scratch = [pltpu.VMEM((size // 2, width), BF)] * 2
-    scratch += [pltpu.SemaphoreType.DMA((n,)) for n in (half, half, half, half, 2 * half, 2 * half)]
+    gain, *others = rest
+    scratch = [pltpu.VMEM((size, width), one.dtype) for one in others]
+    scratch += [pltpu.SemaphoreType.DMA((2,)), pltpu.VMEM((size, width), BF)]
+    scratch += [pltpu.VMEM((size // 2, width), BF)] * 2
+    sizes = (half, half, half, half, 2 * half, 2 * half, 2 * half)
+    scratch += [pltpu.SemaphoreType.DMA((n,)) for n in sizes]
     return comm_call(
         functools.partial(hop_tiles, source, backward, per_chip),
         "hop_back" if backward else "hop",
@@ -565,7 +629,8 @@
         (part,) + rest,
         outs,
         scratch + scatter_scratch(size, width),
-        [pl.ANY] + [pltpu.VMEM] * len(rest),
+        [pl.ANY, pltpu.VMEM] + [pl.ANY] * len(others),
+        to=[pltpu.VMEM, pl.ANY] + [pltpu.VMEM] * backward,
     )
 
 
@@ -695,34 +760,16 @@
     return body
 
 
-def ffn_back_tiles(active, tile, shards, *refs):
-    grad, gu, up_w, down_w = refs[:4]
-    up_v, down_v, sems = refs[-3:]
-    outs = refs[-4 - (4 if shards > 1 else 2) : -3]
-
+def ffn_back_tiles(active, tile, grad, gu, up_w, down_w, grad_gu, act, part, up_v, down_v, sems):
     def run():
-        wait_all(load_up(up_w, up_v, sems) + load_down(down_w, down_v, sems))
-        body = back_body(up_v, down_v)
-        part = outs[-1]
-        if shards == 1:
-            here = lambda i: i
-            items = [(out, tile, here) for out in outs]
-            grid = (grad.shape[0] // tile,)
-            stream(body, grid, [(grad, tile, here), (gu, tile, here)], items)
-            return
-        core = lax.axis_index("tensor") % 2
-        spot = lax.axis_index("dp")
-        count = grad.shape[0] // tile // 2
-        for half in range(2):
-            chosen = core if half == 0 else 1 - core
-            here = lambda i: 2 * i + chosen
-            there = lambda i: spot * count + i
-            stream(
-                body,
-                (count,),
-                [(grad, tile, here), (gu, tile, here)],
-                [(outs[half], tile, there), (outs[2 + half], tile, there), (part, tile, here)],
-            )
+        wait_all(load_down(down_w, down_v, sems) + load_up(up_w, up_v, sems))
+        here = lambda i: i
+        stream(
+            back_body(up_v, down_v),
+            (grad.shape[0] // tile,),
+            [(ref, tile, here) for ref in (grad, gu)],
+            [(ref, tile, here) for ref in (grad_gu, act, part)],
+        )
 
     only(active, run)
 
@@ -741,22 +788,71 @@
     only(active, run)
 
 
-def others_back_tiles(tile, shards, first, second, down_w, gu, unused, grad_gu, act, down_v, sems):
-    wait_all(load_down(down_w, down_v, sems))
+def weight_tiles(tile, shards, chunks, *refs):
+    sides = refs[:8], refs[8:16]
+    others_gu = refs[16:18]
+    down_w, out_up, out_down, up_sum, down_sum, down_v, sems = refs[18:]
+    hidden = out_down.shape[0]
+    lanes = down_sum.shape[0]
+    piece = lanes // chunks
+    copies = load_down(down_w, down_v, sems)
+    up_sum[...] = jnp.zeros_like(up_sum)
+    down_sum[...] = jnp.zeros_like(down_sum)
     spot = lax.axis_index("dp")
-    count = first.shape[0] // tile // shards
-    place = lambda k, i: ((spot + 1 + k) % shards) * count + i
-
-    def run(grad):
-        stream(
-            back_body(None, down_v),
-            (shards - 1, count),
-            [(grad, tile, place), (gu, tile, place)],
-            [(grad_gu, tile, place), (act, tile, place)],
-        )
-
-    only(0, lambda: run(first))
-    only(1, lambda: run(second))
+
+    def add(c, z_t, g_t, grad_gate, grad_up, act):
+        rows = slice(c * piece, (c + 1) * piece)
+        more = slice(lanes + c * piece, lanes + (c + 1) * piece)
+        up_sum[rows, :] += dot(grad_gate, z_t[...], (0, 0))
+        up_sum[more, :] += dot(grad_up, z_t[...], (0, 0))
+        down_sum[rows, :] += dot(act, g_t[...], (0, 0))
+
+    def own_body(z_t, grad_t, g_t, act_t):
+        for c in range(chunks):
+            rows = slice(c * piece, (c + 1) * piece)
+            more = slice(lanes + c * piece, lanes + (c + 1) * piece)
+            add(c, z_t, g_t, grad_t[:, rows], grad_t[:, more], act_t[:, rows])
+
+    def body(z_t, g_t, gu_t):
+        for c in range(chunks):
+            rows = slice(c * piece, (c + 1) * piece)
+            more = slice(lanes + c * piece, lanes + (c + 1) * piece)
+            grad_act = dot(g_t[...], down_v[rows, :], (1, 1))
+            gate = gu_t[:, rows].astype(F32)
+            up = gu_t[:, more].astype(F32)
+            sig = 1.0 / (1.0 + jnp.exp(-gate))
+            silu = gate * sig
+            slope = sig + silu * (1.0 - sig)
+            add(
+                c,
+                z_t,
+                g_t,
+                (grad_act * up * slope).astype(BF),
+                (grad_act * silu).astype(BF),
+                (silu * up).astype(BF),
+            )
+
+    def run(z_mine, z_mate, g_mine, g_mate, full, grad_gu, grad_full, act):
+        here = lambda i: i
+        items = [(ref, tile, here) for ref in (full, grad_gu, grad_full, act)]
+        stream(own_body, (full.shape[0] // tile,), items, [])
+        count = z_mine.shape[0] // tile // shards
+        place = lambda k, i: ((spot + 1 + k) % shards) * count + i
+        for z, g, gu in ((z_mine, g_mine, others_gu[0]), (z_mate, g_mate, others_gu[1])):
+            items = [(ref, tile, place) for ref in (z, g, gu)]
+            stream(body, (shards - 1, count), items, [])
+
+    wait_all(copies)
+    for section in range(2):
+        only(section, functools.partial(run, *sides[section]))
+    copies = [
+        pltpu.make_async_copy(up_sum.at[pl.ds(c * lanes, hidden)], out_up.at[c], sems.at[c])
+        for c in range(2)
+    ]
+    copies += [pltpu.make_async_copy(down_sum.at[pl.ds(0, hidden)], out_down, sems.at[2])]
+    for copy in copies:
+        copy.start()
+    wait_all(copies)
 
 
 def ffn_pallas(kernel, name, inputs, outs, weights, micros, aliases=None):
@@ -805,46 +901,54 @@
     )[0]
 
 
-def ffn_back_call(active, tile, shards, grad, gu, up_w, down_w, into=()):
+def ffn_back_call(active, tile, grad, gu, up_w, down_w):
     up, down = weight_shapes(up_w)
-    if shards == 1:
-        outs = ((grad.shape[0], up[0]), (grad.shape[0], down[0]))
-    else:
-        rows = grad.shape[0] // 2 * shards
-        outs = ((rows, up[0]),) * 2 + ((rows, down[0]),) * 2
     return ffn_pallas(
-        functools.partial(ffn_back_tiles, active, tile, shards),
+        functools.partial(ffn_back_tiles, active, tile),
         "ffn_back",
-        (grad, gu, up_w, down_w) + tuple(into),
-        outs + (grad.shape,),
+        (grad, gu, up_w, down_w),
+        (gu.shape, (grad.shape[0], down[0]), grad.shape),
         (up, down),
         48,
-        {4 + i: i for i in range(len(into))},
     )
 
 
 def others_up_call(active, tile, shards, source, up_w, into, *earlier):
+    up = weight_shapes(up_w)[0]
+    more = earlier if into is None else (into,) + earlier
     return ffn_pallas(
         functools.partial(others_up_tiles, active, tile, shards),
         "others_up",
-        (source, up_w, into) + earlier,
-        (into.shape,),
-        (weight_shapes(up_w)[0],),
+        (source, up_w) + more,
+        ((source.shape[0], up[0]),),
+        (up,),
         42,
-        {2: 0},
+        {} if into is None else {2: 0},
     )[0]
 
 
-def others_back_call(tile, shards, first, second, down_w, gu, act):
-    return ffn_pallas(
-        functools.partial(others_back_tiles, tile, shards),
-        "others_back",
-        (first, second, down_w, gu, act),
-        (gu.shape, act.shape),
-        ((act.shape[1], down_w.shape[1]),),
-        32,
-        {3: 0, 4: 1},
-    )
+def weight_call(tile, shards, first, second, others_gu, down_w):
+    hidden, width = down_w.shape
+    lanes = padded(hidden)
+    inputs = tuple(first) + tuple(second) + tuple(others_gu) + (down_w,)
+    return pl.pallas_call(
+        functools.partial(weight_tiles, tile, shards, 1),
+        name="weights",
+        out_shape=(
+            jax.ShapeDtypeStruct((2, hidden, width), F32),
+            jax.ShapeDtypeStruct((hidden, width), F32),
+        ),
+        in_specs=[pl.BlockSpec(memory_space=pl.ANY)] * len(inputs),
+        out_specs=(pl.BlockSpec(memory_space=pl.ANY),) * 2,
+        scratch_shapes=[
+            pltpu.VMEM((2 * lanes, width), F32),
+            pltpu.VMEM((lanes, width), F32),
+            pltpu.VMEM((lanes, width), BF),
+            pltpu.SemaphoreType.DMA((3,)),
+        ],
+        cost_estimate=estimate(60),
+        compiler_params=pltpu.CompilerParams(vmem_limit_bytes=WEIGHT_BYTES),
+    )(*inputs)
 
 
 def hold_call(values, *others):
@@ -862,28 +966,50 @@
     )(values, *others)
 
 
-def total_tiles(values, out, held, landed, sends, receives):
-    peers = Peers()
+def total_tiles(values, out, near, far, sends, receives, far_sends, far_receives):
+    section = lax.axis_index("section")
+    place = lax.axis_index("tensor")
     spot = lax.axis_index("dp")
-    partners = [
-        peers.mate,
-        peers.beside,
-        peers.across,
-        {"dp": spot + 1 - 2 * (spot % 2)},
-        {"dp": spot + 2 - 4 * (spot // 2)},
+    size = near.shape[0]
+    chips = size // 2
+    shards = far.shape[0]
+    own = section * chips + place
+    steps = [(a, b) for a in range(2) for b in range(chips) if a + b > 0]
+    peers = [{"section": (section + a) % 2, "tensor": (place + b) % chips} for a, b in steps]
+    shard_peers = [{"dp": (spot + c) % shards} for c in range(1, shards)]
+    greet(peers + shard_peers, len(peers) + len(shard_peers))
+    near[own] = values[...]
+    copies = [
+        remote(near.at[own], near.at[own], sends.at[i], receives.at[own], peer)
+        for i, peer in enumerate(peers)
     ]
-    greet(partners, len(partners))
-    held[0] = values[...]
-    for i, partner in enumerate(partners):
-        copy = remote(held.at[i], landed.at[i], sends.at[i], receives.at[i], partner)
+    for copy in copies:
         copy.start()
-        copy.wait()
-        held[i + 1] = held[i] + landed[i]
-    out[...] = held[len(partners)]
-
-
-def total_call(number, values):
-    count = 5
+    for (a, b), peer in zip(steps, peers):
+        theirs = ((section + a) % 2) * chips + (place + b) % chips
+        remote(near.at[theirs], near.at[theirs], sends.at[0], receives.at[theirs], peer).wait_recv()
+    total = near[0]
+    for i in range(1, size):
+        total = total + near[i]
+    far[spot] = total
+    far_copies = [
+        remote(far.at[spot], far.at[spot], far_sends.at[i], far_receives.at[spot], peer)
+        for i, peer in enumerate(shard_peers)
+    ]
+    for copy in far_copies:
+        copy.start()
+    for c, peer in enumerate(shard_peers):
+        theirs = (spot + c + 1) % shards
+        remote(far.at[theirs], far.at[theirs], far_sends.at[0], far_receives.at[theirs], peer).wait_recv()
+    total = far[0]
+    for i in range(1, shards):
+        total = total + far[i]
+    out[...] = total
+    for copy in copies + far_copies:
+        copy.wait_send()
+
+
+def total_call(number, values, size, shards):
     return comm_call(
         total_tiles,
         "total",
@@ -891,12 +1017,15 @@
         (values,),
         (jax.ShapeDtypeStruct(values.shape, F32),),
         [
-            pltpu.VMEM((count + 1,) + values.shape, F32),
-            pltpu.VMEM((count,) + values.shape, F32),
-            pltpu.SemaphoreType.DMA((count,)),
-            pltpu.SemaphoreType.DMA((count,)),
+            pltpu.VMEM((size,) + values.shape, F32),
+            pltpu.VMEM((shards,) + values.shape, F32),
+            pltpu.SemaphoreType.DMA((size,)),
+            pltpu.SemaphoreType.DMA((size,)),
+            pltpu.SemaphoreType.DMA((shards,)),
+            pltpu.SemaphoreType.DMA((shards,)),
         ],
         [pltpu.VMEM],
+        10,
     )[0]
 
 
@@ -1205,7 +1334,7 @@
     def sum_norm(section, number, part, residual, gain):
         if fused:
             out, full, low = sum_call(
-                section, number, False, seq_local, part, tokens(residual), row(gain)
+                section, number, False, seq_local, part, row(gain), tokens(residual)
             )
             return homed(out), full, low
         out = residual.astype(F32) + chip_sum(core_sum(part, section), section)
@@ -1219,9 +1348,9 @@
                 True,
                 seq_local,
                 part,
+                row(gain),
                 tokens(hidden_in),
                 tokens(grad),
-                row(gain),
             )
             return homed(out), full, terms[0]
         dz = chip_sum(core_sum(part, section), section)
@@ -1232,7 +1361,7 @@
     def hop(number, part, hidden_in, gain):
         if fused:
             home, full = hop_call(
-                0, number, False, seq_local, part, tokens(hidden_in), row(gain)
+                0, number, False, seq_local, part, row(gain), tokens(hidden_in)
             )
             return homed(home), full
         result = pick(hidden_in, chip, 1) + chip_scatter(core_sum(part, 0), 0)
@@ -1247,10 +1376,9 @@
                 True,
                 seq_local,
                 part,
+                row(gain),
                 tokens(values),
                 tokens(grad),
-                row(gain),
-                row(gain),
             )
             return homed(home), full, terms[0]
         dz = chip_scatter(core_sum(part, 1), 1)
@@ -1383,11 +1511,9 @@
             grad_out[:, :cut].reshape(attn_out.shape),
         )
 
-    shards = dp if fused else 1
-
     def weights(full, grad_gu, grad_full, act):
-        grad_up = sum(mm("tf,td->fd", one, two) for one, two in zip(grad_gu, full))
-        grad_down = sum(mm("tf,td->fd", one, two) for one, two in zip(act, grad_full))
+        grad_up = mm("tf,td->fd", grad_gu, full, BF)
+        grad_down = mm("tf,td->fd", act, grad_full, BF)
         return grad_up.reshape(2, -1, width)[:, :hidden], grad_down[:hidden]
 
     def choose(function, first_args, second_args):
@@ -1425,15 +1551,15 @@
         all_b = gather_shards(low2)
     gu2 = ffn_call(1, seq_local, full2, up_w, None)
 
-    *kept2, part = ffn_back_call(1, seq_local, shards, start_full, gu2, up_w, down_w)
+    grad_gu2, act2, part = ffn_back_call(1, seq_local, start_full, gu2, up_w, down_w)
     if fused:
         all_a = with_mate(all_a, (0, 1), gu2)
-        kept2[0] = others_up_call(0, seq_local, dp, all_a[0], up_w, kept2[0])
-        part = hold_call(part, kept2[0])
+        gu_mine = others_up_call(0, seq_local, dp, all_a[0], up_w, None)
+        part = hold_call(part, gu_mine)
     gh3, gm3, gain_ffn2 = sum_back(1, 4, part, h3, start_home, gains[1, 1])
     if fused:
-        kept2[1] = others_up_call(0, seq_local, dp, all_a[1], up_w, kept2[1], gm3)
-        gm3 = hold_call(gm3, kept2[1])
+        gu_mate = others_up_call(0, seq_local, dp, all_a[1], up_w, None, gm3)
+        gm3 = hold_call(gm3, gu_mate)
     unused, (part, grad_raw, head_grads) = either(
         nothing, (), attn_backward, (gm3, *saved) + setup
     )
@@ -1441,24 +1567,22 @@
     if fused:
         all_c = gather_shards(tokens(g_home))
 
-    *kept1, part = ffn_back_call(
-        0, seq_local, shards, g_full, gu1, up_w, down_w, kept2 if fused else ()
-    )
+    grad_gu1, act1, part = ffn_back_call(0, seq_local, g_full, gu1, up_w, down_w)
     part_out = down_call(1, seq_local, gu2, down_w, g_home)
-    late = (hold_call(z3, part_out), grad_raw, saved[-1], gm3)
-    unused, attn_grads = either(nothing, (), attn_weights, late)
-    part = hold_call(part, attn_grads[0])
     if fused:
         all_b = with_mate(all_b, (1,), part_out)
-        kept1[0] = others_up_call(1, seq_local, dp, all_b[0], up_w, kept1[0], attn_grads[0])
-        part = hold_call(part, kept1[0])
+        gu_mine = others_up_call(1, seq_local, dp, all_b[0], up_w, gu_mine, part_out)
+        part = hold_call(part, gu_mine)
     gh1, gm1, gain_ffn1 = sum_back(0, 6, part, h1, g_home, gains[0, 1])
-    (part, conv_grads), unused = either(
-        conv_backward, (gm1, project, mixed, start_full), nothing, ()
+    (part, conv_grads), attn_grads = either(
+        conv_backward,
+        (gm1, project, mixed, start_full),
+        attn_weights,
+        (z3, grad_raw, saved[-1], gm3),
     )
     if fused:
-        kept1[1] = others_up_call(1, seq_local, dp, all_b[1], up_w, kept1[1], gm1)
-        part_out = hold_call(part_out, kept1[1])
+        gu_mate = others_up_call(1, seq_local, dp, all_b[1], up_w, gu_mate, gm1)
+        part_out = hold_call(part_out, gu_mate)
     total = end(7, part, part_out)
     change, terms = norm_back(local.astype(F32), gains[0, 0], total)
     gain_mix1 = jnp.sum(terms, axis=(0, 1))
@@ -1466,28 +1590,19 @@
 
     if fused:
         all_c = with_mate(all_c, (0,), total)
-        for half in range(2):
-            kept1[half], kept1[2 + half] = others_back_call(
-                seq_local,
-                dp,
-                all_c[half],
-                all_a[half],
-                down_w,
-                kept1[half],
-                kept1[2 + half],
-            )
-        grad_up, grad_down = choose(
-            weights,
-            (all_a, kept1[:2], all_c, kept1[2:]),
-            (all_b, kept1[:2], all_a, kept1[2:]),
+        grad_up, grad_down = weight_call(
+            seq_local,
+            dp,
+            (*all_a, *all_c, full1, grad_gu1, g_full, act1),
+            (*all_b, *all_a, full2, grad_gu2, start_full, act2),
+            (gu_mine, gu_mate),
+            down_w,
         )
     else:
         grad_up, grad_down = choose(
-            weights,
-            ((full1,), kept1[:1], (g_full,), kept1[1:]),
-            ((full2,), kept2[:1], (start_full,), kept2[1:]),
+            weights, (full1, grad_gu1, g_full, act1), (full2, grad_gu2, start_full, act2)
         )
-        grad_up, grad_down = lax.psum((grad_up.astype(BF), grad_down.astype(BF)), "dp")
+        grad_up, grad_down = lax.psum((grad_up, grad_down), "dp")
     full_gu = grad_up.astype(F32).transpose(2, 0, 1)[None]
     full_down = grad_down.astype(F32).T[None]
 
@@ -1496,7 +1611,8 @@
     second_gains = jnp.concatenate([zero, zero, gain_mix2, gain_ffn2])
     small = jnp.concatenate([jnp.where(is_first, first_gains, second_gains), head_grads.reshape(-1)])
     if fused:
-        small = total_call(11, hold_call(small.reshape(1, -1), grad_down))[0]
+        small = hold_call(small.reshape(8, -1), grad_down)
+        small = total_call(11, small, 4 * chips, dp).reshape(-1)
     else:
         small = lax.psum(small, ("section", "tensor", "dp"))
     mixer_sums = lax.psum(tuple(conv_grads) + tuple(attn_grads), ("section", "dp"))

time: 1190 us -> 1110 us (0.933)
  matrix products: 223 us -> 45.6 us
  Pallas kernels: 779 us -> 854 us
  waiting for transfers between devices: 14.7 us -> 58.2 us
  local copies, waits for them, and re-layouts: 80.3 us -> 63.7 us
    pallas_call x0 -> x1, Pallas kernels: none -> 216 us  [weight_call(): pl.pallas_call(functools.partial(weight_tiles, tile, shards, 1), name='we...]
    dot_general x10 -> x6, matrix products: 223 us -> 45.6 us  [mm(): jnp.einsum(spec, left, right, preferred_element_type=F32).astype(kind)]
    pallas_call x11 -> x9, Pallas kernels: 255 us -> 181 us  [ffn_pallas(): pl.pallas_call(kernel, name=name, out_shape=tuple((jax.ShapeDtypeStruct(s...]
    pallas_call x9, Pallas kernels: 524 us -> 457 us  [comm_call(): pl.pallas_call(kernel, name=name, out_shape=outs, in_specs=[pl.BlockSpec(...]
    all_gather x3, waiting for transfers between devices: 14.7 us -> 37.5 us  [gather_shards(): return lax.all_gather(home_tokens, 'dp', axis=0, tiled=True)]
    psum x1, waiting for transfers between devices: 0.01 us -> 19.9 us  [on_device(): lax.psum(tuple(conv_grads) + tuple(attn_grads), ('section', 'dp'))]
    slice x1 -> x0, local copies, waits for them, and re-layouts: 16.2 us -> none  [weights(): return (grad_up.reshape(2, -1, width)[:, :hidden], grad_down[:hidden])]
  transfers between devices with their start and end apart: 7 -> 7, of which waited for: 1 -> 4; matrix products, arithmetic and copies ran while one was open for 25% -> 9% of each run, Pallas kernels for 57% -> 69%
where the time goes in v4:
time: 1110 us; the launch traced here: 1100 us
  Pallas kernels  854 us (77%)
  local copies, waits for them, and re-layouts  63.7 us (6%)
  waiting for transfers between devices  58.2 us (5%)
  other arithmetic  47.9 us (4%)
  matrix products  45.6 us (4%)
  between operations  14.9 us (1%)
    pallas_call x9, Pallas kernels, comm_call(): pl.pallas_call(kernel, name=name, out_shape=outs, in_specs=[pl.BlockSpec(...  457 us
    pallas_call x1, Pallas kernels, weight_call(): pl.pallas_call(functools.partial(weight_tiles, tile, shards, 1), name='we...  216 us
    pallas_call x9, Pallas kernels, ffn_pallas(): pl.pallas_call(kernel, name=name, out_shape=tuple((jax.ShapeDtypeStruct(s...  181 us
    dot_general x6, matrix products, mm(): jnp.einsum(spec, left, right, preferred_element_type=F32).astype(kind)  45.6 us
    all_gather x3, waiting for transfers between devices, gather_shards(): return lax.all_gather(home_tokens, 'dp', axis=0, tiled=True)  37.5 us
    another operation x17, local copies, waits for them, and re-layouts, within(): return mapped(*args)  31.9 us
  transfers between devices with their start and end apart: 7, of which 4 were waited for; matrix products, arithmetic and copies ran while one was open for 9% of the time, Pallas kernels for 69%

profile of v4, /device:TPU:0, one launch (start us, length us, event | category | flops | bytes accessed | tf_op | source)
XLA Modules:
  0.0 1100.9 jit_solution(9963628268920200208)
XLA Ops:
  8.0 1.2 slice_reduce_fusion.6
  9.2 6.2 copy.67
  15.4 43.1 %start.1 = (bf16[1024,1536]{1,0:T(8,128)(2,1)}, bf16[2048,1536]{1,0:T(8,128)(2,1)}) custom-call(bf16[512,1536]{1,0:T(8,128)(2,1)} %bitcast.111, f32[1,1536]{1,0:T(1,128)} %get-tuple-element.357.gain), custom_call_target="tpu_custom_call" | custom-call | bytes 171600000 | tf_op jit(solution)/shard_map/start/pallas_call | solution.py:140
  58.5 27.7 %conditional.4 = (bf16[2048,1536]{1,0:T(8,128)(2,1)}, bf16[2,1024,1152]{2,1,0:T(8,128)(2,1)}, bf16[2048,384]{1,0:T(8,128)(2,1)}, bf16[1536,768]{1,0:T(8,128)(2,1...) conditional(s32[]{:T(128)} %convert_element_type.121, ...), branch_computations={%region_0.2_spmd, %region_2.3_spmd} | conditional | flops 9677053952 | bytes 69523032 | solution.py:1404
  58.7 11.5 %fusion.42 = f32[2048,1152]{1,0:T(8,128)S(1)} fusion(bf16[2048,1536]{1,0:T(8,128)(2,1)} %get-tuple-element.82, bf16[1536,1152]{0,1:T(8,128)(2,1)} %get-tuple-element.302), kind=kOutput, calls=%fused_computation.110 | convolution fusion | flops 7247757312 | bytes 19267584 | tf_op jit(solution)/shard_map/cond/branch_1_fun/td,de->te/dot_general | solution.py:22
  70.7 2.3 fusion.10
  73.0 6.7 convolution_convert_fusion.5
  79.7 2.6 convert_element_type.98
  82.3 1.6 broadcast.150
  83.8 1.3 broadcast.151
  86.2 48.6 %sum_norm.2 = (f32[1024,1536]{1,0:T(8,128)}, bf16[2048,1536]{1,0:T(8,128)(2,1)}, bf16[1024,1536]{1,0:T(8,128)(2,1)}) custom-call(bf16[2048,1536]{1,0:T(8,128)(2,1)} %get-tuple-element.188.refs_0_, f32[1,1536]{1,0:T(1,128)} %get-tuple-element.356.refs_1_, bf16[1024,1536]{1,0:T(8,128)(2,1)} %get-tuple-element.189.refs_2_.refs_3_), custom_call_target="tpu_custom_call" | custom-call | bytes 171600000 | tf_op jit(solution)/shard_map/sum_norm/pallas_call | solution.py:140
  135.5 44.6 %ffn.1 = (bf16[2048,3584]{1,0:T(8,128)(2,1)}, bf16[2048,1536]{1,0:T(8,128)(2,1)}) custom-call(bf16[2048,1536]{1,0:T(8,128)(2,1)} %get-tuple-element.190.refs_0_.refs_4_, bf16[2,1728,1536]{2,1,0:T(8,128)(2,1)} %bitcast.92, bf16[1728,1536]{1,0:T(8,128)(2,1)} %bitcast.100), custom_call_target="tpu_custom_call" | custom-call | bytes 145200000 | tf_op jit(solution)/shard_map/ffn/pallas_call | solution.py:859
  180.1 47.3 %hop.1 = (bf16[1024,1536]{1,0:T(8,128)(2,1)}, bf16[2048,1536]{1,0:T(8,128)(2,1)}) custom-call(bf16[2048,1536]{1,0:T(8,128)(2,1)} %get-tuple-element.191.refs_0_, f32[1,1536]{1,0:T(1,128)} %get-tuple-element.355.refs_1_, f32[1024,1536]{1,0:T(8,128)} %get-tuple-element.192.refs_2_), custom_call_target="tpu_custom_call" | custom-call | bytes 171600000 | tf_op jit(solution)/shard_map/hop/pallas_call | solution.py:140
  227.4 21.8 %conditional.5 = (bf16[2048,1536]{1,0:T(8,128)(2,1)}, f32[2,1024,768]{2,1,0:T(8,128)}, bf16[2,1024,768]{2,1,0:T(8,128)(2,1)}, bf16[2,2,3,1024,1024]{4,3,2,1,0:T(...) conditional(s32[]{:T(128)} %convert_element_type.121, (bf16[2048,1536]{1,0:T(8,128)(2,1)}, ...), branch_computations={%region_3.4_spmd, %region_4.5_spmd} | conditional | flops 8056209408 | bytes 114036496 | solution.py:1404
  227.9 8.6 broadcast.156
  236.5 3.1 broadcast.153
  239.6 3.1 broadcast.154
  242.7 3.2 broadcast.157
  245.9 1.9 broadcast.155
  247.8 1.5 broadcast.158
  249.2 79.7 %sum_norm.3 = (f32[1024,1536]{1,0:T(8,128)}, bf16[2048,1536]{1,0:T(8,128)(2,1)}, bf16[1024,1536]{1,0:T(8,128)(2,1)}) custom-call(bf16[2048,1536]{1,0:T(8,128)(2,1)} %get-tuple-element.198.refs_0_, f32[1,1536]{1,0:T(1,128)} %get-tuple-element.354.refs_1_, bf16[1024,1536]{1,0:T(8,128)(2,1)} %get-tuple-element.199.refs_2_), custom_call_target="tpu_custom_call" | custom-call | bytes 171600000 | tf_op jit(solution)/shard_map/sum_norm/pallas_call | solution.py:140
  329.0 24.1 %all-gather.4.cloned.1.call-done.refs_0_ = bf16[4096,1536]{1,0:T(8,128)(2,1)} async-done(((bf16[1024,1536]{1,0:T(8,128)(2,1)}), bf16[4096,1536]{1,0:T(8,128)(2,1)}) %all-gather.4.cloned.1.call-update) | async-done | bytes 12582928 | tf_op jit(solution)/shard_map/all_gather | solution.py:1529
  353.2 43.5 %others_up.4.refs_1_.refs_0_ = bf16[4096,3584]{1,0:T(8,128)(2,1)} custom-call(bf16[4096,1536]{1,0:T(8,128)(2,1)} %hold.15.source.refs_0_.refs_10_, bf16[2,1728,1536]{2,1,0:T(8,128)(2,1)} %bitcast.95), custom_call_target="tpu_custom_call" | custom-call | bytes 138600000 | tf_op jit(solution)/shard_map/others_up/pallas_call | solution.py:859
  396.8 62.0 %sum_back.2 = (f32[1024,1536]{1,0:T(8,128)}, bf16[2048,1536]{1,0:T(8,128)(2,1)}, f32[1,1536]{1,0:T(1,128)}) custom-call(bf16[2048,1536]{1,0:T(8,128)(2,1)} %hold.16.refs_0_, f32[1,1536]{1,0:T(1,128)} %get-tuple-element.354.refs_1_, f32[1024,1536]{1,0:T(8,128)} %get-tuple-element.203.refs_2_, bf16[1024,1536]{1,0:T(8,128)(2,1)} %get-tuple-element.189.refs_2_.refs_3_), custom_call_target="tpu_custom_call" | custom-call | bytes 171600000 | tf_op jit(solution)/shard_map/sum_back/pallas_call | solution.py:140
  458.8 43.6 %others_up.5.refs_1_.refs_0_ = bf16[4096,3584]{1,0:T(8,128)(2,1)} custom-call(bf16[4096,1536]{1,0:T(8,128)(2,1)} %collective-permute-done.source.refs_1_.refs_11_, bf16[2,1728,1536]{2,1,0:T(8,128)(2,1)} %bitcast.96, bf16[2048,1536]{1,0:T(8,128)(2,1)} %get-tuple-element.204.refs_0_), custom_call_target="tpu_custom_call" | custom-call | bytes 138600000 | tf_op jit(solution)/shard_map/others_up/pallas_call | solution.py:859
  502.4 12.5 %conditional.6 = (bf16[2048,1536]{1,0:T(8,128)(2,1)}, bf16[2048,768]{1,0:T(8,128)(2,1)}, f32[2,64]{1,0:T(2,128)S(1)}) conditional(s32[]{:T(128)} %convert_element_type.121, (bf16[2048,1536]{1,0:T(8,128)(2,1)}, bf16[512,1536]{1,0:T(8,128)(2,1)}, f32[2,1024,768]{2,1,0:T(8,128)}, bf16[2,1024,768]{2,1,0:T(8,128)(2,1)}, ...), branch_computations={%region_5.6_spmd, %region_6.7_spmd} | conditional | flops 8057257984 | bytes 163657984 | solution.py:1404
  510.0 3.1 broadcast.159
  513.1 1.9 broadcast.160
  514.9 64.9 %hop_back.1 = (bf16[1024,1536]{1,0:T(8,128)(2,1)}, bf16[2048,1536]{1,0:T(8,128)(2,1)}, f32[1,1536]{1,0:T(1,128)}) custom-call(bf16[2048,1536]{1,0:T(8,128)(2,1)} %get-tuple-element.210.refs_0_, f32[1,1536]{1,0:T(1,128)} %get-tuple-element.355.refs_1_, bf16[1024,1536]{1,0:T(8,128)(2,1)} %get-tuple-element.199.refs_2_, f32[1024,1536]{1,0:T(8,128)} %get-tuple-element.211.refs_3_), custom_call_target="tpu_custom_call" | custom-call | bytes 171600000 | tf_op jit(solution)/shard_map/hop_back/pallas_call | solution.py:140
  580.0 5.3 collective-permute-start.1
  585.3 49.5 %ffn_back.3 = (bf16[2048,3584]{1,0:T(8,128)(2,1)}, bf16[2048,1792]{1,0:T(8,128)(2,1)}, bf16[2048,1536]{1,0:T(8,128)(2,1)}) custom-call(bf16[2048,1536]{1,0:T(8,128)(2,1)} %get-tuple-element.212.grad.refs_6_, bf16[2048,3584]{1,0:T(8,128)(2,1)} %get-tuple-element.213.gu, bf16[2,1728,1536]{2,1,0:T(8,128)(2,1)} %bitcast.98, bf16[1728,1536]{1,0:T(8,128)(2,1)} %bitcast.103), custom_call_target="tpu_custom_call" | custom-call | bytes 158400000 | tf_op jit(solution)/shard_map/ffn_back/pallas_call | solution.py:859
  634.9 52.5 %sum_back.3 = (f32[1024,1536]{1,0:T(8,128)}, bf16[2048,1536]{1,0:T(8,128)(2,1)}, f32[1,1536]{1,0:T(1,128)}) custom-call(bf16[2048,1536]{1,0:T(8,128)(2,1)} %hold.19.refs_0_, f32[1,1536]{1,0:T(1,128)} %get-tuple-element.356.refs_1_, f32[1024,1536]{1,0:T(8,128)} %get-tuple-element.192.refs_2_, bf16[1024,1536]{1,0:T(8,128)(2,1)} %get-tuple-element.216.refs_3_), custom_call_target="tpu_custom_call" | custom-call | bytes 171600000 | tf_op jit(solution)/shard_map/sum_back/pallas_call | solution.py:140
  687.4 55.0 %conditional.7 = (bf16[2048,1536]{1,0:T(8,128)(2,1)}, bf16[1536,384]{0,1:T(8,128)(2,1)}, bf16[1536,384]{0,1:T(8,128)(2,1)}, bf16[1536,384]{0,1:T(8,128)(2,1)}, b...) conditional(s32[]{:T(128)} %convert_element_type.121, ...), branch_computations={%region_8.9_spmd, %region_9.13_spmd} | conditional | flops 19388383232 | bytes 212552992 | solution.py:1404
  687.6 3.0 convert_element_type.104
  691.0 2.4 copy-done.2
  693.7 5.3 fusion.43
  699.0 6.5 multiply_reduce_fusion.2
  705.6 4.1 convolution_convert_fusion.8
  709.7 1.1 pad_maximum_fusion.6
  710.9 5.7 multiply_convert_fusion.2
  718.5 8.1 fusion.13
  726.6 1.9 fusion.40
  728.5 1.4 copy-done.6
  730.3 10.0 convolution_convert_fusion.7
  740.5 1.1 broadcast.181
  743.7 40.6 %end.1 = f32[512,1536]{1,0:T(8,128)} custom-call(bf16[2048,1536]{1,0:T(8,128)(2,1)} %get-tuple-element.222.first, bf16[2048,1536]{1,0:T(8,128)(2,1)} %hold.20.second), custom_call_target="tpu_custom_call" | custom-call | bytes 171600000 | tf_op jit(solution)/shard_map/end/pallas_call | solution.py:140
  784.3 13.3 %all-gather.8.cloned.1.call-done.refs_0_ = bf16[4096,1536]{1,0:T(8,128)(2,1)} async-done(((bf16[1024,1536]{1,0:T(8,128)(2,1)}), bf16[4096,1536]{1,0:T(8,128)(2,1)}) %all-gather.8.cloned.1.call-update) | async-done | bytes 12582928 | tf_op jit(solution)/shard_map/all_gather | solution.py:1529
  797.6 2.0 collective-permute-start.2
  799.6 2.4 copy.72
  802.0 2.4 copy.73
  804.4 2.4 copy.74
  806.8 1.9 fusion.29
  809.2 2.3 multiply_reduce_fusion.3
  812.2 6.1 fusion.34
  819.0 215.5 %weights.1 = (f32[2,1728,1536]{2,1,0:T(8,128)}, f32[1728,1536]{1,0:T(8,128)}) custom-call(bf16[4096,1536]{1,0:T(8,128)(2,1)} %hold.15.source.refs_0_.refs_10_, bf16[4096,1536]{1,0:T(8,128)(2,1)} %collective-permute-done.source.refs_1_.refs_11_, bf16[4096,1536]{1,0:T(8,128)(2,1)} %hold.21.refs_2_, bf16[4096,1536]{1,0:T(8,128)(2,1)} %collective-permute-done.2.refs_3_, ...), custom_call_target="tpu_custom_call" | custom-call | bytes 198000000 | tf_op jit(solution)/shard_map/weights/pallas_call | solution.py:934
  1034.5 18.6 %total.1 = f32[8,784]{1,0:T(8,128)} custom-call(f32[8,784]{1,0:T(8,128)} %hold.22.values), custom_call_target="tpu_custom_call" | custom-call | bytes 33000000 | tf_op jit(solution)/shard_map/total/pallas_call | solution.py:140
  1053.2 1.4 reshape.224.refs_1_
  1054.6 19.9 %all-reduce.16.cloned.1.call-done = (bf16[1536,384]{1,0:T(8,128)(2,1)}, bf16[1536,384]{1,0:T(8,128)(2,1)}, bf16[1536,384]{1,0:T(8,128)(2,1)}, bf16[400,1536]{1,0...) async-done(((bf16[1536,384]{1,0:T(8,128)(2,1)}, bf16[1536,384]{1,0:T(8,128)(2,1)}, bf16[1536,384]{1,0:T(8,128)(2,1)}, ...) | async-done | bytes 7913488 | tf_op jit(solution)/shard_map/psum | solution.py:1618
  1074.5 3.0 slice.162
  1077.5 1.3 slice.161
  1078.9 3.0 convert_element_type.130
  1081.9 2.4 convert_element_type.129
  1084.3 2.8 convert_element_type.128
  1089.0 4.8 convert_bitcast_fusion
  (128 shorter events, 12.1 us)
Async XLA Ops:
  7.2 346.0 %all-gather.4.cloned.1.call-start = ((), (), s32[]{:S(2)}) async-start(), calls=%async_computation | async-start | bytes 15728640 | tf_op jit(solution)/shard_map/all_gather | solution.py:1529
  9.2 6.2 copy-start.22
  9.2 49.3 %copy-start.12 = (bf16[1536,384]{1,0:T(8,128)(2,1)S(1)}, bf16[1536,384]{1,0:T(8,128)(2,1)}, u32[]{:S(2)}) copy-start(bf16[1536,384]{1,0:T(8,128)(2,1)} %param.27) | copy-start | bytes 3538948
  9.2 49.3 %copy-start.13 = (s32[2,1024]{1,0:T(2,128)S(1)}, s32[2,1024]{1,0:T(2,128)}, u32[]{:S(2)}) copy-start(s32[2,1024]{1,0:T(2,128)} %param.21) | copy-start | bytes 24580
  15.4 43.1 %copy-start.17 = (f32[3,384]{1,0:T(4,128)}, f32[3,384]{1,0:T(4,128)S(1)}, u32[]{:S(2)}) copy-start(f32[3,384]{1,0:T(4,128)S(1)} %convert_element_type.123) | copy-start | bytes 13828
  70.7 2.3 copy-start.24
  134.8 0.7 copy-start.28
  134.9 445.1 %all-gather.6.cloned.1.call-start = ((), (), s32[]{:S(2)}) async-start(), calls=%async_computation.1 | async-start | bytes 15728640 | tf_op jit(solution)/shard_map/all_gather | solution.py:1529
  180.1 47.3 %copy-start.1 = (f32[2,1024,64]{2,1,0:T(8,128)S(1)}, f32[2,1024,64]{2,1,0:T(8,128)}, u32[]{:S(2)}) copy-start(f32[2,1024,64]{2,1,0:T(8,128)} %get-tuple-element.196) | copy-start | bytes 1572868
  328.9 468.7 %all-gather.8.cloned.1.call-start = ((), (), s32[]{:S(2)}) async-start(), calls=%async_computation.2 | async-start | bytes 15728640 | tf_op jit(solution)/shard_map/all_gather | solution.py:1529
  353.1 105.7 %collective-permute-start = (bf16[4096,1536]{1,0:T(8,128)(2,1)}, bf16[4096,1536]{1,0:T(8,128)(2,1)}, u32[]{:S(2)}, u32[]{:S(2)}) collective-permute-start(bf16[4096,1536]{1,0:T(8,128)(2,1)} %hold.15.source.refs_0_.refs_10_), channel_id=1, source_target_pairs={{0,4},{4,0},{8,12},{12,8},{16,20},{20,16},{24,28},{28,24},{1,5},{5... | collective-permute-start | bytes 37748744 | tf_op jit(solution)/shard_map/ppermute | solution.py:1535
  514.9 64.9 %copy-start.26 = (f32[2,64]{1,0:T(2,128)}, f32[2,64]{1,0:T(2,128)S(1)}, u32[]{:S(2)}) copy-start(f32[2,64]{1,0:T(2,128)S(1)} %get-tuple-element.226) | copy-start | bytes 1540
  579.8 494.7 %all-reduce.16.cloned.1.call-start = ((), (), s32[]{:S(2)}) async-start(), calls=%async_computation.3 | async-start | bytes 15826944 | tf_op jit(solution)/shard_map/psum | solution.py:1618
  580.0 162.5 %collective-permute-start.1 = (bf16[4096,1536]{1,0:T(8,128)(2,1)}, bf16[4096,1536]{1,0:T(8,128)(2,1)}, u32[]{:S(2)}, u32[]{:S(2)}) collective-permute-start(bf16[4096,1536]{1,0:T(8,128)(2,1)} %hold.18.source.refs_8_), channel_id=1, source_target_pairs={{16,20},{20,16},{24,28},{28,24},{17,21},{21,17},{25,29},{29,25},{1... | collective-permute-start | bytes 37748744 | tf_op jit(solution)/shard_map/ppermute | solution.py:1535
  634.8 52.6 %copy-start.14 = (s32[2,1024]{1,0:T(2,128)S(1)}, s32[2,1024]{1,0:T(2,128)}, u32[]{:S(2)}) copy-start(s32[2,1024]{1,0:T(2,128)} %param.21) | copy-start | bytes 24580
  634.8 52.6 %copy-start.18 = (f32[3,384]{1,0:T(4,128)S(1)}, f32[3,384]{1,0:T(4,128)}, u32[]{:S(2)}) copy-start(f32[3,384]{1,0:T(4,128)} %copy-done.17) | copy-start | bytes 13828
  634.8 52.6 %copy-start.23 = (bf16[2048,768]{1,0:T(8,128)(2,1)S(1)}, bf16[2048,768]{1,0:T(8,128)(2,1)}, u32[]{:S(2)}) copy-start(bf16[2048,768]{1,0:T(8,128)(2,1)} %get-tuple-element.218) | copy-start | bytes 9437188
  690.6 2.8 copy-start.2
  690.6 3.1 copy-start.25
  709.7 7.4 slice-start
  710.9 6.2 slice-start.1
  716.6 1.4 copy-start.9
  716.6 1.9 copy-start.10
  726.6 3.3 copy-start.6
  726.6 3.7 copy-start.11
  742.4 1.0 copy-start.5
  742.4 1.3 copy-start.7
  797.6 21.4 %collective-permute-start.2 = (bf16[4096,1536]{1,0:T(8,128)(2,1)}, bf16[4096,1536]{1,0:T(8,128)(2,1)}, u32[]{:S(2)}, u32[]{:S(2)}) collective-permute-start(bf16[4096,1536]{1,0:T(8,128)(2,1)} %hold.21.refs_2_), channel_id=1, source_target_pairs={{0,4},{4,0},{8,12},{12,8},{1,5},{5,1},{9,13},{13,9},{2,6},{6,2},{1... | collective-permute-start | bytes 37748744 | tf_op jit(solution)/shard_map/ppermute | solution.py:1535
  806.7 2.0 copy-start.19
  806.7 2.1 copy-start.21
  806.7 2.1 copy-start.20
  806.7 2.2 copy-start.27
  806.7 2.4 copy-start
  806.7 2.4 copy-start.16
  1074.5 4.3 copy-start.15
  1087.1 0.7 slice-start.2
  1087.1 1.9 copy-start.4
  1087.1 1.9 copy-start.3
Sparse Core Ops, SparseCore 0:
  135.0 218.1 all-gather.3
  354.7 216.4 all-gather.5
  580.0 217.6 all-gather.7
  806.9 267.5 all-reduce.15

commit v5 on v4

--- a/solution.py
+++ b/solution.py
@@ -13,7 +13,7 @@
 BF = jnp.bfloat16
 F32 = jnp.float32
 MESH = pl.DeviceIdType.MESH
-TILE = 64
+TILE = 32
 VMEM_BYTES = 60 * 1024 * 1024
 WEIGHT_BYTES = 62 * 1024 * 1024
 
@@ -1450,7 +1450,9 @@
         grad_cout = mm("te,td->ed", mixed, grad_full, BF)
         grad_cin = mm("td,te->de", full, grad_low, BF)
         taps = jnp.stack(grad_kernel).astype(BF)
-        each = [grad_cin[:, i * channels : (i + 1) * channels] for i in range(3)]
+        each = [
+            hold_call(grad_cin[:, i * channels : (i + 1) * channels], part) for i in range(3)
+        ]
         grad_cout = jnp.concatenate([grad_cout, jnp.pad(taps, ((0, 16 - taps.shape[0]), (0, width - channels)))])
         return part, each + [grad_cout]
 

time: 1110 us -> 1100 us (level)
  transfers between devices with their start and end apart: 7 -> 7, of which waited for: 4 -> 4; matrix products, arithmetic and copies ran while one was open for 9% -> 8% of each run, Pallas kernels for 69% -> 70%
where the time goes in v5:
time: 1100 us; the launch traced here: 1090 us
  Pallas kernels  848 us (77%)
  waiting for transfers between devices  64.2 us (6%)
  local copies, waits for them, and re-layouts  56.1 us (5%)
  other arithmetic  48 us (4%)
  matrix products  48 us (4%)
  between operations  14.9 us (1%)
    pallas_call x9, Pallas kernels, comm_call(): pl.pallas_call(kernel, name=name, out_shape=outs, in_specs=[pl.BlockSpec(...  451 us
    pallas_call x1, Pallas kernels, weight_call(): pl.pallas_call(functools.partial(weight_tiles, tile, shards, 1), name='we...  216 us
    pallas_call x9, Pallas kernels, ffn_pallas(): pl.pallas_call(kernel, name=name, out_shape=tuple((jax.ShapeDtypeStruct(s...  182 us
    dot_general x6, matrix products, mm(): jnp.einsum(spec, left, right, preferred_element_type=F32).astype(kind)  48 us
    all_gather x3, waiting for transfers between devices, gather_shards(): return lax.all_gather(home_tokens, 'dp', axis=0, tiled=True)  37.2 us
    another operation x17, local copies, waits for them, and re-layouts, within(): return mapped(*args)  31.9 us
  transfers between devices with their start and end apart: 7, of which 4 were waited for; matrix products, arithmetic and copies ran while one was open for 8% of the time, Pallas kernels for 70%

profile of v5, /device:TPU:0, one launch (start us, length us, event | category | flops | bytes accessed | tf_op | source)
XLA Modules:
  0.0 1088.7 jit_solution(15780509437386244001)
XLA Ops:
  8.0 1.2 slice_reduce_fusion.6
  9.2 6.2 copy.67
  15.4 43.5 %start.1 = (bf16[1024,1536]{1,0:T(8,128)(2,1)}, bf16[2048,1536]{1,0:T(8,128)(2,1)}) custom-call(bf16[512,1536]{1,0:T(8,128)(2,1)} %bitcast.111, f32[1,1536]{1,0:T(1,128)} %get-tuple-element.357.gain), custom_call_target="tpu_custom_call" | custom-call | bytes 171600000 | tf_op jit(solution)/shard_map/start/pallas_call | solution.py:140
  58.9 27.7 %conditional.4 = (bf16[2048,1536]{1,0:T(8,128)(2,1)}, bf16[2,1024,1152]{2,1,0:T(8,128)(2,1)}, bf16[2048,384]{1,0:T(8,128)(2,1)}, bf16[1536,768]{1,0:T(8,128)(2,1...) conditional(s32[]{:T(128)} %convert_element_type.121, ...), branch_computations={%region_0.2_spmd, %region_2.3_spmd} | conditional | flops 9677053952 | bytes 69523032 | solution.py:1404
  59.2 11.5 %fusion.42 = f32[2048,1152]{1,0:T(8,128)S(1)} fusion(bf16[2048,1536]{1,0:T(8,128)(2,1)} %get-tuple-element.82, bf16[1536,1152]{0,1:T(8,128)(2,1)} %get-tuple-element.302), kind=kOutput, calls=%fused_computation.110 | convolution fusion | flops 7247757312 | bytes 19267584 | tf_op jit(solution)/shard_map/cond/branch_1_fun/td,de->te/dot_general | solution.py:22
  71.1 2.3 fusion.10
  73.4 6.7 convolution_convert_fusion.5
  80.1 2.6 convert_element_type.98
  82.7 1.6 broadcast.150
  84.2 1.3 broadcast.151
  85.6 1.0 broadcast.152.clone
  86.6 47.8 %sum_norm.2 = (f32[1024,1536]{1,0:T(8,128)}, bf16[2048,1536]{1,0:T(8,128)(2,1)}, bf16[1024,1536]{1,0:T(8,128)(2,1)}) custom-call(bf16[2048,1536]{1,0:T(8,128)(2,1)} %get-tuple-element.188.refs_0_, f32[1,1536]{1,0:T(1,128)} %get-tuple-element.356.refs_1_, bf16[1024,1536]{1,0:T(8,128)(2,1)} %get-tuple-element.189.refs_2_.refs_3_), custom_call_target="tpu_custom_call" | custom-call | bytes 171600000 | tf_op jit(solution)/shard_map/sum_norm/pallas_call | solution.py:140
  135.1 44.6 %ffn.1 = (bf16[2048,3584]{1,0:T(8,128)(2,1)}, bf16[2048,1536]{1,0:T(8,128)(2,1)}) custom-call(bf16[2048,1536]{1,0:T(8,128)(2,1)} %get-tuple-element.190.refs_0_.refs_4_, bf16[2,1728,1536]{2,1,0:T(8,128)(2,1)} %bitcast.92, bf16[1728,1536]{1,0:T(8,128)(2,1)} %bitcast.100), custom_call_target="tpu_custom_call" | custom-call | bytes 145200000 | tf_op jit(solution)/shard_map/ffn/pallas_call | solution.py:859
  179.8 46.4 %hop.1 = (bf16[1024,1536]{1,0:T(8,128)(2,1)}, bf16[2048,1536]{1,0:T(8,128)(2,1)}) custom-call(bf16[2048,1536]{1,0:T(8,128)(2,1)} %get-tuple-element.191.refs_0_, f32[1,1536]{1,0:T(1,128)} %get-tuple-element.355.refs_1_, f32[1024,1536]{1,0:T(8,128)} %get-tuple-element.192.refs_2_), custom_call_target="tpu_custom_call" | custom-call | bytes 171600000 | tf_op jit(solution)/shard_map/hop/pallas_call | solution.py:140
  226.2 21.8 %conditional.5 = (bf16[2048,1536]{1,0:T(8,128)(2,1)}, f32[2,1024,768]{2,1,0:T(8,128)}, bf16[2,1024,768]{2,1,0:T(8,128)(2,1)}, bf16[2,2,3,1024,1024]{4,3,2,1,0:T(...) conditional(s32[]{:T(128)} %convert_element_type.121, (bf16[2048,1536]{1,0:T(8,128)(2,1)}, ...), branch_computations={%region_3.4_spmd, %region_4.5_spmd} | conditional | flops 8056209408 | bytes 114036496 | solution.py:1404
  226.6 8.6 broadcast.156
  235.2 3.1 broadcast.153
  238.3 3.1 broadcast.154
  241.4 3.2 broadcast.157
  244.6 1.9 broadcast.155
  246.5 1.5 broadcast.158
  248.0 78.1 %sum_norm.3 = (f32[1024,1536]{1,0:T(8,128)}, bf16[2048,1536]{1,0:T(8,128)(2,1)}, bf16[1024,1536]{1,0:T(8,128)(2,1)}) custom-call(bf16[2048,1536]{1,0:T(8,128)(2,1)} %get-tuple-element.198.refs_0_, f32[1,1536]{1,0:T(1,128)} %get-tuple-element.354.refs_1_, bf16[1024,1536]{1,0:T(8,128)(2,1)} %get-tuple-element.199.refs_2_), custom_call_target="tpu_custom_call" | custom-call | bytes 171600000 | tf_op jit(solution)/shard_map/sum_norm/pallas_call | solution.py:140
  326.2 26.6 %all-gather.4.cloned.1.call-done.refs_0_ = bf16[4096,1536]{1,0:T(8,128)(2,1)} async-done(((bf16[1024,1536]{1,0:T(8,128)(2,1)}), bf16[4096,1536]{1,0:T(8,128)(2,1)}) %all-gather.4.cloned.1.call-update) | async-done | bytes 12582928 | tf_op jit(solution)/shard_map/all_gather | solution.py:1531
  352.9 43.5 %others_up.4.refs_1_.refs_0_ = bf16[4096,3584]{1,0:T(8,128)(2,1)} custom-call(bf16[4096,1536]{1,0:T(8,128)(2,1)} %hold.21.source.refs_0_.refs_10_, bf16[2,1728,1536]{2,1,0:T(8,128)(2,1)} %bitcast.95), custom_call_target="tpu_custom_call" | custom-call | bytes 138600000 | tf_op jit(solution)/shard_map/others_up/pallas_call | solution.py:859
  396.4 58.4 %sum_back.2 = (f32[1024,1536]{1,0:T(8,128)}, bf16[2048,1536]{1,0:T(8,128)(2,1)}, f32[1,1536]{1,0:T(1,128)}) custom-call(bf16[2048,1536]{1,0:T(8,128)(2,1)} %hold.22.refs_0_, f32[1,1536]{1,0:T(1,128)} %get-tuple-element.354.refs_1_, f32[1024,1536]{1,0:T(8,128)} %get-tuple-element.203.refs_2_, bf16[1024,1536]{1,0:T(8,128)(2,1)} %get-tuple-element.189.refs_2_.refs_3_), custom_call_target="tpu_custom_call" | custom-call | bytes 171600000 | tf_op jit(solution)/shard_map/sum_back/pallas_call | solution.py:140
  454.8 43.8 %others_up.5.refs_1_.refs_0_ = bf16[4096,3584]{1,0:T(8,128)(2,1)} custom-call(bf16[4096,1536]{1,0:T(8,128)(2,1)} %collective-permute-done.source.refs_1_.refs_11_, bf16[2,1728,1536]{2,1,0:T(8,128)(2,1)} %bitcast.96, bf16[2048,1536]{1,0:T(8,128)(2,1)} %get-tuple-element.204.refs_0_), custom_call_target="tpu_custom_call" | custom-call | bytes 138600000 | tf_op jit(solution)/shard_map/others_up/pallas_call | solution.py:859
  498.6 5.5 conditional.6
  499.1 3.1 broadcast.159
  502.2 1.9 broadcast.160
  504.0 68.5 %hop_back.1 = (bf16[1024,1536]{1,0:T(8,128)(2,1)}, bf16[2048,1536]{1,0:T(8,128)(2,1)}, f32[1,1536]{1,0:T(1,128)}) custom-call(bf16[2048,1536]{1,0:T(8,128)(2,1)} %get-tuple-element.210.refs_0_, f32[1,1536]{1,0:T(1,128)} %get-tuple-element.355.refs_1_, bf16[1024,1536]{1,0:T(8,128)(2,1)} %get-tuple-element.199.refs_2_, f32[1024,1536]{1,0:T(8,128)} %get-tuple-element.211.refs_3_), custom_call_target="tpu_custom_call" | custom-call | bytes 171600000 | tf_op jit(solution)/shard_map/hop_back/pallas_call | solution.py:140
  572.7 5.3 collective-permute-start.1
  578.0 49.7 %ffn_back.3 = (bf16[2048,3584]{1,0:T(8,128)(2,1)}, bf16[2048,1792]{1,0:T(8,128)(2,1)}, bf16[2048,1536]{1,0:T(8,128)(2,1)}) custom-call(bf16[2048,1536]{1,0:T(8,128)(2,1)} %get-tuple-element.212.grad.refs_6_, bf16[2048,3584]{1,0:T(8,128)(2,1)} %get-tuple-element.213.gu, bf16[2,1728,1536]{2,1,0:T(8,128)(2,1)} %bitcast.98, bf16[1728,1536]{1,0:T(8,128)(2,1)} %bitcast.103), custom_call_target="tpu_custom_call" | custom-call | bytes 158400000 | tf_op jit(solution)/shard_map/ffn_back/pallas_call | solution.py:859
  627.7 53.4 %sum_back.3 = (f32[1024,1536]{1,0:T(8,128)}, bf16[2048,1536]{1,0:T(8,128)(2,1)}, f32[1,1536]{1,0:T(1,128)}) custom-call(bf16[2048,1536]{1,0:T(8,128)(2,1)} %hold.25.refs_0_, f32[1,1536]{1,0:T(1,128)} %get-tuple-element.356.refs_1_, f32[1024,1536]{1,0:T(8,128)} %get-tuple-element.192.refs_2_, bf16[1024,1536]{1,0:T(8,128)(2,1)} %get-tuple-element.216.refs_3_), custom_call_target="tpu_custom_call" | custom-call | bytes 171600000 | tf_op jit(solution)/shard_map/sum_back/pallas_call | solution.py:140
  681.1 56.9 %conditional.7 = (bf16[2048,1536]{1,0:T(8,128)(2,1)}, bf16[1536,384]{1,0:T(8,128)(2,1)}, bf16[1536,384]{1,0:T(8,128)(2,1)}, bf16[1536,384]{1,0:T(8,128)(2,1)}, b...) conditional(s32[]{:T(128)} %convert_element_type.121, ...), branch_computations={%region_8.9_spmd, %region_9.13_spmd} | conditional | flops 19388383232 | bytes 216161504 | solution.py:1404
  681.3 3.0 convert_element_type.104
  684.7 2.4 copy-done.2
  687.4 5.3 fusion.43
  692.7 6.5 multiply_reduce_fusion.2
  699.3 4.1 convolution_convert_fusion.8
  703.4 1.2 pad_maximum_fusion.6
  704.6 5.7 multiply_convert_fusion.2
  710.8 0.9 copy-done.9
  711.7 10.4 fusion.13
  722.2 1.9 fusion.40
  724.1 1.3 copy-done.6
  725.9 10.0 convolution_convert_fusion.7.refs_1_
  736.1 1.1 broadcast.181
  739.3 41.1 %end.1 = f32[512,1536]{1,0:T(8,128)} custom-call(bf16[2048,1536]{1,0:T(8,128)(2,1)} %get-tuple-element.222.first, bf16[2048,1536]{1,0:T(8,128)(2,1)} %hold.26.second), custom_call_target="tpu_custom_call" | custom-call | bytes 171600000 | tf_op jit(solution)/shard_map/end/pallas_call | solution.py:140
  780.4 10.6 all-gather.8.cloned.1.call-done.refs_0_
  791.0 2.0 collective-permute-start.2
  793.0 1.9 fusion.29
  795.4 2.3 multiply_reduce_fusion.3
  798.4 6.2 fusion.34
  804.6 7.7 collective-permute-done.2.refs_3_
  812.4 215.6 %weights.1 = (f32[2,1728,1536]{2,1,0:T(8,128)}, f32[1728,1536]{1,0:T(8,128)}) custom-call(bf16[4096,1536]{1,0:T(8,128)(2,1)} %hold.21.source.refs_0_.refs_10_, bf16[4096,1536]{1,0:T(8,128)(2,1)} %collective-permute-done.source.refs_1_.refs_11_, bf16[4096,1536]{1,0:T(8,128)(2,1)} %hold.27.refs_2_, bf16[4096,1536]{1,0:T(8,128)(2,1)} %collective-permute-done.2.refs_3_, ...), custom_call_target="tpu_custom_call" | custom-call | bytes 198000000 | tf_op jit(solution)/shard_map/weights/pallas_call | solution.py:934
  1027.9 13.7 %total.1 = f32[8,784]{1,0:T(8,128)} custom-call(f32[8,784]{1,0:T(8,128)} %hold.28.values), custom_call_target="tpu_custom_call" | custom-call | bytes 33000000 | tf_op jit(solution)/shard_map/total/pallas_call | solution.py:140
  1041.6 1.4 reshape.224.refs_1_
  1043.1 19.2 %all-reduce.16.cloned.1.call-done = (bf16[1536,384]{1,0:T(8,128)(2,1)}, bf16[1536,384]{1,0:T(8,128)(2,1)}, bf16[1536,384]{1,0:T(8,128)(2,1)}, bf16[400,1536]{1,0...) async-done(((bf16[1536,384]{1,0:T(8,128)(2,1)}, bf16[1536,384]{1,0:T(8,128)(2,1)}, bf16[1536,384]{1,0:T(8,128)(2,1)}, ...) | async-done | bytes 7913488 | tf_op jit(solution)/shard_map/psum | solution.py:1620
  1062.3 3.0 slice.162
  1065.3 1.3 slice.161
  1066.7 3.0 convert_element_type.130
  1069.6 2.4 convert_element_type.129
  1072.1 2.8 convert_element_type.128
  1076.8 4.8 convert_bitcast_fusion
  (126 shorter events, 8.9 us)
Async XLA Ops:
  7.2 345.6 %all-gather.4.cloned.1.call-start = ((), (), s32[]{:S(2)}) async-start(), calls=%async_computation | async-start | bytes 15728640 | tf_op jit(solution)/shard_map/all_gather | solution.py:1531
  9.2 6.2 copy-start.21
  9.2 49.7 %copy-start.11 = (bf16[1536,384]{1,0:T(8,128)(2,1)S(1)}, bf16[1536,384]{1,0:T(8,128)(2,1)}, u32[]{:S(2)}) copy-start(bf16[1536,384]{1,0:T(8,128)(2,1)} %param.27) | copy-start | bytes 3538948
  9.2 49.7 %copy-start.12 = (s32[2,1024]{1,0:T(2,128)S(1)}, s32[2,1024]{1,0:T(2,128)}, u32[]{:S(2)}) copy-start(s32[2,1024]{1,0:T(2,128)} %param.21) | copy-start | bytes 24580
  15.4 43.5 %copy-start.16 = (f32[3,384]{1,0:T(4,128)}, f32[3,384]{1,0:T(4,128)S(1)}, u32[]{:S(2)}) copy-start(f32[3,384]{1,0:T(4,128)S(1)} %convert_element_type.123) | copy-start | bytes 13828
  71.1 2.3 copy-start.23
  134.5 0.7 copy-start.27
  134.5 438.2 %all-gather.6.cloned.1.call-start = ((), (), s32[]{:S(2)}) async-start(), calls=%async_computation.1 | async-start | bytes 15728640 | tf_op jit(solution)/shard_map/all_gather | solution.py:1531
  179.8 46.4 %copy-start.1 = (f32[2,1024,64]{2,1,0:T(8,128)S(1)}, f32[2,1024,64]{2,1,0:T(8,128)}, u32[]{:S(2)}) copy-start(f32[2,1024,64]{2,1,0:T(8,128)} %get-tuple-element.196) | copy-start | bytes 1572868
  326.1 464.9 %all-gather.8.cloned.1.call-start = ((), (), s32[]{:S(2)}) async-start(), calls=%async_computation.2 | async-start | bytes 15728640 | tf_op jit(solution)/shard_map/all_gather | solution.py:1531
  352.8 102.0 %collective-permute-start = (bf16[4096,1536]{1,0:T(8,128)(2,1)}, bf16[4096,1536]{1,0:T(8,128)(2,1)}, u32[]{:S(2)}, u32[]{:S(2)}) collective-permute-start(bf16[4096,1536]{1,0:T(8,128)(2,1)} %hold.21.source.refs_0_.refs_10_), channel_id=1, source_target_pairs={{0,4},{4,0},{8,12},{12,8},{16,20},{20,16},{24,28},{28,24},{1,5},{5... | collective-permute-start | bytes 37748744 | tf_op jit(solution)/shard_map/ppermute | solution.py:1537
  504.0 68.5 %copy-start.25 = (f32[2,64]{1,0:T(2,128)}, f32[2,64]{1,0:T(2,128)S(1)}, u32[]{:S(2)}) copy-start(f32[2,64]{1,0:T(2,128)S(1)} %get-tuple-element.226) | copy-start | bytes 1540
  572.6 489.7 %all-reduce.16.cloned.1.call-start = ((), (), s32[]{:S(2)}) async-start(), calls=%async_computation.3 | async-start | bytes 15826944 | tf_op jit(solution)/shard_map/psum | solution.py:1620
  572.7 165.3 %collective-permute-start.1 = (bf16[4096,1536]{1,0:T(8,128)(2,1)}, bf16[4096,1536]{1,0:T(8,128)(2,1)}, u32[]{:S(2)}, u32[]{:S(2)}) collective-permute-start(bf16[4096,1536]{1,0:T(8,128)(2,1)} %hold.24.source.refs_8_), channel_id=1, source_target_pairs={{16,20},{20,16},{24,28},{28,24},{17,21},{21,17},{25,29},{29,25},{1... | collective-permute-start | bytes 37748744 | tf_op jit(solution)/shard_map/ppermute | solution.py:1537
  627.7 53.4 %copy-start.13 = (s32[2,1024]{1,0:T(2,128)S(1)}, s32[2,1024]{1,0:T(2,128)}, u32[]{:S(2)}) copy-start(s32[2,1024]{1,0:T(2,128)} %param.21) | copy-start | bytes 24580
  627.7 53.4 %copy-start.17 = (f32[3,384]{1,0:T(4,128)S(1)}, f32[3,384]{1,0:T(4,128)}, u32[]{:S(2)}) copy-start(f32[3,384]{1,0:T(4,128)} %copy-done.16) | copy-start | bytes 13828
  627.7 53.4 %copy-start.22 = (bf16[2048,768]{1,0:T(8,128)(2,1)S(1)}, bf16[2048,768]{1,0:T(8,128)(2,1)}, u32[]{:S(2)}) copy-start(bf16[2048,768]{1,0:T(8,128)(2,1)} %get-tuple-element.218) | copy-start | bytes 9437188
  684.3 2.8 copy-start.2
  684.3 3.1 copy-start.24
  703.4 7.4 slice-start
  704.6 6.2 slice-start.1
  710.3 1.4 copy-start.9
  722.1 3.3 copy-start.6
  722.2 3.8 copy-start.10
  738.0 1.0 copy-start.5
  738.0 1.3 copy-start.7
  791.0 21.4 %collective-permute-start.2 = (bf16[4096,1536]{1,0:T(8,128)(2,1)}, bf16[4096,1536]{1,0:T(8,128)(2,1)}, u32[]{:S(2)}, u32[]{:S(2)}) collective-permute-start(bf16[4096,1536]{1,0:T(8,128)(2,1)} %hold.27.refs_2_), channel_id=1, source_target_pairs={{0,4},{4,0},{8,12},{12,8},{1,5},{5,1},{9,13},{13,9},{2,6},{6,2},{1... | collective-permute-start | bytes 37748744 | tf_op jit(solution)/shard_map/ppermute | solution.py:1537
  792.9 2.1 copy-start.18
  793.0 2.1 copy-start.20
  793.0 2.1 copy-start.19
  793.0 2.2 copy-start.26
  793.0 2.4 copy-start
  793.0 2.4 copy-start.15
  1062.3 4.3 copy-start.14
  1074.9 0.7 slice-start.2
  1074.9 1.9 copy-start.4
  1074.9 1.9 copy-start.3
Sparse Core Ops, SparseCore 0:
  134.6 218.1 all-gather.3
  354.3 216.4 all-gather.5
  572.7 218.2 all-gather.7
  797.3 264.9 all-reduce.15
